TPU v7x, 128 devices: a whole 4x4x4 slice. The times are simulated.
128 devices in a mesh: dp: 16 (over z, x_hi, core), context: 2 (over x_lo), tensor: 4 (over y).
Axes of the slice: x: 4 (x_hi: 2, x_lo: 2; x = x_hi * 2 + x_lo), y: 4, z: 4, core: 2. Of those that a mesh axis runs over, the one named last changes fastest.
Arguments:
- hidden: bfloat16 [32768, 5120], P(('dp', 'context'), 'tensor'), may hold values from -4 to 4
- seq_id: int32 [32768], P(('dp', 'context')), may hold values from 0 to 511, as said below
- dest_page: int32 [512], P(('dp', 'context')), may hold values from 0 to 255, as said below
- norm_gain: bfloat16 [5120], replicated, may hold values from 0.099609375 to 1.8984375
- w_query: bfloat16 [5120, 2560], P(None, 'tensor'), may hold values from -0.078125 to 0.078125
- q_bias: bfloat16 [2560], P('tensor'), may hold values from -120 to 120
- w_key: bfloat16 [5120, 512], P(None, 'tensor'), may hold values from -0.078125 to 0.078125
- w_value: bfloat16 [5120, 512], P(None, 'tensor'), may hold values from -0.078125 to 0.078125
- v_bias: bfloat16 [512], P('tensor'), may hold values from -3 to 3
- w_out: bfloat16 [2560, 5120], P('tensor'), may hold values from -0.125 to 0.125
Outputs:
- mixed: bfloat16 [32768, 5120], P(('dp', 'context'), 'tensor')
Inputs may be any that keep to these rules, and one draw needn't show every extreme that they name: `dest_page`: for each context index the values of all owners' pages form a permutation; page p of owner o on context index c is assigned to group value // 16, page value % 16 of that group's device with the same context index; the two context indices of an owner send their page p to the same group; at most 1 pages of one owner device go to one group, and some owner device sends exactly 1. `seq_id`: all tokens of a page share a value; a value is held only by pages assigned to one group.
All inputs are finite; a program needn't handle non-finite values.
Results may differ from a plain program's by a relative error of at most 0.018.
Values may be sent and summed in bfloat16 or wider, within the bound.
No kernel may reach another device: no remote copies, remote signals or barrier semaphores. Data moves between devices by JAX's collectives and lax.ppermute only.
A program may use at most 192 MiB of HBM per device.

v0:
```python
import math

import jax
import jax.numpy as jnp
from jax import lax
from jax.experimental import pallas as pl
from jax.experimental.pallas import tpu as pltpu
from jax.sharding import Mesh
from jax.sharding import PartitionSpec as P

HEAD = 128
PAGE = 64
EPSILON = 1e-06
DP = ("z", "xh", "core")
TENSOR = 4
PARTS = ((0, 32), (32, 48), (48, 64))
FACTS = 128
DIGIT = 32
MIB = 1024 * 1024


def ring_gather(block):
    right = [(i, (i + 1) % TENSOR) for i in range(TENSOR)]
    left = [(i, (i - 1) % TENSOR) for i in range(TENSOR)]
    half = block.shape[0] // 2
    from_left = lax.ppermute(block, "tensor", right)
    from_right = lax.ppermute(block, "tensor", left)
    far_top = lax.ppermute(from_left[:half], "tensor", right)
    far_low = lax.ppermute(from_right[half:], "tensor", left)
    return (block, from_left, from_right, far_top, far_low)


def project_kernel(steps, first, final, facts, counts, order, page, *refs):
    refs = list(refs)
    pieces = [[refs.pop(0) for _ in range(count)] for count in counts]
    gain, weights = refs.pop(0), refs.pop(0)
    if not first:
        total_in, squares_in = refs.pop(0), refs.pop(0)
    if final:
        bias, out, total, squares = refs
    else:
        total, squares = refs
    step = pl.program_id(0)

    for index in range(steps):

        @pl.when(step == index)
        def _(index=index):
            start = 0
            for piece in pieces[index]:
                at = pl.ds(start, piece.shape[0])
                start += piece.shape[0]
                wide = piece[...].astype(jnp.float32)
                square = jnp.sum(wide * wide, axis=1, keepdims=True)
                scaled = (wide * gain[0].astype(jnp.float32)).astype(jnp.bfloat16)
                product = jnp.dot(scaled, weights[...], preferred_element_type=jnp.float32)
                if index == 0 and first:
                    total[at], squares[at] = product, square
                elif index == 0:
                    total[at], squares[at] = total_in[at] + product, squares_in[at] + square
                else:
                    total[at], squares[at] = total[at] + product, squares[at] + square

    if not final:
        return

    @pl.when(step == steps - 1)
    def _():
        features = TENSOR * pieces[0][0].shape[1]
        scale = lax.rsqrt(squares[...] * (1.0 / features) + EPSILON)
        result = (total[...] * scale + bias[...]).astype(jnp.bfloat16)
        pages, count, columns = out.shape
        columns = result.shape[1]
        for index in range(pages):
            target = page[index]
            out[target, :, :columns] = result[index * count : (index + 1) * count]
            if facts:
                lane = lax.broadcasted_iota(jnp.int32, (count, FACTS), 1)
                fact = jnp.where(
                    lane == 0,
                    page[pages + index],
                    jnp.where(
                        lane == 1,
                        page[2 * pages + index],
                        jnp.where(lane == 2, page[3 * pages + index], 0),
                    ),
                )
                out[target, :, columns:] = fact.astype(jnp.float32).astype(jnp.bfloat16)


def project(order, page, pieces, first, gain, weights, bias, carry=None, facts=False):
    steps = len(pieces)
    final = first + steps == TENSOR
    rows = sum(p.shape[0] for p in pieces[0])
    width, columns = pieces[0][0].shape[1], weights.shape[1]
    pages = page.shape[0] // 4
    counts = [len(group) for group in pieces]

    def kernel(*refs):
        project_kernel(steps, carry is None, final, facts, counts, *refs)

    def whole(shape):
        return pl.BlockSpec(shape, lambda k, order, page: (0,) * len(shape))

    operands = [p for group in pieces for p in group]
    in_specs = [whole(p.shape) for p in operands]
    operands += [gain.reshape(TENSOR, 1, width), weights]
    in_specs += [
        pl.BlockSpec((1, 1, width), lambda k, order, page: (order[first + k], 0, 0)),
        pl.BlockSpec((width, columns), lambda k, order, page: (order[first + k], 0)),
    ]
    if carry is not None:
        operands += list(carry)
        in_specs += [whole(c.shape) for c in carry]
    sums = [(rows, columns), (rows, 1)]
    if final:
        operands.append(bias)
        in_specs.append(whole(bias.shape))
        shape = (pages, rows // pages, columns + (FACTS if facts else 0))
        out_shape = jax.ShapeDtypeStruct(shape, jnp.bfloat16)
        out_specs = whole(shape)
        scratch = [pltpu.VMEM(shape, jnp.float32) for shape in sums]
    else:
        out_shape = [jax.ShapeDtypeStruct(shape, jnp.float32) for shape in sums]
        out_specs = [whole(shape) for shape in sums]
        scratch = []
    return pl.pallas_call(
        kernel,
        out_shape=out_shape,
        grid_spec=pltpu.PrefetchScalarGridSpec(
            num_scalar_prefetch=2,
            grid=(steps,),
            in_specs=in_specs,
            out_specs=out_specs,
            scratch_shapes=scratch,
        ),
        compiler_params=pltpu.CompilerParams(vmem_limit_bytes=36 * MIB),
        cost_estimate=pl.CostEstimate(
            flops=4 * rows * width * steps * columns,
            bytes_accessed=2 * steps * width * (rows + columns) + 2 * rows * columns,
            transcendentals=rows,
        ),
        name="project",
    )(order, page, *operands)


def attend_kernel(heads, first, parts, source, sequence, context, *refs):
    own, other = refs[:parts], refs[parts : 2 * parts]
    out, keys, values, turned, best, total, summed = refs[2 * parts :]
    pages = own[0].shape[0]
    key_at = own[-1].shape[2] - 2 * HEAD
    half = pages * PAGE
    per = 4
    rows = per * PAGE
    blocks = pages // per
    lanes = heads * rows
    factor = math.log2(math.e) / math.sqrt(HEAD)

    def place_page(slot, carry):
        start = 0
        for part in range(parts):
            count = own[part].shape[1]
            at = pl.ds(pl.multiple_of(half + slot * PAGE + start, 16), count)
            page = source[pages + slot]
            keys[at, :] = own[part][page, :, key_at : key_at + HEAD]
            values[at, :] = own[part][page, :, key_at + HEAD : key_at + 2 * HEAD]
            at = pl.ds(pl.multiple_of(slot * PAGE + start, 16), count)
            page = source[slot]
            keys[at, :] = other[part][page, :, :HEAD]
            values[at, :] = other[part][page, :, HEAD : 2 * HEAD]
            start += count
        return carry

    lax.fori_loop(0, pages, place_page, 0)
    for block in range(2 * blocks):
        turned[block] = values[pl.ds(block * rows, rows), :].astype(jnp.float32).T.astype(jnp.bfloat16)

    def query_block(index, carry):
        slot = index * per
        query = jnp.concatenate(
            [
                own[part][source[pages + slot + page], :, (first + head) * HEAD : (first + head + 1) * HEAD]
                for head in range(heads)
                for page in range(per)
                for part in range(parts)
            ],
            axis=0,
        )
        sequence_q = [sequence[pages + slot + page] for page in range(per)]
        within = lax.broadcasted_iota(jnp.int32, (1, lanes), 1) % rows
        seq_lane = jnp.full((1, lanes), sequence_q[per - 1], jnp.int32)
        for page in range(per - 2, -1, -1):
            seq_lane = jnp.where(within < (page + 1) * PAGE, sequence_q[page], seq_lane)

        def scores_of(block, diagonal):
            at = pl.ds(pl.multiple_of(block * rows, rows), rows)
            scores = lax.dot_general(
                keys[at, :], query, (((1,), (1,)), ((), ())), preferred_element_type=jnp.float32
            )
            cut = []
            for page in range(per):
                visible = seq_lane == sequence[block * per + page]
                if diagonal:
                    place = lax.broadcasted_iota(jnp.int32, (PAGE, lanes), 0) + page * PAGE
                    visible = visible & (place <= within)
                cut.append(jnp.where(visible, scores[page * PAGE : (page + 1) * PAGE], -1e30))
            return jnp.concatenate(cut, axis=0)

        def apply(block, weight):
            return jnp.dot(
                turned[block], weight.astype(jnp.bfloat16), preferred_element_type=jnp.float32
            )

        last = blocks + index
        scores = scores_of(last, True)
        top = jnp.max(scores, axis=0, keepdims=True)
        weight = jnp.exp2((scores - top) * factor)
        best[...] = top
        total[...] = jnp.sum(weight, axis=0, keepdims=True)
        summed[...] = apply(last, weight)

        def key_block(block, carry):
            seen = False
            for page in range(per):
                for seq in sequence_q:
                    seen = seen | (sequence[block * per + page] == seq)

            @pl.when(seen)
            def _():
                scores = scores_of(block, False)
                top = jnp.maximum(best[...], jnp.max(scores, axis=0, keepdims=True))
                weight = jnp.exp2((scores - top) * factor)
                fade = jnp.exp2((best[...] - top) * factor)
                best[...] = top
                total[...] = total[...] * fade + jnp.sum(weight, axis=0, keepdims=True)
                summed[...] = summed[...] * fade + apply(block, weight)

            return carry

        lax.fori_loop(jnp.where(context[0] > 0, 0, blocks), last, key_block, 0)
        result = (summed[...] / total[...]).T.astype(jnp.bfloat16)
        for head in range(heads):
            for page in range(per):
                start = head * rows + page * PAGE
                out[source[pages + slot + page], :, head * HEAD : (head + 1) * HEAD] = result[
                    start : start + PAGE
                ]
        return carry

    lax.fori_loop(0, blocks, query_block, 0)


def attend(heads, first, source, sequence, context, own, other):
    pages = own[0].shape[0]
    parts = len(own)

    def kernel(*refs):
        attend_kernel(heads, first, parts, *refs)

    half = pages * PAGE
    lanes = heads * 4 * PAGE
    vmem = pl.BlockSpec(memory_space=pltpu.VMEM)
    smem = pl.BlockSpec(memory_space=pltpu.SMEM)
    return pl.pallas_call(
        kernel,
        out_shape=jax.ShapeDtypeStruct((pages, PAGE, heads * HEAD), jnp.bfloat16),
        in_specs=[smem] * 3 + [vmem] * (2 * parts),
        out_specs=vmem,
        scratch_shapes=[
            pltpu.VMEM((2 * half, HEAD), jnp.bfloat16),
            pltpu.VMEM((2 * half, HEAD), jnp.bfloat16),
            pltpu.VMEM((pages // 2, HEAD, 4 * PAGE), jnp.bfloat16),
            pltpu.VMEM((1, lanes), jnp.float32),
            pltpu.VMEM((1, lanes), jnp.float32),
            pltpu.VMEM((HEAD, lanes), jnp.float32),
        ],
        compiler_params=pltpu.CompilerParams(vmem_limit_bytes=24 * MIB),
        cost_estimate=pl.CostEstimate(
            flops=4 * half * half * HEAD * heads,
            bytes_accessed=2 * half * (own[0].shape[2] + 2 * HEAD + heads * HEAD),
            transcendentals=half * half * heads,
        ),
        name="attend",
    )(source, sequence, context, *own, *other)


def mix_kernel(steps, rows_at, depth, final, counts, carried, page_of, *refs):
    refs = list(refs)
    pieces = [[refs.pop(0) for _ in range(count)] for count in counts]
    w_out = refs.pop(0)
    before = refs.pop(0) if carried else None
    if final:
        hidden, out, total = refs
    else:
        (total,) = refs
    step = pl.program_id(1)
    band = w_out[:, 0, 0, rows_at : rows_at + depth, :].reshape(-1, w_out.shape[-1])

    for index in range(steps):

        @pl.when(step == index)
        def _(index=index):
            start = 0
            for piece in pieces[index]:
                at = pl.ds(start, piece.shape[0])
                product = jnp.dot(piece[...], band, preferred_element_type=jnp.float32)
                if index > 0:
                    product = total[at] + product
                elif carried:
                    product = before[at] + product
                if not (final and index == steps - 1):
                    total[at] = product
                else:
                    for item in range(piece.shape[0] // PAGE):
                        page = page_of[start // PAGE + item]
                        rows = product[item * PAGE : (item + 1) * PAGE]
                        out[page] = (hidden[page].astype(jnp.float32) + rows).astype(jnp.bfloat16)
                start += piece.shape[0]


def mix(page_of, pieces, first, w_out, rows_at, depth, before=None, hidden=None):
    steps = len(pieces)
    rows = sum(p.shape[0] for p in pieces[0])
    outer, cuts, _, stored, columns = w_out.shape
    final, carried = hidden is not None, before is not None
    counts = [len(group) for group in pieces]

    def kernel(*refs):
        mix_kernel(steps, rows_at, depth, final, counts, carried, *refs)

    paged = pl.BlockSpec((rows // PAGE, PAGE, columns), lambda n, k, page_of: (0, 0, n))
    flat = pl.BlockSpec((rows, columns), lambda n, k, page_of: (0, n))
    operands = [p for group in pieces for p in group]
    in_specs = [pl.BlockSpec(p.shape, lambda n, k, page_of: (0, 0)) for p in operands]
    operands.append(w_out)
    in_specs.append(
        pl.BlockSpec(
            (outer, 1, 1, stored, columns), lambda n, k, page_of: (0, n, first + k, 0, 0)
        )
    )
    if carried:
        operands.append(before)
        in_specs.append(flat)
    if final:
        operands.append(hidden)
        in_specs.append(paged)
        out_shape = jax.ShapeDtypeStruct(hidden.shape, jnp.bfloat16)
        out_spec = paged
        scratch = [pltpu.VMEM((rows, columns), jnp.float32)]
    else:
        out_shape = jax.ShapeDtypeStruct((rows, cuts * columns), jnp.float32)
        out_spec = flat
        scratch = []
    return pl.pallas_call(
        kernel,
        out_shape=out_shape,
        grid_spec=pltpu.PrefetchScalarGridSpec(
            num_scalar_prefetch=1,
            grid=(cuts, steps),
            in_specs=in_specs,
            out_specs=out_spec,
            scratch_shapes=scratch,
        ),
        compiler_params=pltpu.CompilerParams(vmem_limit_bytes=40 * MIB),
        cost_estimate=pl.CostEstimate(
            flops=4 * rows * outer * depth * steps * cuts * columns,
            bytes_accessed=2 * outer * depth * steps * cuts * columns + 6 * rows * cuts * columns,
            transcendentals=0,
        ),
        name="mix",
    )(page_of, *operands)


def recut(w_out, context, outer_index, outer, cuts):
    columns = w_out.shape[1] // (2 * TENSOR)
    bands = []
    for first, end in cuts:
        depth = (end - first) * HEAD // outer
        bands.append(
            lax.dynamic_slice_in_dim(w_out, first * HEAD + outer_index * depth, depth, 0)
        )
    band = jnp.concatenate(bands, axis=0)
    me = lax.axis_index("tensor")

    def cut(step):
        target = (me + step) % TENSOR
        return lax.dynamic_slice_in_dim(band, (target * 2 + context) * columns, columns, 1)

    def shift(step):
        return [(i, (i + step) % TENSOR) for i in range(TENSOR)]

    pieces = [
        cut(0),
        lax.ppermute(cut(1), "tensor", shift(1)),
        lax.ppermute(cut(3), "tensor", shift(3)),
        lax.ppermute(cut(2), "tensor", shift(2)),
    ]
    whole = lax.all_gather(jnp.stack(pieces), ("z", "xh", "context"), axis=0, tiled=False)
    return whole.reshape(outer, 2, TENSOR, band.shape[0], columns)


def places(local, sequence):
    pages = local.shape[0]
    ladder = jnp.arange(pages, dtype=jnp.int32)
    hit = local[None, :] == ladder[:, None]
    source = jnp.sum(jnp.where(hit, ladder[None, :], 0), axis=1)
    return jnp.stack([source, jnp.sum(jnp.where(hit, sequence[None, :], 0), axis=1)])


def read_facts(facts):
    facts = facts.astype(jnp.float32).astype(jnp.int32)
    return places(facts[:, 0], facts[:, 1] * DIGIT + facts[:, 2])


def body(hidden, seq_id, dest_page, norm_gain, w_query, q_bias, w_key, w_value, v_bias, w_out):
    pages = dest_page.shape[0]
    me = lax.axis_index("tensor")
    context = lax.axis_index("context")
    heads = w_query.shape[1] // HEAD
    cuts = [(0, 3), (3, heads)]
    order = jnp.stack([me, (me + 3) % TENSOR, (me + 1) % TENSOR, (me + 2) % TENSOR]).astype(jnp.int32)
    sequence = seq_id[::PAGE]
    group = dest_page // pages
    page = jnp.concatenate([group, dest_page % pages, sequence // DIGIT, sequence % DIGIT])
    slots = jnp.arange(pages, dtype=jnp.int32)
    page_of = jnp.sum(jnp.where(group[None, :] == slots[:, None], slots[None, :], 0), axis=1)

    paged = hidden.reshape(pages, PAGE, hidden.shape[1])
    gathered = [
        ring_gather(paged[:, at:end].reshape(pages * (end - at), -1)) for at, end in PARTS
    ]
    w_out, _ = lax.optimization_barrier((w_out, gathered[0][1]))
    w_all = recut(w_out, context, lax.axis_index(("z", "xh")), 8, cuts)

    weights = jnp.concatenate([w_query, w_key, w_value], axis=1)
    bias = jnp.concatenate([q_bias, jnp.zeros_like(v_bias), v_bias]).astype(jnp.float32)[None, :]
    own, other = [], []
    for index, (mine, left, right, top, low) in enumerate(gathered):
        facts = index == 0
        if index < len(PARTS) - 1:
            pieces = [(mine,), (left,), (right,), (top, low)]
            rows = project(order, page, pieces, 0, norm_gain, weights, bias, facts=facts)
        else:
            carry = project(order, page, [(mine,), (left,), (right,)], 0, norm_gain, weights, bias)
            rows = project(order, page, [(top, low)], 3, norm_gain, weights, bias, carry, facts)
        rows = lax.all_to_all(rows, DP, split_axis=0, concat_axis=0, tiled=True)
        own.append(rows)
        other.append(lax.ppermute(rows[:, :, w_query.shape[1] :], "context", [(0, 1)]))

    at = weights.shape[1]
    here = read_facts(own[0][:, 0, at : at + 3])
    there = read_facts(other[0][:, 0, 2 * HEAD : 2 * HEAD + 3])
    there = jnp.where(context > 0, there, here)
    source = jnp.concatenate([there[0], here[0]])
    sequence = jnp.concatenate([there[1], here[1]])

    second = context.astype(jnp.int32).reshape(1)
    parts = []
    for first, end in cuts:
        parts.append(attend(end - first, first, source, sequence, second, own, other))
    exchanged = [
        lax.all_to_all(part, DP, split_axis=0, concat_axis=0, tiled=True) for part in parts
    ]
    exchanged[0], _ = lax.optimization_barrier((exchanged[0], parts[1]))
    total, rows_at = None, 0
    for index, (first, end) in enumerate(cuts):
        depth = (end - first) * HEAD // 8
        mine, left, right, top, low = ring_gather(exchanged[index].reshape(pages * PAGE, -1))
        if end < heads:
            pieces = [(mine,), (left,), (right,), (top, low)]
            total = mix(page_of, pieces, 0, w_all, rows_at, depth)
        else:
            pieces = [(mine,), (left,), (right,)]
            total = mix(page_of, pieces, 0, w_all, rows_at, depth, total)
            result = mix(page_of, [(top, low)], 3, w_all, rows_at, depth, total, paged)
        rows_at += depth
    return result.reshape(hidden.shape)


def solution(mesh):
    fine = Mesh(
        mesh.devices.reshape(4, 2, 2, 2, TENSOR), ("z", "xh", "core", "context", "tensor")
    )
    rows = DP + ("context",)
    return jax.shard_map(
        body,
        mesh=fine,
        in_specs=(
            P(rows, "tensor"),
            P(rows),
            P(rows),
            P(),
            P(None, "tensor"),
            P("tensor"),
            P(None, "tensor"),
            P(None, "tensor"),
            P("tensor"),
            P("tensor", None),
        ),
        out_specs=P(rows, "tensor"),
        check_vma=False,
    )
```

profile of v0, /device:TPU:2, one launch (start us, length us, event | category | flops | bytes accessed | tf_op | source)
XLA Modules:
  0.0 326.7 jit_solution(14102824886013706440)
XLA Ops:
  10.7 30.5 %collective-permute-done.refs_3_ = bf16[512,1280]{1,0:T(8,128)(2,1)} collective-permute-done((bf16[512,1280]{1,0:T(8,128)(2,1)}, bf16[512,1280]{1,0:T(8,128)(2,1)}, u32[]{:S(2)}, u32[]{:S(2)}) %collective-permute-start) | collective-permute-done | bytes 1310752 | tf_op jit(solution)/shard_map/ppermute | solution.py:26
  61.0 3.5 %constant_dynamic-update-slice_fusion.2 = bf16[5120,896]{1,0:T(8,128)(2,1)S(1)} fusion(bf16[5120,640]{1,0:T(8,128)(2,1)} %param.14), kind=kLoop, calls=%fused_computation.20 | loop fusion | bytes 13107200
  65.2 3.5 %copy-done = bf16[5120,896]{1,0:T(8,128)(2,1)} copy-done((bf16[5120,896]{1,0:T(8,128)(2,1)}, bf16[5120,896]{1,0:T(8,128)(2,1)S(1)}, u32[]{:S(2)}) %copy-start) | copy-done | bytes 9175064
  69.6 5.2 %collective-permute-done.9.refs_3_ = bf16[256,1280]{1,0:T(8,128)(2,1)} collective-permute-done((bf16[256,1280]{1,0:T(8,128)(2,1)}, bf16[256,1280]{1,0:T(8,128)(2,1)}, u32[]{:S(2)}, u32[]{:S(2)}) %collective-permute-start.9) | collective-permute-done | bytes 655392 | tf_op jit(solution)/shard_map/ppermute | solution.py:26
  77.1 3.3 %collective-permute-start.12 = (bf16[128,1280]{1,0:T(8,128)(2,1)S(1)}, bf16[128,1280]{1,0:T(8,128)(2,1)S(1)}, u32[]{:S(2)}, u32[]{:S(2)}) collective-permute-start(bf16[128,1280]{1,0:T(8,128)(2,1)S(1)} %slice.119), channel_id=1, source_target_pairs={{0,3},{1,0},{2,1},{3,2},{4,7},{5,4},{6,5},{7,6},{8,11},{9,8},{10,9... | collective-permute-start | bytes 983048 | tf_op jit(solution)/shard_map/ppermute | solution.py:29
  80.3 8.5 %collective-permute-done.5.refs_3_ = bf16[256,1280]{1,0:T(8,128)(2,1)} collective-permute-done((bf16[256,1280]{1,0:T(8,128)(2,1)S(1)}, bf16[256,1280]{1,0:T(8,128)(2,1)}, u32[]{:S(2)}, u32[]{:S(2)}) %collective-permute-start.5) | collective-permute-done | bytes 655392 | tf_op jit(solution)/shard_map/ppermute | solution.py:26
  92.3 3.2 collective-permute-start.8
  97.6 17.2 %collective-permute-done.1.refs_4_ = bf16[512,1280]{1,0:T(8,128)(2,1)} collective-permute-done((bf16[512,1280]{1,0:T(8,128)(2,1)}, bf16[512,1280]{1,0:T(8,128)(2,1)}, u32[]{:S(2)}, u32[]{:S(2)}) %collective-permute-start.1) | collective-permute-done | bytes 1310752 | tf_op jit(solution)/shard_map/ppermute | solution.py:27
  116.8 3.2 collective-permute-start.3
  120.1 3.6 %copy-done.1 = bf16[5120,896]{1,0:T(8,128)(2,1)S(1)} copy-done((bf16[5120,896]{1,0:T(8,128)(2,1)S(1)}, bf16[5120,896]{1,0:T(8,128)(2,1)}, u32[]{:S(2)}) %copy-start.1) | copy-done | bytes 9175064
  123.7 4.7 %project.6 = (f32[256,896]{1,0:T(8,128)S(1)}, f32[256,1]{1,0:T(8,128)S(1)}) custom-call(s32[4]{0:T(128)S(1)} %pad_add_fusion.refs_0_, s32[64]{0:T(128)S(1)} %pad_add_fusion.1.refs_1_, bf16[256,1280]{1,0:T(8,128)(2,1)} %bitcast.21.refs_2_, bf16[256,1280]{1,0:T(8,128)(2,1)} %collective-permute-done.9.refs_3_, ...), custom_call_target="tpu_custom_call" | custom-call | flops 3523215360 | bytes 9306112 | tf_op jit(solution)/shard_map/project/pallas_call | solution.py:127
  130.7 7.0 %all-to-all-start.2 = ((bf16[16,16,896]{2,1,0:T(8,128)(2,1)}), bf16[16,16,896]{2,1,0:T(8,128)(2,1)S(1)}, u32[]{:S(2)}, u32[]{:S(2)}) async-start(bf16[16,16,896]{2,1,0:T(8,128)(2,1)} %project.7), calls=%async_computation.2 | async-start | bytes 917504 | tf_op jit(solution)/shard_map/all_to_all | solution.py:446
  137.7 3.6 %copy-done.2 = bf16[5120,896]{1,0:T(8,128)(2,1)S(1)} copy-done((bf16[5120,896]{1,0:T(8,128)(2,1)S(1)}, bf16[5120,896]{1,0:T(8,128)(2,1)}, u32[]{:S(2)}) %copy-start.2) | copy-done | bytes 9175064
  142.4 5.7 %project.5 = bf16[16,16,896]{2,1,0:T(8,128)(2,1)S(1)} custom-call(s32[4]{0:T(128)S(1)} %pad_add_fusion.refs_0_, s32[64]{0:T(128)S(1)} %pad_add_fusion.1.refs_1_, bf16[256,1280]{1,0:T(8,128)(2,1)S(1)} %bitcast.45, bf16[256,1280]{1,0:T(8,128)(2,1)} %collective-permute-done.5.refs_3_, bf16[256,1280]{1,0:T(8,128)(2,1)} %collective-permute-done.6.refs_4_, ...), custom_call_target="tpu_custom_call" | custom-call | flops 4697620480 | bytes 12255232 | tf_op jit(solution)/shard_map/project/pallas_call | solution.py:127
  149.3 6.7 %all-to-all-start.1 = ((bf16[16,16,896]{2,1,0:T(8,128)(2,1)}), bf16[16,16,896]{2,1,0:T(8,128)(2,1)S(1)}, u32[]{:S(2)}, u32[]{:S(2)}) async-start(bf16[16,16,896]{2,1,0:T(8,128)(2,1)} %copy-done.13), calls=%async_computation.1 | async-start | bytes 917504 | tf_op jit(solution)/shard_map/all_to_all | solution.py:446
  156.1 3.6 %copy-done.3 = bf16[5120,896]{1,0:T(8,128)(2,1)S(1)} copy-done((bf16[5120,896]{1,0:T(8,128)(2,1)S(1)}, bf16[5120,896]{1,0:T(8,128)(2,1)}, u32[]{:S(2)}) %copy-start.3) | copy-done | bytes 9175064
  160.4 9.5 %project.4 = bf16[16,32,1024]{2,1,0:T(8,128)(2,1)S(1)} custom-call(s32[4]{0:T(128)S(1)} %pad_add_fusion.refs_0_, s32[64]{0:T(128)S(1)} %pad_add_fusion.1.refs_1_, bf16[512,1280]{1,0:T(8,128)(2,1)} %bitcast.5.refs_2_, bf16[512,1280]{1,0:T(8,128)(2,1)} %collective-permute-done.refs_3_, bf16[512,1280]{1,0:T(8,128)(2,1)} %collective-permute-done.1.refs_4_, ...), custom_call_target="tpu_custom_call" | custom-call | flops 9395240960 | bytes 15335424 | tf_op jit(solution)/shard_map/project/pallas_call | solution.py:127
  170.9 7.3 %all-to-all-start = ((bf16[16,32,1024]{2,1,0:T(8,128)(2,1)}), bf16[16,32,1024]{2,1,0:T(8,128)(2,1)}, u32[]{:S(2)}, u32[]{:S(2)}) async-start(bf16[16,32,1024]{2,1,0:T(8,128)(2,1)} %copy-done.9), calls=%async_computation | async-start | bytes 2097152 | tf_op jit(solution)/shard_map/all_to_all | solution.py:446
  182.1 14.2 %all-to-all-done.refs_3_ = bf16[16,32,1024]{2,1,0:T(8,128)(2,1)} async-done(((bf16[16,32,1024]{2,1,0:T(8,128)(2,1)}), bf16[16,32,1024]{2,1,0:T(8,128)(2,1)}, u32[]{:S(2)}, u32[]{:S(2)}) %all-to-all-start) | async-done | bytes 1048608 | tf_op jit(solution)/shard_map/all_to_all | solution.py:446
  200.9 10.0 %collective-permute-done.4.refs_6_ = bf16[16,32,384]{2,1,0:T(8,128)(2,1)} collective-permute-done((bf16[16,32,384]{2,1,0:T(8,128)(2,1)}, bf16[16,32,384]{2,1,0:T(8,128)(2,1)}, u32[]{:S(2)}, u32[]{:S(2)}) %collective-permute-start.4) | collective-permute-done | bytes 393248 | tf_op jit(solution)/shard_map/ppermute | solution.py:448
  213.9 15.2 %attend.3 = bf16[16,64,384]{2,1,0:T(8,128)(2,1)} custom-call(s32[32]{0:T(128)S(1)} %pad_add_fusion.2.refs_0_, s32[32]{0:T(128)S(1)} %pad_add_fusion.3.refs_1_, s32[1]{0:T(128)} %bitcast.19.refs_2_, bf16[16,32,1024]{2,1,0:T(8,128)(2,1)} %all-to-all-done.refs_3_, bf16[16,16,896]{2,1,0:T(8,128)(2,1)S(1)} %all-to-all-done.1.refs_4_, ...), custom_call_target="tpu_custom_call" | custom-call | flops 1610612736 | bytes 3407872 | tf_op jit(solution)/shard_map/attend/pallas_call | solution.py:264
  229.1 4.5 %all-to-all-start.4 = ((bf16[16,64,384]{2,1,0:T(8,128)(2,1)}), bf16[16,64,384]{2,1,0:T(8,128)(2,1)}, u32[]{:S(2)}, u32[]{:S(2)}) async-start(bf16[16,64,384]{2,1,0:T(8,128)(2,1)} %attend.3), calls=%async_computation.4 | async-start | bytes 1572864 | tf_op jit(solution)/shard_map/all_to_all | solution.py:462
  233.6 11.6 %attend.2 = bf16[16,64,256]{2,1,0:T(8,128)(2,1)S(1)} custom-call(s32[32]{0:T(128)S(1)} %pad_add_fusion.2.refs_0_, s32[32]{0:T(128)S(1)} %pad_add_fusion.3.refs_1_, s32[1]{0:T(128)} %bitcast.19.refs_2_, bf16[16,32,1024]{2,1,0:T(8,128)(2,1)} %all-to-all-done.refs_3_, bf16[16,16,896]{2,1,0:T(8,128)(2,1)S(1)} %all-to-all-done.1.refs_4_, ...), custom_call_target="tpu_custom_call" | custom-call | flops 1073741824 | bytes 3145728 | tf_op jit(solution)/shard_map/attend/pallas_call | solution.py:264
  248.6 3.2 collective-permute-start.23
  251.9 15.9 %all_to_all.25 = bf16[16,64,256]{2,1,0:T(8,128)(2,1)S(1)} all-to-all(bf16[16,64,256]{2,1,0:T(8,128)(2,1)} %copy-done.12), channel_id=1, replica_groups=mesh['z'=4,'xh'=2,'core'=2,'context'=2,'tensor'=4] {'z','xh','core'}, dimensions={0} | all-to-all | bytes 1048576 | tf_op jit(solution)/shard_map/all_to_all | solution.py:462
  267.8 3.2 collective-permute-start.17
  271.2 3.3 %collective-permute-start.25 = (bf16[512,384]{1,0:T(8,128)(2,1)S(1)}, bf16[512,384]{1,0:T(8,128)(2,1)S(1)}, u32[]{:S(2)}, u32[]{:S(2)}) collective-permute-start(bf16[512,384]{1,0:T(8,128)(2,1)S(1)} %slice.125), channel_id=1, source_target_pairs={{0,3},{1,0},{2,1},{3,2},{4,7},{5,4},{6,5},{7,6},{8,11},{9,8},{10,9... | collective-permute-start | bytes 1179656 | tf_op jit(solution)/shard_map/ppermute | solution.py:29
  274.6 9.2 %collective-permute-done.15.refs_2_ = bf16[1024,256]{1,0:T(8,128)(2,1)S(1)} collective-permute-done((bf16[1024,256]{1,0:T(8,128)(2,1)S(1)}, bf16[1024,256]{1,0:T(8,128)(2,1)S(1)}, u32[]{:S(2)}, u32[]{:S(2)}) %collective-permute-start.15) | collective-permute-done | bytes 524320 | tf_op jit(solution)/shard_map/ppermute | solution.py:26
  288.8 3.5 %collective-permute-done.24.refs_4_ = bf16[512,384]{1,0:T(8,128)(2,1)S(1)} collective-permute-done((bf16[512,384]{1,0:T(8,128)(2,1)S(1)}, bf16[512,384]{1,0:T(8,128)(2,1)S(1)}, u32[]{:S(2)}, u32[]{:S(2)}) %collective-permute-start.24) | collective-permute-done | bytes 393248 | tf_op jit(solution)/shard_map/ppermute | solution.py:28
  298.0 10.7 %mix.3.refs_5_ = f32[1024,1280]{1,0:T(8,128)S(1)} custom-call(s32[16]{0:T(128)S(1)} %select_reduce_fusion.4.refs_0_, bf16[1024,384]{1,0:T(8,128)(2,1)} %bitcast.28.refs_1_, bf16[1024,384]{1,0:T(8,128)(2,1)S(1)} %copy-done.15, bf16[1024,384]{1,0:T(8,128)(2,1)S(1)} %copy-done.17, bf16[512,384]{1,0:T(8,128)(2,1)S(1)} %copy-done.21, ...), custom_call_target="tpu_custom_call" | custom-call | flops 8053063680 | bytes 11796480 | tf_op jit(solution)/shard_map/mix/pallas_call | solution.py:354
  308.8 6.9 %mix.4.refs_4_ = f32[1024,1280]{1,0:T(8,128)S(1)} custom-call(s32[16]{0:T(128)S(1)} %select_reduce_fusion.4.refs_0_, bf16[1024,256]{1,0:T(8,128)(2,1)S(1)} %bitcast.42, bf16[1024,256]{1,0:T(8,128)(2,1)S(1)} %copy-done.6, bf16[1024,256]{1,0:T(8,128)(2,1)S(1)} %copy-done.8, bf16[8,2,4,80,640]{4,3,2,1,0:T(8,128)(2,1)} %bitcast.47, f32[1024,1280]{1,0:T(8,128)S(1)} %mix.3.refs_5_), custom_call_target="tpu_custom_call" | custom-call | flops 4026531840 | bytes 9830400 | tf_op jit(solution)/shard_map/mix/pallas_call | solution.py:354
  315.7 4.2 %mix.5 = bf16[16,64,1280]{2,1,0:T(8,128)(2,1)} custom-call(s32[16]{0:T(128)S(1)} %select_reduce_fusion.4.refs_0_, bf16[512,256]{1,0:T(8,128)(2,1)S(1)} %collective-permute-done.16.refs_1_, bf16[512,256]{1,0:T(8,128)(2,1)} %collective-permute-done.18.refs_2_, bf16[8,2,4,80,640]{4,3,2,1,0:T(8,128)(2,1)} %bitcast.48, f32[1024,1280]{1,0:T(8,128)S(1)} %mix.4.refs_4_, ...), custom_call_target="tpu_custom_call" | custom-call | flops 1342177280 | bytes 8519680 | tf_op jit(solution)/shard_map/mix/pallas_call | solution.py:354
  (145 shorter events, 67.3 us)
Async XLA Ops:
  6.5 287.2 %all-gather.3.cloned.1.call-start = ((), (), s32[]{:S(2)}) async-start(), calls=%async_computation.5 | async-start | bytes 6963200 | tf_op jit(solution)/shard_map/all_gather | solution.py:398
  9.1 32.1 %collective-permute-start = (bf16[512,1280]{1,0:T(8,128)(2,1)}, bf16[512,1280]{1,0:T(8,128)(2,1)}, u32[]{:S(2)}, u32[]{:S(2)}) collective-permute-start(bf16[512,1280]{1,0:T(8,128)(2,1)} %bitcast.5.refs_2_), channel_id=1, source_target_pairs={{0,1},{1,2},{2,3},{3,0},{4,5},{5,6},{6,7},{7,4},{8,9},{9,10},{10,1... | collective-permute-start | bytes 3932168 | tf_op jit(solution)/shard_map/ppermute | solution.py:26
  43.4 6.0 %collective-permute-start.19 = (bf16[80,640]{1,0:T(8,128)(2,1)S(1)}, bf16[80,640]{1,0:T(8,128)(2,1)S(1)}, u32[]{:S(2)}, u32[]{:S(2)}) collective-permute-start(bf16[80,640]{1,0:T(8,128)(2,1)S(1)} %get-tuple-element.20), channel_id=1, source_target_pairs={{0,1},{1,2},{2,3},{3,0},{4,5},{5,6},{6,7},{7,4},{8,9},{9,10},{10,1... | collective-permute-start | bytes 307208 | tf_op jit(solution)/shard_map/ppermute | solution.py:394
  43.8 6.3 %collective-permute-start.20 = (bf16[80,640]{1,0:T(8,128)(2,1)S(1)}, bf16[80,640]{1,0:T(8,128)(2,1)S(1)}, u32[]{:S(2)}, u32[]{:S(2)}) collective-permute-start(bf16[80,640]{1,0:T(8,128)(2,1)S(1)} %get-tuple-element.21), channel_id=1, source_target_pairs={{0,3},{1,0},{2,1},{3,2},{4,7},{5,4},{6,5},{7,6},{8,11},{9,8},{10,9... | collective-permute-start | bytes 307208 | tf_op jit(solution)/shard_map/ppermute | solution.py:395
  46.7 6.2 %collective-permute-start.21 = (bf16[80,640]{1,0:T(8,128)(2,1)S(1)}, bf16[80,640]{1,0:T(8,128)(2,1)S(1)}, u32[]{:S(2)}, u32[]{:S(2)}) collective-permute-start(bf16[80,640]{1,0:T(8,128)(2,1)S(1)} %get-tuple-element.22), channel_id=1, source_target_pairs={{0,2},{1,3},{2,0},{3,1},{4,6},{5,7},{6,4},{7,5},{8,10},{9,11},{10,... | collective-permute-start | bytes 307208 | tf_op jit(solution)/shard_map/ppermute | solution.py:396
  54.7 21.4 %collective-permute-start.11 = (bf16[256,1280]{1,0:T(8,128)(2,1)}, bf16[256,1280]{1,0:T(8,128)(2,1)}, u32[]{:S(2)}, u32[]{:S(2)}) collective-permute-start(bf16[256,1280]{1,0:T(8,128)(2,1)} %bitcast.21.refs_2_), channel_id=1, source_target_pairs={{0,3},{1,0},{2,1},{3,2},{4,7},{5,4},{6,5},{7,6},{8,11},{9,8},{10,9... | collective-permute-start | bytes 1966088 | tf_op jit(solution)/shard_map/ppermute | solution.py:27
  55.6 19.2 %collective-permute-start.9 = (bf16[256,1280]{1,0:T(8,128)(2,1)}, bf16[256,1280]{1,0:T(8,128)(2,1)}, u32[]{:S(2)}, u32[]{:S(2)}) collective-permute-start(bf16[256,1280]{1,0:T(8,128)(2,1)} %bitcast.21.refs_2_), channel_id=1, source_target_pairs={{0,1},{1,2},{2,3},{3,0},{4,5},{5,6},{6,7},{7,4},{8,9},{9,10},{10,1... | collective-permute-start | bytes 1966088 | tf_op jit(solution)/shard_map/ppermute | solution.py:26
  56.8 32.1 %collective-permute-start.5 = (bf16[256,1280]{1,0:T(8,128)(2,1)S(1)}, bf16[256,1280]{1,0:T(8,128)(2,1)}, u32[]{:S(2)}, u32[]{:S(2)}) collective-permute-start(bf16[256,1280]{1,0:T(8,128)(2,1)S(1)} %bitcast.43), channel_id=1, source_target_pairs={{0,1},{1,2},{2,3},{3,0},{4,5},{5,6},{6,7},{7,4},{8,9},{9,10},{10,1... | collective-permute-start | bytes 1966088 | tf_op jit(solution)/shard_map/ppermute | solution.py:26
  56.8 33.7 %collective-permute-start.6 = (bf16[256,1280]{1,0:T(8,128)(2,1)S(1)}, bf16[256,1280]{1,0:T(8,128)(2,1)}, u32[]{:S(2)}, u32[]{:S(2)}) collective-permute-start(bf16[256,1280]{1,0:T(8,128)(2,1)S(1)} %bitcast.44), channel_id=1, source_target_pairs={{0,3},{1,0},{2,1},{3,2},{4,7},{5,4},{6,5},{7,6},{8,11},{9,8},{10,9... | collective-permute-start | bytes 1966088 | tf_op jit(solution)/shard_map/ppermute | solution.py:27
  60.1 54.8 %collective-permute-start.1 = (bf16[512,1280]{1,0:T(8,128)(2,1)}, bf16[512,1280]{1,0:T(8,128)(2,1)}, u32[]{:S(2)}, u32[]{:S(2)}) collective-permute-start(bf16[512,1280]{1,0:T(8,128)(2,1)} %bitcast.5.refs_2_), channel_id=1, source_target_pairs={{0,3},{1,0},{2,1},{3,2},{4,7},{5,4},{6,5},{7,6},{8,11},{9,8},{10,9... | collective-permute-start | bytes 3932168 | tf_op jit(solution)/shard_map/ppermute | solution.py:27
  69.5 68.1 %copy-start.18 = (bf16[4,1,1280]{2,1,0:T(2,128)(2,1)}, bf16[4,1,1280]{2,1,0:T(2,128)(2,1)S(1)}, u32[]{:S(2)}) copy-start(bf16[4,1,1280]{2,1,0:T(2,128)(2,1)S(1)} %reshape.114.refs_7_.refs_5_.refs_4_) | copy-start | bytes 30724
  75.8 41.0 %collective-permute-start.10 = (bf16[128,1280]{1,0:T(8,128)(2,1)S(1)}, bf16[128,1280]{1,0:T(8,128)(2,1)S(1)}, u32[]{:S(2)}, u32[]{:S(2)}) collective-permute-start(bf16[128,1280]{1,0:T(8,128)(2,1)S(1)} %slice.118), channel_id=1, source_target_pairs={{0,1},{1,2},{2,3},{3,0},{4,5},{5,6},{6,7},{7,4},{8,9},{9,10},{10,1... | collective-permute-start | bytes 983048 | tf_op jit(solution)/shard_map/ppermute | solution.py:28
  77.1 51.3 %collective-permute-start.12 = (bf16[128,1280]{1,0:T(8,128)(2,1)S(1)}, bf16[128,1280]{1,0:T(8,128)(2,1)S(1)}, u32[]{:S(2)}, u32[]{:S(2)}) collective-permute-start(bf16[128,1280]{1,0:T(8,128)(2,1)S(1)} %slice.119), channel_id=1, source_target_pairs={{0,3},{1,0},{2,1},{3,2},{4,7},{5,4},{6,5},{7,6},{8,11},{9,8},{10,9... | collective-permute-start | bytes 983048 | tf_op jit(solution)/shard_map/ppermute | solution.py:29
  90.5 47.1 %collective-permute-start.7 = (bf16[128,1280]{1,0:T(8,128)(2,1)}, bf16[128,1280]{1,0:T(8,128)(2,1)}, u32[]{:S(2)}, u32[]{:S(2)}) collective-permute-start(bf16[128,1280]{1,0:T(8,128)(2,1)} %slice.115), channel_id=1, source_target_pairs={{0,1},{1,2},{2,3},{3,0},{4,5},{5,6},{6,7},{7,4},{8,9},{9,10},{10,1... | collective-permute-start | bytes 983048 | tf_op jit(solution)/shard_map/ppermute | solution.py:28
  92.3 45.3 %collective-permute-start.8 = (bf16[128,1280]{1,0:T(8,128)(2,1)}, bf16[128,1280]{1,0:T(8,128)(2,1)}, u32[]{:S(2)}, u32[]{:S(2)}) collective-permute-start(bf16[128,1280]{1,0:T(8,128)(2,1)} %slice.116), channel_id=1, source_target_pairs={{0,3},{1,0},{2,1},{3,2},{4,7},{5,4},{6,5},{7,6},{8,11},{9,8},{10,9... | collective-permute-start | bytes 983048 | tf_op jit(solution)/shard_map/ppermute | solution.py:29
  114.8 41.2 %collective-permute-start.2 = (bf16[256,1280]{1,0:T(8,128)(2,1)}, bf16[256,1280]{1,0:T(8,128)(2,1)}, u32[]{:S(2)}, u32[]{:S(2)}) collective-permute-start(bf16[256,1280]{1,0:T(8,128)(2,1)} %slice.109), channel_id=1, source_target_pairs={{0,1},{1,2},{2,3},{3,0},{4,5},{5,6},{6,7},{7,4},{8,9},{9,10},{10,1... | collective-permute-start | bytes 1966088 | tf_op jit(solution)/shard_map/ppermute | solution.py:28
  116.8 39.2 %collective-permute-start.3 = (bf16[256,1280]{1,0:T(8,128)(2,1)}, bf16[256,1280]{1,0:T(8,128)(2,1)}, u32[]{:S(2)}, u32[]{:S(2)}) collective-permute-start(bf16[256,1280]{1,0:T(8,128)(2,1)} %slice.110), channel_id=1, source_target_pairs={{0,3},{1,0},{2,1},{3,2},{4,7},{5,4},{6,5},{7,6},{8,11},{9,8},{10,9... | collective-permute-start | bytes 1966088 | tf_op jit(solution)/shard_map/ppermute | solution.py:29
  130.7 18.6 %all-to-all-start.2 = ((bf16[16,16,896]{2,1,0:T(8,128)(2,1)}), bf16[16,16,896]{2,1,0:T(8,128)(2,1)S(1)}, u32[]{:S(2)}, u32[]{:S(2)}) async-start(bf16[16,16,896]{2,1,0:T(8,128)(2,1)} %project.7), calls=%async_computation.2 | async-start | bytes 917504 | tf_op jit(solution)/shard_map/all_to_all | solution.py:446
  149.3 21.6 %all-to-all-start.1 = ((bf16[16,16,896]{2,1,0:T(8,128)(2,1)}), bf16[16,16,896]{2,1,0:T(8,128)(2,1)S(1)}, u32[]{:S(2)}, u32[]{:S(2)}) async-start(bf16[16,16,896]{2,1,0:T(8,128)(2,1)} %copy-done.13), calls=%async_computation.1 | async-start | bytes 917504 | tf_op jit(solution)/shard_map/all_to_all | solution.py:446
  170.9 25.4 %all-to-all-start = ((bf16[16,32,1024]{2,1,0:T(8,128)(2,1)}), bf16[16,32,1024]{2,1,0:T(8,128)(2,1)}, u32[]{:S(2)}, u32[]{:S(2)}) async-start(bf16[16,32,1024]{2,1,0:T(8,128)(2,1)} %copy-done.9), calls=%async_computation | async-start | bytes 2097152 | tf_op jit(solution)/shard_map/all_to_all | solution.py:446
  178.8 35.1 %collective-permute-start.14 = (bf16[16,16,256]{2,1,0:T(8,128)(2,1)}, bf16[16,16,256]{2,1,0:T(8,128)(2,1)}, u32[]{:S(2)}, u32[]{:S(2)}) collective-permute-start(bf16[16,16,256]{2,1,0:T(8,128)(2,1)} %slice.121), channel_id=1, source_target_pairs={{0,4},{1,5},{2,6},{3,7},{8,12},{9,13},{10,14},{11,15},{16,20},{17,... | collective-permute-start | bytes 393224 | tf_op jit(solution)/shard_map/ppermute | solution.py:448
  180.8 33.1 %collective-permute-start.13 = (bf16[16,16,256]{2,1,0:T(8,128)(2,1)}, bf16[16,16,256]{2,1,0:T(8,128)(2,1)}, u32[]{:S(2)}, u32[]{:S(2)}) collective-permute-start(bf16[16,16,256]{2,1,0:T(8,128)(2,1)} %slice.120), channel_id=1, source_target_pairs={{0,4},{1,5},{2,6},{3,7},{8,12},{9,13},{10,14},{11,15},{16,20},{17,... | collective-permute-start | bytes 393224 | tf_op jit(solution)/shard_map/ppermute | solution.py:448
  198.1 12.8 %collective-permute-start.4 = (bf16[16,32,384]{2,1,0:T(8,128)(2,1)}, bf16[16,32,384]{2,1,0:T(8,128)(2,1)}, u32[]{:S(2)}, u32[]{:S(2)}) collective-permute-start(bf16[16,32,384]{2,1,0:T(8,128)(2,1)} %slice.111), channel_id=1, source_target_pairs={{0,4},{1,5},{2,6},{3,7},{8,12},{9,13},{10,14},{11,15},{16,20},{17,... | collective-permute-start | bytes 1179656 | tf_op jit(solution)/shard_map/ppermute | solution.py:448
  229.1 19.5 %all-to-all-start.4 = ((bf16[16,64,384]{2,1,0:T(8,128)(2,1)}), bf16[16,64,384]{2,1,0:T(8,128)(2,1)}, u32[]{:S(2)}, u32[]{:S(2)}) async-start(bf16[16,64,384]{2,1,0:T(8,128)(2,1)} %attend.3), calls=%async_computation.4 | async-start | bytes 1572864 | tf_op jit(solution)/shard_map/all_to_all | solution.py:462
  248.6 22.4 %collective-permute-start.22 = (bf16[1024,384]{1,0:T(8,128)(2,1)}, bf16[1024,384]{1,0:T(8,128)(2,1)S(1)}, u32[]{:S(2)}, u32[]{:S(2)}) collective-permute-start(bf16[1024,384]{1,0:T(8,128)(2,1)} %bitcast.28.refs_1_), channel_id=1, source_target_pairs={{0,1},{1,2},{2,3},{3,0},{4,5},{5,6},{6,7},{7,4},{8,9},{9,10},{10,1... | collective-permute-start | bytes 2359304 | tf_op jit(solution)/shard_map/ppermute | solution.py:26
  248.6 22.5 %collective-permute-start.23 = (bf16[1024,384]{1,0:T(8,128)(2,1)}, bf16[1024,384]{1,0:T(8,128)(2,1)S(1)}, u32[]{:S(2)}, u32[]{:S(2)}) collective-permute-start(bf16[1024,384]{1,0:T(8,128)(2,1)} %bitcast.28.refs_1_), channel_id=1, source_target_pairs={{0,3},{1,0},{2,1},{3,2},{4,7},{5,4},{6,5},{7,6},{8,11},{9,8},{10,9... | collective-permute-start | bytes 2359304 | tf_op jit(solution)/shard_map/ppermute | solution.py:27
  267.8 16.1 %collective-permute-start.15 = (bf16[1024,256]{1,0:T(8,128)(2,1)S(1)}, bf16[1024,256]{1,0:T(8,128)(2,1)S(1)}, u32[]{:S(2)}, u32[]{:S(2)}) collective-permute-start(bf16[1024,256]{1,0:T(8,128)(2,1)S(1)} %bitcast.40), channel_id=1, source_target_pairs={{0,1},{1,2},{2,3},{3,0},{4,5},{5,6},{6,7},{7,4},{8,9},{9,10},{10,1... | collective-permute-start | bytes 1572872 | tf_op jit(solution)/shard_map/ppermute | solution.py:26
  267.8 16.8 %collective-permute-start.17 = (bf16[1024,256]{1,0:T(8,128)(2,1)S(1)}, bf16[1024,256]{1,0:T(8,128)(2,1)S(1)}, u32[]{:S(2)}, u32[]{:S(2)}) collective-permute-start(bf16[1024,256]{1,0:T(8,128)(2,1)S(1)} %bitcast.41), channel_id=1, source_target_pairs={{0,3},{1,0},{2,1},{3,2},{4,7},{5,4},{6,5},{7,6},{8,11},{9,8},{10,9... | collective-permute-start | bytes 1572872 | tf_op jit(solution)/shard_map/ppermute | solution.py:27
  271.1 21.2 %collective-permute-start.24 = (bf16[512,384]{1,0:T(8,128)(2,1)S(1)}, bf16[512,384]{1,0:T(8,128)(2,1)S(1)}, u32[]{:S(2)}, u32[]{:S(2)}) collective-permute-start(bf16[512,384]{1,0:T(8,128)(2,1)S(1)} %slice.124), channel_id=1, source_target_pairs={{0,1},{1,2},{2,3},{3,0},{4,5},{5,6},{6,7},{7,4},{8,9},{9,10},{10,1... | collective-permute-start | bytes 1179656 | tf_op jit(solution)/shard_map/ppermute | solution.py:28
  271.2 21.8 %collective-permute-start.25 = (bf16[512,384]{1,0:T(8,128)(2,1)S(1)}, bf16[512,384]{1,0:T(8,128)(2,1)S(1)}, u32[]{:S(2)}, u32[]{:S(2)}) collective-permute-start(bf16[512,384]{1,0:T(8,128)(2,1)S(1)} %slice.125), channel_id=1, source_target_pairs={{0,3},{1,0},{2,1},{3,2},{4,7},{5,4},{6,5},{7,6},{8,11},{9,8},{10,9... | collective-permute-start | bytes 1179656 | tf_op jit(solution)/shard_map/ppermute | solution.py:29
  284.6 31.1 %collective-permute-start.16 = (bf16[512,256]{1,0:T(8,128)(2,1)}, bf16[512,256]{1,0:T(8,128)(2,1)S(1)}, u32[]{:S(2)}, u32[]{:S(2)}) collective-permute-start(bf16[512,256]{1,0:T(8,128)(2,1)} %slice.122), channel_id=1, source_target_pairs={{0,1},{1,2},{2,3},{3,0},{4,5},{5,6},{6,7},{7,4},{8,9},{9,10},{10,1... | collective-permute-start | bytes 786440 | tf_op jit(solution)/shard_map/ppermute | solution.py:28
  285.7 30.0 %collective-permute-start.18 = (bf16[512,256]{1,0:T(8,128)(2,1)}, bf16[512,256]{1,0:T(8,128)(2,1)}, u32[]{:S(2)}, u32[]{:S(2)}) collective-permute-start(bf16[512,256]{1,0:T(8,128)(2,1)} %slice.123), channel_id=1, source_target_pairs={{0,3},{1,0},{2,1},{3,2},{4,7},{5,4},{6,5},{7,6},{8,11},{9,8},{10,9... | collective-permute-start | bytes 786440 | tf_op jit(solution)/shard_map/ppermute | solution.py:29
  (29 other events, 217.3 us)
Sparse Core Ops, SparseCore 0:
  53.9 62.5 all-gather.2
where the time goes:
time: 328 us; the launch traced here: 327 us
  waiting for transfers between devices  107 us (33%)
  Pallas kernels  70.7 us (22%)
  starting transfers between devices  63.9 us (19%)
  local copies, waits for them, and re-layouts  49.8 us (15%)
  blocking collectives  15.9 us (5%)
  between operations  13.9 us (4%)
  other arithmetic  5.59 us (2%)
    ppermute x5, waiting for transfers between devices, ring_gather(): from_left = lax.ppermute(block, 'tensor', right)  53.5 us
    unnamed x62, local copies, waits for them, and re-layouts  28.6 us
    pallas_call x2, Pallas kernels, attend(): pl.pallas_call(kernel, out_shape=jax.ShapeDtypeStruct((pages, PAGE, heads...  26.8 us
    pallas_call x4, Pallas kernels, project(): pl.pallas_call(kernel, out_shape=out_shape, grid_spec=pltpu.PrefetchScala...  22.2 us
    pallas_call x3, Pallas kernels, mix(): pl.pallas_call(kernel, out_shape=out_shape, grid_spec=pltpu.PrefetchScala...  21.8 us
    all_to_all x3, starting transfers between devices, body(): rows = lax.all_to_all(rows, DP, split_axis=0, concat_axis=0, tiled=True)  21 us
    ppermute x5, waiting for transfers between devices, ring_gather(): from_right = lax.ppermute(block, 'tensor', left)  17.2 us
    ppermute x5, starting transfers between devices, ring_gather(): far_low = lax.ppermute(from_right[half:], 'tensor', left)  16.1 us
  transfers between devices with their start and end apart: 31, of which 13 were waited for; matrix products, arithmetic and copies ran while one was open for 8% of the time, Pallas kernels for 20%

commit v1 on v0

v1 whole, which is shorter than its diff:
```python
import math

import jax
import jax.numpy as jnp
from jax import lax
from jax.experimental import pallas as pl
from jax.experimental.pallas import tpu as pltpu
from jax.sharding import Mesh
from jax.sharding import PartitionSpec as P

HEAD = 128
PAGE = 64
EPSILON = 1e-06
DP = ("z", "xh", "core")
TENSOR = 4
FACTS = 128
DIGIT = 32
MIB = 1024 * 1024
SMALL = pl.CostEstimate(flops=1024, bytes_accessed=1024, transcendentals=0)


def to_right(block):
    return lax.ppermute(block, "tensor", [(i, (i + 1) % TENSOR) for i in range(TENSOR)])


def to_left(block):
    return lax.ppermute(block, "tensor", [(i, (i - 1) % TENSOR) for i in range(TENSOR)])


def ring_near(top, low):
    return (to_right(top), to_right(low)), (to_left(top), to_left(low))


def ring_far(left, right):
    return to_right(left), to_left(right)


def project_near_kernel(count, *refs):
    pieces, weights, gains = refs[: 2 * count], refs[2 * count : 3 * count], refs[3 * count]
    total, squares = refs[3 * count + 1 :]
    step = pl.program_id(0)
    for index in range(count):

        @pl.when(step == index)
        def _(index=index):
            for half in range(2):
                piece = pieces[2 * index + half]
                at = pl.ds(half * piece.shape[0], piece.shape[0])
                product, square = banded(piece, gains[index], weights[index])
                if index == 0:
                    total[at], squares[at] = product, square
                else:
                    total[at], squares[at] = total[at] + product, squares[at] + square


def banded(piece, gain, weights):
    wide = piece[...].astype(jnp.float32)
    scaled = (wide * gain.astype(jnp.float32)).astype(jnp.bfloat16)
    product = jnp.dot(scaled, weights[...], preferred_element_type=jnp.float32)
    return product, jnp.sum(wide * wide, axis=1, keepdims=True)


def project_near(pieces, weights, gains):
    count = len(pieces)
    half, width = pieces[0][0].shape
    rows = 2 * half
    pieces = [half for piece in pieces for half in piece]
    columns = weights[0].shape[1]
    sums = [(rows, columns), (rows, 1)]

    def kernel(*refs):
        project_near_kernel(count, *refs)

    def whole(shape):
        return pl.BlockSpec(shape, lambda k: (0,) * len(shape))

    return pl.pallas_call(
        kernel,
        out_shape=[jax.ShapeDtypeStruct(shape, jnp.float32) for shape in sums],
        grid=(count,),
        in_specs=[whole((half, width)) for _ in pieces]
        + [whole(a.shape) for a in (*weights, gains)],
        out_specs=[whole(shape) for shape in sums],
        compiler_params=pltpu.CompilerParams(vmem_limit_bytes=56 * MIB),
        cost_estimate=SMALL,
        name="project_near",
    )(*pieces, *weights, gains)


def project_far_kernel(blocks, page, top, low, weights, gain, bias, total, squares, queries, others):
    step = pl.program_id(0)
    pages, count, heads_wide = queries.shape
    columns = weights.shape[1]
    features = TENSOR * top.shape[1]

    def finish(piece):
        product, square = banded(piece, gain[0], weights)
        scale = lax.rsqrt((squares[...] + square) * (1.0 / features) + EPSILON)
        result = ((total[...] + product) * scale + bias[...]).astype(jnp.bfloat16)
        for item in range(pages // blocks):
            index = step * (pages // blocks) + item
            target = page[index]
            rows = result[item * count : (item + 1) * count]
            queries[target] = rows[:, :heads_wide]
            others[target, :, : columns - heads_wide] = rows[:, heads_wide:]
            lane = lax.broadcasted_iota(jnp.int32, (count, FACTS), 1)
            fact = jnp.zeros_like(lane)
            for place in range(3):
                fact = jnp.where(lane == place, page[(place + 1) * pages + index], fact)
            others[target, :, columns - heads_wide :] = fact.astype(jnp.float32).astype(jnp.bfloat16)

    pl.when(step < blocks // 2)(lambda: finish(top))
    pl.when(step >= blocks // 2)(lambda: finish(low))


def project_far(page, top, low, weights, gain, bias, carry, heads_wide):
    blocks = 4
    half, width = carry[0].shape[0] // 2, top.shape[1]
    columns = weights.shape[1]
    pages = page.shape[0] // 4
    block = 2 * half // blocks
    shapes = [
        (pages, 2 * half // pages, wide) for wide in (heads_wide, columns - heads_wide + FACTS)
    ]

    def kernel(*refs):
        project_far_kernel(blocks, *refs)

    def whole(shape):
        return pl.BlockSpec(shape, lambda r, page: (0,) * len(shape))

    return pl.pallas_call(
        kernel,
        out_shape=[jax.ShapeDtypeStruct(shape, jnp.bfloat16) for shape in shapes],
        grid_spec=pltpu.PrefetchScalarGridSpec(
            num_scalar_prefetch=1,
            grid=(blocks,),
            in_specs=[
                pl.BlockSpec((block, width), lambda r, page: (jnp.minimum(r, blocks // 2 - 1), 0)),
                pl.BlockSpec((block, width), lambda r, page: (jnp.maximum(r - blocks // 2, 0), 0)),
                whole(weights.shape),
                whole(gain.shape),
                whole(bias.shape),
                pl.BlockSpec((block, columns), lambda r, page: (r, 0)),
                pl.BlockSpec((block, 1), lambda r, page: (r, 0)),
            ],
            out_specs=[whole(shape) for shape in shapes],
        ),
        compiler_params=pltpu.CompilerParams(vmem_limit_bytes=28 * MIB),
        cost_estimate=SMALL,
        name="project_far",
    )(page, top, low, weights, gain, bias, *carry)


def attend_kernel(heads, first, source, sequence, context, queries, own, other, out, *scratch):
    keys, values, turned, best, total, summed = scratch
    pages = own.shape[0]
    half = pages * PAGE
    per = 4
    rows = per * PAGE
    blocks = pages // per
    lanes = heads * rows
    factor = math.log2(math.e) / math.sqrt(HEAD)

    def place_page(slot, carry):
        for base, lookup, array in ((0, 0, other), (half, pages, own)):
            page = source[lookup + slot]
            at = pl.ds(pl.multiple_of(base + slot * PAGE, PAGE), PAGE)
            keys[at, :] = array[page, :, :HEAD]
            values[at, :] = array[page, :, HEAD : 2 * HEAD]
        return carry

    lax.fori_loop(0, pages, place_page, 0)
    for block in range(2 * blocks):
        turned[block] = values[pl.ds(block * rows, rows), :].astype(jnp.float32).T.astype(jnp.bfloat16)

    def query_block(index, carry):
        slot = index * per
        query = jnp.concatenate(
            [
                queries[source[pages + slot + page], :, (first + head) * HEAD : (first + head + 1) * HEAD]
                for head in range(heads)
                for page in range(per)
            ],
            axis=0,
        )
        sequence_q = [sequence[pages + slot + page] for page in range(per)]
        within = lax.broadcasted_iota(jnp.int32, (1, lanes), 1) % rows
        seq_lane = jnp.full((1, lanes), sequence_q[per - 1], jnp.int32)
        for page in range(per - 2, -1, -1):
            seq_lane = jnp.where(within < (page + 1) * PAGE, sequence_q[page], seq_lane)

        def scores_of(block, diagonal):
            at = pl.ds(pl.multiple_of(block * rows, rows), rows)
            scores = lax.dot_general(
                keys[at, :], query, (((1,), (1,)), ((), ())), preferred_element_type=jnp.float32
            )
            cut = []
            for page in range(per):
                visible = seq_lane == sequence[block * per + page]
                if diagonal:
                    place = lax.broadcasted_iota(jnp.int32, (PAGE, lanes), 0) + page * PAGE
                    visible = visible & (place <= within)
                cut.append(jnp.where(visible, scores[page * PAGE : (page + 1) * PAGE], -1e30))
            return jnp.concatenate(cut, axis=0)

        def apply(block, weight):
            return jnp.dot(
                turned[block], weight.astype(jnp.bfloat16), preferred_element_type=jnp.float32
            )

        last = blocks + index
        scores = scores_of(last, True)
        top = jnp.max(scores, axis=0, keepdims=True)
        weight = jnp.exp2((scores - top) * factor)
        best[...] = top
        total[...] = jnp.sum(weight, axis=0, keepdims=True)
        summed[...] = apply(last, weight)

        def key_block(block, carry):
            seen = False
            for page in range(per):
                for seq in sequence_q:
                    seen = seen | (sequence[block * per + page] == seq)

            @pl.when(seen)
            def _():
                scores = scores_of(block, False)
                top = jnp.maximum(best[...], jnp.max(scores, axis=0, keepdims=True))
                weight = jnp.exp2((scores - top) * factor)
                fade = jnp.exp2((best[...] - top) * factor)
                best[...] = top
                total[...] = total[...] * fade + jnp.sum(weight, axis=0, keepdims=True)
                summed[...] = summed[...] * fade + apply(block, weight)

            return carry

        lax.fori_loop(jnp.where(context[0] > 0, 0, blocks), last, key_block, 0)
        result = (summed[...] / total[...]).T.astype(jnp.bfloat16)
        for head in range(heads):
            for page in range(per):
                start = head * rows + page * PAGE
                out[source[pages + slot + page], :, head * HEAD : (head + 1) * HEAD] = result[
                    start : start + PAGE
                ]
        return carry

    lax.fori_loop(0, blocks, query_block, 0)


def attend(heads, first, source, sequence, context, queries, own, other):
    pages = own.shape[0]

    def kernel(*refs):
        attend_kernel(heads, first, *refs)

    half = pages * PAGE
    lanes = heads * 4 * PAGE
    vmem = pl.BlockSpec(memory_space=pltpu.VMEM)
    smem = pl.BlockSpec(memory_space=pltpu.SMEM)
    return pl.pallas_call(
        kernel,
        out_shape=jax.ShapeDtypeStruct((pages, PAGE, heads * HEAD), jnp.bfloat16),
        in_specs=[smem] * 3 + [vmem] * 3,
        out_specs=vmem,
        scratch_shapes=[
            pltpu.VMEM((2 * half, HEAD), jnp.bfloat16),
            pltpu.VMEM((2 * half, HEAD), jnp.bfloat16),
            pltpu.VMEM((pages // 2, HEAD, 4 * PAGE), jnp.bfloat16),
            pltpu.VMEM((1, lanes), jnp.float32),
            pltpu.VMEM((1, lanes), jnp.float32),
            pltpu.VMEM((HEAD, lanes), jnp.float32),
        ],
        compiler_params=pltpu.CompilerParams(vmem_limit_bytes=20 * MIB),
        cost_estimate=SMALL,
        name="attend",
    )(source, sequence, context, queries, own, other)


def rows_of(w_out, cut):
    begin, end = cut
    return w_out[:, 0, 0, begin:end, :].reshape(-1, w_out.shape[-1])


def mix_near_kernel(steps, counts, carried, paged, page_of, me, *refs):
    refs = list(refs)
    pieces = [[refs.pop(0) for _ in range(count)] for count in counts]
    w_own, w_all = refs.pop(0), refs.pop(0)
    before = refs.pop(0) if carried else None
    hidden = refs.pop(0) if paged else None
    (total,) = refs
    step = pl.program_id(1)

    for index, (place, cut) in enumerate(steps):

        @pl.when(step == index)
        def _(index=index, place=place, cut=cut):
            if place == 0:
                band = w_own[8 * cut[0] : 8 * cut[1], :]
            else:
                band = rows_of(w_all, cut)
            start = 0
            for piece in pieces[index]:
                count = piece.shape[0]
                at = pl.ds(start, count)
                product = jnp.dot(piece[...], band, preferred_element_type=jnp.float32)
                if index > 0:
                    product = total[at] + product
                elif carried:
                    product = before[at] + product
                if index == len(steps) - 1 and paged:
                    rows = [hidden[page_of[(start + k) // PAGE]] for k in range(0, count, PAGE)]
                    product = product + jnp.concatenate(rows, axis=0).astype(jnp.float32)
                total[at] = product
                start += count


def mix_near(page_of, me, pieces, steps, w_out, w_all, before=None, hidden=None):
    rows = sum(p.shape[0] for p in pieces[0])
    outer, cuts, _, stored, columns = w_all.shape
    counts = [len(group) for group in pieces]

    def kernel(*refs):
        mix_near_kernel(steps, counts, before is not None, hidden is not None, *refs)

    def place_of(k):
        return sum(jnp.where(k == i, max(place, 1) - 1, 0) for i, (place, _) in enumerate(steps))

    flat = pl.BlockSpec((rows, columns), lambda n, k, page_of, me: (0, n))
    operands = [p for group in pieces for p in group]
    in_specs = [pl.BlockSpec(p.shape, lambda n, k, page_of, me: (0, 0)) for p in operands]
    operands += [w_out, w_all]
    in_specs += [
        pl.BlockSpec((w_out.shape[0], columns), lambda n, k, page_of, me: (0, me[0] * cuts + n)),
        pl.BlockSpec(
            (outer, 1, 1, stored, columns),
            lambda n, k, page_of, me: (0, n, place_of(k), 0, 0),
        ),
    ]
    if before is not None:
        operands.append(before)
        in_specs.append(flat)
    if hidden is not None:
        operands.append(hidden)
        in_specs.append(
            pl.BlockSpec((rows // PAGE, PAGE, columns), lambda n, k, page_of, me: (0, 0, n))
        )
    return pl.pallas_call(
        kernel,
        out_shape=jax.ShapeDtypeStruct((rows, cuts * columns), jnp.float32),
        grid_spec=pltpu.PrefetchScalarGridSpec(
            num_scalar_prefetch=2,
            grid=(cuts, len(steps)),
            in_specs=in_specs,
            out_specs=flat,
        ),
        compiler_params=pltpu.CompilerParams(vmem_limit_bytes=36 * MIB),
        cost_estimate=SMALL,
        name="mix_near",
    )(page_of, me, *operands)


def mix_far_kernel(blocks, cut, page_of, top, low, w_all, before, out):
    step = pl.program_id(1)
    band = rows_of(w_all, cut)

    def finish(piece):
        rows = before[...] + jnp.dot(piece[...], band, preferred_element_type=jnp.float32)
        rows = rows.astype(jnp.bfloat16)
        count = rows.shape[0] // PAGE
        for item in range(count):
            out[page_of[step * count + item]] = rows[item * PAGE : (item + 1) * PAGE]

    pl.when(step < blocks // 2)(lambda: finish(top))
    pl.when(step >= blocks // 2)(lambda: finish(low))


def mix_far(page_of, top, low, cut, w_all, before):
    blocks = 4
    half, width = top.shape
    outer, cuts, places, stored, columns = w_all.shape
    block = 2 * half // blocks
    pages = 2 * half // PAGE

    def kernel(*refs):
        mix_far_kernel(blocks, cut, *refs)

    return pl.pallas_call(
        kernel,
        out_shape=jax.ShapeDtypeStruct((pages, PAGE, cuts * columns), jnp.bfloat16),
        grid_spec=pltpu.PrefetchScalarGridSpec(
            num_scalar_prefetch=1,
            grid=(cuts, blocks),
            in_specs=[
                pl.BlockSpec((block, width), lambda n, r, page_of: (jnp.minimum(r, blocks // 2 - 1), 0)),
                pl.BlockSpec((block, width), lambda n, r, page_of: (jnp.maximum(r - blocks // 2, 0), 0)),
                pl.BlockSpec(
                    (outer, 1, 1, stored, columns), lambda n, r, page_of: (0, n, places - 1, 0, 0)
                ),
                pl.BlockSpec((block, columns), lambda n, r, page_of: (r, n)),
            ],
            out_specs=pl.BlockSpec((pages, PAGE, columns), lambda n, r, page_of: (0, 0, n)),
        ),
        compiler_params=pltpu.CompilerParams(vmem_limit_bytes=20 * MIB),
        cost_estimate=SMALL,
        name="mix_far",
    )(page_of, top, low, w_all, before)


def w_out_shares(w_out, context, outer_index, outer, cuts):
    columns = w_out.shape[1] // (2 * TENSOR)
    bands = []
    for first, end in cuts:
        depth = (end - first) * HEAD // outer
        bands.append(
            lax.dynamic_slice_in_dim(w_out, first * HEAD + outer_index * depth, depth, 0)
        )
    band = jnp.concatenate(bands, axis=0)
    me = lax.axis_index("tensor")
    right, far, left = [
        lax.dynamic_slice_in_dim(band, ((me + step) % TENSOR * 2 + context) * columns, columns, 1)
        for step in range(1, TENSOR)
    ]
    far = lax.ppermute(far, "tensor", [(i, (i + 2) % TENSOR) for i in range(TENSOR)])
    return [to_right(right), to_left(left), far]


def places(local, sequence):
    pages = local.shape[0]
    ladder = jnp.arange(pages, dtype=jnp.int32)
    hit = local[None, :] == ladder[:, None]
    source = jnp.sum(jnp.where(hit, ladder[None, :], 0), axis=1)
    return jnp.stack([source, jnp.sum(jnp.where(hit, sequence[None, :], 0), axis=1)])


def read_facts(facts):
    facts = facts.astype(jnp.float32).astype(jnp.int32)
    return places(facts[:, 0], facts[:, 1] * DIGIT + facts[:, 2])


def body(hidden, seq_id, dest_page, norm_gain, w_query, q_bias, w_key, w_value, v_bias, w_out):
    pages = dest_page.shape[0]
    me = lax.axis_index("tensor")
    context = lax.axis_index("context")
    heads = w_query.shape[1] // HEAD
    cuts = [(0, 3), (3, heads)]
    order = jnp.stack([me, (me + 3) % TENSOR, (me + 1) % TENSOR, (me + 2) % TENSOR]).astype(jnp.int32)
    sequence = seq_id[::PAGE]
    group = dest_page // pages
    page = jnp.concatenate([group, dest_page % pages, sequence // DIGIT, sequence % DIGIT])
    slots = jnp.arange(pages, dtype=jnp.int32)
    page_of = jnp.sum(jnp.where(group[None, :] == slots[:, None], slots[None, :], 0), axis=1)

    paged = hidden.reshape(pages, PAGE, hidden.shape[1])
    block = jnp.split(hidden, 2)
    w_query, w_key, w_value, block = lax.optimization_barrier((w_query, w_key, w_value, block))
    width, heads_wide = hidden.shape[1], w_query.shape[1]

    def band(array, index):
        return lax.dynamic_slice_in_dim(array, order[index] * width, width, 0)

    weights = [
        jnp.concatenate([band(w, index) for w in (w_query, w_key, w_value)], axis=1)
        for index in range(TENSOR)
    ]
    gains = [band(norm_gain, index)[None, :] for index in range(TENSOR)]
    near_gains, far_gain = jnp.stack(gains[:3]), gains[3][None]
    bias = jnp.concatenate([q_bias, jnp.zeros_like(v_bias), v_bias]).astype(jnp.float32)[None, :]
    hold = lax.optimization_barrier

    def exchange(rows):
        return lax.all_to_all(rows, DP, split_axis=0, concat_axis=0, tiled=True)

    left, right = ring_near(*block)
    shares = w_out_shares(w_out, context, lax.axis_index(("z", "xh")), 8, cuts)
    shares, _ = hold((shares, (left[0], right[1])))
    w_all = lax.all_gather(jnp.stack(shares), ("z", "xh", "context"), axis=0, tiled=False)
    w_all = w_all.reshape((8, 2) + w_all.shape[1:])
    left, right, weights, near_gains = hold((left, right, weights, near_gains))
    far = ring_far(left[0], right[1])
    carry = project_near((block, left, right), weights[:3], near_gains)
    queries, own = project_far(page, *far, weights[3], far_gain, bias, carry, heads_wide)
    own = exchange(own)
    queries, own = hold((queries, own))
    queries = exchange(queries)
    other = lax.ppermute(own, "context", [(0, 1)])

    here = read_facts(own[:, 0, 2 * HEAD : 2 * HEAD + 3])
    there = read_facts(other[:, 0, 2 * HEAD : 2 * HEAD + 3])
    there = jnp.where(context > 0, there, here)
    source = jnp.concatenate([there[0], here[0]])
    sequence = jnp.concatenate([there[1], here[1]])

    second = context.astype(jnp.int32).reshape(1)
    (first, end), (start, stop) = cuts
    part_a = attend(end - first, first, source, sequence, second, queries, own, other)
    queries, part_a = hold((queries, part_a))
    part_b = attend(stop - start, start, source, sequence, second, queries, own, other)
    part_a, part_b = hold((exchange(part_a), part_b))
    flat_a = part_a.reshape(pages * PAGE, -1)
    left, right = to_right(flat_a), to_left(flat_a)
    flat_b = exchange(part_b).reshape(pages * PAGE, -1)
    left, right, flat_b = hold((left, right, flat_b))
    bands = [(first * HEAD // 8, end * HEAD // 8) for first, end in cuts]
    here = me.astype(jnp.int32).reshape(1)
    half = pages * PAGE // 2
    far = ring_far(left[:half], right[half:])
    steps = [(0, bands[0]), (1, bands[0]), (2, bands[0]), (0, bands[1])]
    pieces = [(flat_a,), (left,), (right,), (flat_b,)]
    total = mix_near(page_of, here, pieces, steps, w_out, w_all)
    left, right = to_right(flat_b), to_left(flat_b)
    left, right, far, total = hold((left, right, far, total))
    last = ring_far(left[:half], right[half:])
    steps = [(3, bands[0]), (1, bands[1]), (2, bands[1])]
    total = mix_near(page_of, here, [far, (left,), (right,)], steps, w_out, w_all, total, paged)
    result = mix_far(page_of, *last, bands[1], w_all, total)
    return result.reshape(hidden.shape)


def solution(mesh):
    fine = Mesh(
        mesh.devices.reshape(4, 2, 2, 2, TENSOR), ("z", "xh", "core", "context", "tensor")
    )
    rows = DP + ("context",)
    return jax.shard_map(
        body,
        mesh=fine,
        in_specs=(
            P(rows, "tensor"),
            P(rows),
            P(rows),
            P(),
            P(None, "tensor"),
            P("tensor"),
            P(None, "tensor"),
            P(None, "tensor"),
            P("tensor"),
            P("tensor", None),
        ),
        out_specs=P(rows, "tensor"),
        check_vma=False,
    )
```

time: 328 us -> 271 us (0.83)
  local copies, waits for them, and re-layouts: 49.8 us -> 20.7 us
  starting transfers between devices: 63.9 us -> 36.4 us
  waiting for transfers between devices: 107 us -> 82.4 us
  blocking collectives: 15.9 us -> 36.9 us
    all_to_all x1 -> x2, blocking collectives: 15.9 us -> 36.9 us  [exchange(): return lax.all_to_all(rows, DP, split_axis=0, concat_axis=0, tiled=True)]
    unnamed x62 -> x28, local copies, waits for them, and re-layouts: 28.6 us -> 8.78 us
    all_to_all x4 -> x2, starting transfers between devices: 25.5 us -> 8.22 us  [exchange(): return lax.all_to_all(rows, DP, split_axis=0, concat_axis=0, tiled=True)]
    slice x15 -> x4, local copies, waits for them, and re-layouts: 17.8 us -> 1.62 us  [the longest x2 1.59 us: body(): far = ring_far(left[:half], right[half:])]
    ppermute x26 -> x18, waiting for transfers between devices: 89.6 us -> 74.9 us  [the longest x8 54.3 us: to_right(): lax.ppermute(block, 'tensor', [(i, (i + 1) % TENSOR) for i in range(TENSO...]
    ppermute x26 -> x18, starting transfers between devices: 38.4 us -> 28.2 us  [the longest x8 20.8 us: to_left(): lax.ppermute(block, 'tensor', [(i, (i - 1) % TENSOR) for i in range(TENSO...]
    all_to_all x4 -> x2, waiting for transfers between devices: 17.3 us -> 7.41 us  [exchange(): return lax.all_to_all(rows, DP, split_axis=0, concat_axis=0, tiled=True)]
    concatenate x0 -> x5, other arithmetic: none -> 5.1 us  [the longest x4 5.06 us: body(): jnp.concatenate([band(w, index) for w in (w_query, w_key, w_value)], axis=1)]
  transfers between devices with their start and end apart: 31 -> 21, of which waited for: 13 -> 9; matrix products, arithmetic and copies ran while one was open for 8% -> 5% of each run, Pallas kernels for 20% -> 24%
where the time goes in v1:
time: 271 us; the launch traced here: 268 us
  waiting for transfers between devices  82.4 us (30%)
  Pallas kernels  70.8 us (26%)
  blocking collectives  36.9 us (14%)
  starting transfers between devices  36.4 us (13%)
  local copies, waits for them, and re-layouts  20.7 us (8%)
  between operations  13.7 us (5%)
  other arithmetic  7.07 us (3%)
    ppermute x8, waiting for transfers between devices, to_right(): lax.ppermute(block, 'tensor', [(i, (i + 1) % TENSOR) for i in range(TENSO...  54.3 us
    all_to_all x2, blocking collectives, exchange(): return lax.all_to_all(rows, DP, split_axis=0, concat_axis=0, tiled=True)  36.9 us
    pallas_call x2, Pallas kernels, attend(): pl.pallas_call(kernel, out_shape=jax.ShapeDtypeStruct((pages, PAGE, heads...  24 us
    ppermute x8, starting transfers between devices, to_left(): lax.ppermute(block, 'tensor', [(i, (i - 1) % TENSOR) for i in range(TENSO...  20.8 us
    pallas_call x2, Pallas kernels, mix_near(): pl.pallas_call(kernel, out_shape=jax.ShapeDtypeStruct((rows, cuts * colum...  19.1 us
    ppermute x1, waiting for transfers between devices, body(): other = lax.ppermute(own, 'context', [(0, 1)])  17.2 us
    pallas_call x1, Pallas kernels, project_near(): pl.pallas_call(kernel, out_shape=[jax.ShapeDtypeStruct(shape, jnp.float32...  16.5 us
    unnamed x28, local copies, waits for them, and re-layouts  8.78 us
  transfers between devices with their start and end apart: 21, of which 9 were waited for; matrix products, arithmetic and copies ran while one was open for 5% of the time, Pallas kernels for 24%

profile of v1, /device:TPU:2, one launch (start us, length us, event | category | flops | bytes accessed | tf_op | source)
XLA Modules:
  0.0 268.1 jit_solution(232101738939852579)
XLA Ops:
  6.5 3.5 %fusion.6 = (bf16[512,1280]{1,0:T(8,128)(2,1)}, bf16[512,1280]{1,0:T(8,128)(2,1)}) fusion(bf16[1024,1280]{1,0:T(8,128)(2,1)} %param.10), kind=kLoop, calls=%fused_computation.63 | loop fusion | bytes 5242880 | tf_op jit(solution)/shard_map/split | solution.py:455
  11.6 1.7 collective-permute-start.3
  15.8 2.9 %collective-permute-start.14 = (bf16[80,640]{1,0:T(8,128)(2,1)S(1)}, bf16[80,640]{1,0:T(8,128)(2,1)S(1)}, u32[]{:S(2)}, u32[]{:S(2)}) collective-permute-start(bf16[80,640]{1,0:T(8,128)(2,1)S(1)} %get-tuple-element.95), channel_id=1, source_target_pairs={{0,3},{1,0},{2,1},{3,2},{4,7},{5,4},{6,5},{7,6},{8,11},{9,8},{10,9... | collective-permute-start | bytes 307208 | tf_op jit(solution)/shard_map/ppermute | solution.py:27
  19.4 24.7 %collective-permute-done.13 = bf16[80,640]{1,0:T(8,128)(2,1)S(1)} collective-permute-done((bf16[80,640]{1,0:T(8,128)(2,1)S(1)}, bf16[80,640]{1,0:T(8,128)(2,1)S(1)}, u32[]{:S(2)}, u32[]{:S(2)}) %collective-permute-start.13) | collective-permute-done | bytes 102432 | tf_op jit(solution)/shard_map/ppermute | solution.py:23
  45.8 1.8 collective-permute-done.15
  49.6 2.1 collective-permute-start.2
  52.0 3.5 %constant_dynamic-slice_fusion.4 = (bf16[1280,640]{1,0:T(8,128)(2,1)S(1)}, bf16[1280,640]{1,0:T(8,128)(2,1)S(1)}, bf16[1280,640]{1,0:T(8,128)(2,1)S(1)}, bf16[1280,640]{1,0:T(8,128)(2,1)S(1)}) fusion(bf16[5120,640]{1,0:T(8,128)(2,1)} %param.14, s32[]{:T(128)S(6)} %select_n.113, s32[]{:T(128)S(6)} %select_n.111, s32[]{:T(128)S(6)} %select_n.109, s32[]{:T(128)S(6)} %select_n.107), kind=kLoop, calls=%fused_computation.30 | loop fusion | bytes 13107216 | tf_op jit(solution)/shard_map/dynamic_slice | solution.py:460
  61.2 18.1 %collective-permute-done.1.refs_3_ = bf16[512,1280]{1,0:T(8,128)(2,1)} collective-permute-done((bf16[512,1280]{1,0:T(8,128)(2,1)}, bf16[512,1280]{1,0:T(8,128)(2,1)}, u32[]{:S(2)}, u32[]{:S(2)}) %collective-permute-start.1) | collective-permute-done | bytes 1310752 | tf_op jit(solution)/shard_map/ppermute | solution.py:23
  79.3 3.2 %collective-permute-start.5 = (bf16[512,1280]{1,0:T(8,128)(2,1)}, bf16[512,1280]{1,0:T(8,128)(2,1)}, u32[]{:S(2)}, u32[]{:S(2)}) collective-permute-start(bf16[512,1280]{1,0:T(8,128)(2,1)} %collective-permute-done.3.refs_5_), channel_id=1, source_target_pairs={{0,3},{1,0},{2,1},{3,2},{4,7},{5,4},{6,5},{7,6},{8,11},{9,8},{10,9... | collective-permute-start | bytes 3932168 | tf_op jit(solution)/shard_map/ppermute | solution.py:27
  83.5 16.5 %project_near.1 = (f32[1024,896]{1,0:T(8,128)}, f32[1024,1]{1,0:T(8,128)}) custom-call(bf16[512,1280]{1,0:T(8,128)(2,1)} %get-tuple-element.40.refs_0_, bf16[512,1280]{1,0:T(8,128)(2,1)} %get-tuple-element.41.refs_1_, bf16[512,1280]{1,0:T(8,128)(2,1)} %collective-permute-done.refs_2_, bf16[512,1280]{1,0:T(8,128)(2,1)} %collective-permute-done.1.refs_3_, ...), custom_call_target="tpu_custom_call" | custom-call | flops 1024 | bytes 1024 | tf_op jit(solution)/shard_map/project_near/pallas_call | solution.py:77
  100.1 9.2 %collective-permute-done.4.refs_1_ = bf16[512,1280]{1,0:T(8,128)(2,1)} collective-permute-done((bf16[512,1280]{1,0:T(8,128)(2,1)}, bf16[512,1280]{1,0:T(8,128)(2,1)}, u32[]{:S(2)}, u32[]{:S(2)}) %collective-permute-start.4) | collective-permute-done | bytes 1310752 | tf_op jit(solution)/shard_map/ppermute | solution.py:23
  109.3 2.0 copy-done.4
  112.4 5.8 %project_far.1 = (bf16[16,64,640]{2,1,0:T(8,128)(2,1)S(1)}, bf16[16,64,384]{2,1,0:T(8,128)(2,1)S(1)}) custom-call(s32[64]{0:T(128)S(1)} %pad_add_fusion.refs_0_, bf16[512,1280]{1,0:T(8,128)(2,1)} %collective-permute-done.4.refs_1_, bf16[512,1280]{1,0:T(8,128)(2,1)} %collective-permute-done.5.refs_2_, bf16[1280,896]{1,0:T(8,128)(2,1)S(1)} %pad_maximum_fusion.3.refs_3_, ...), custom_call_target="tpu_custom_call" | custom-call | flops 1024 | bytes 1024 | tf_op jit(solution)/shard_map/project_far/pallas_call | solution.py:132
  118.1 22.0 %all_to_all.20.refs_4_ = bf16[16,64,384]{2,1,0:T(8,128)(2,1)S(1)} all-to-all(bf16[16,64,384]{2,1,0:T(8,128)(2,1)S(1)} %get-tuple-element.57), channel_id=1, replica_groups=mesh['z'=4,'xh'=2,'core'=2,'context'=2,'tensor'=4] {'z','xh','core'}, dimensions={0} | all-to-all | bytes 1572864 | tf_op jit(solution)/shard_map/all_to_all | solution.py:472
  141.4 3.7 %all-to-all-start.1 = ((bf16[16,64,640]{2,1,0:T(8,128)(2,1)}), bf16[16,64,640]{2,1,0:T(8,128)(2,1)S(1)}, u32[]{:S(2)}, u32[]{:S(2)}) async-start(bf16[16,64,640]{2,1,0:T(8,128)(2,1)} %copy-done.6), calls=%async_computation.1 | async-start | bytes 2621440 | tf_op jit(solution)/shard_map/all_to_all | solution.py:472
  145.2 17.2 %collective-permute-done.6.refs_5_ = bf16[16,64,384]{2,1,0:T(8,128)(2,1)S(1)} collective-permute-done((bf16[16,64,384]{2,1,0:T(8,128)(2,1)S(1)}, bf16[16,64,384]{2,1,0:T(8,128)(2,1)S(1)}, u32[]{:S(2)}, u32[]{:S(2)}) %collective-permute-start.6) | collective-permute-done | bytes 786464 | tf_op jit(solution)/shard_map/ppermute | solution.py:486
  162.9 3.1 %all-to-all-done.1.refs_3_ = bf16[16,64,640]{2,1,0:T(8,128)(2,1)S(1)} async-done(((bf16[16,64,640]{2,1,0:T(8,128)(2,1)}), bf16[16,64,640]{2,1,0:T(8,128)(2,1)S(1)}, u32[]{:S(2)}, u32[]{:S(2)}) %all-to-all-start.1) | async-done | bytes 1310752 | tf_op jit(solution)/shard_map/all_to_all | solution.py:472
  166.0 13.4 %attend.2 = bf16[16,64,384]{2,1,0:T(8,128)(2,1)S(1)} custom-call(s32[32]{0:T(128)S(1)} %pad_add_fusion.1.refs_0_, s32[32]{0:T(128)S(1)} %pad_add_fusion.2.refs_1_, s32[1]{0:T(128)} %bitcast.13.refs_2_, bf16[16,64,640]{2,1,0:T(8,128)(2,1)S(1)} %all-to-all-done.1.refs_3_, bf16[16,64,384]{2,1,0:T(8,128)(2,1)S(1)} %all_to_all.20.refs_4_, ...), custom_call_target="tpu_custom_call" | custom-call | flops 1024 | bytes 1024 | tf_op jit(solution)/shard_map/attend/pallas_call | solution.py:261
  180.2 4.5 %all-to-all-start.2 = ((bf16[16,64,384]{2,1,0:T(8,128)(2,1)}), bf16[16,64,384]{2,1,0:T(8,128)(2,1)}, u32[]{:S(2)}, u32[]{:S(2)}) async-start(bf16[16,64,384]{2,1,0:T(8,128)(2,1)} %copy-done.5), calls=%async_computation.2 | async-start | bytes 1572864 | tf_op jit(solution)/shard_map/all_to_all | solution.py:472
  184.7 10.7 %attend.3 = bf16[16,64,256]{2,1,0:T(8,128)(2,1)S(1)} custom-call(s32[32]{0:T(128)S(1)} %pad_add_fusion.1.refs_0_, s32[32]{0:T(128)S(1)} %pad_add_fusion.2.refs_1_, s32[1]{0:T(128)} %bitcast.13.refs_2_, bf16[16,64,640]{2,1,0:T(8,128)(2,1)S(1)} %all-to-all-done.1.refs_3_, bf16[16,64,384]{2,1,0:T(8,128)(2,1)S(1)} %all_to_all.20.refs_4_, ...), custom_call_target="tpu_custom_call" | custom-call | flops 1024 | bytes 1024 | tf_op jit(solution)/shard_map/attend/pallas_call | solution.py:261
  195.4 4.3 %all-to-all-done.2 = bf16[16,64,384]{2,1,0:T(8,128)(2,1)} async-done(((bf16[16,64,384]{2,1,0:T(8,128)(2,1)}), bf16[16,64,384]{2,1,0:T(8,128)(2,1)}, u32[]{:S(2)}, u32[]{:S(2)}) %all-to-all-start.2) | async-done | bytes 786464 | tf_op jit(solution)/shard_map/all_to_all | solution.py:472
  200.6 2.4 collective-permute-start.8
  203.0 15.0 %all_to_all.21 = bf16[16,64,256]{2,1,0:T(8,128)(2,1)S(1)} all-to-all(bf16[16,64,256]{2,1,0:T(8,128)(2,1)S(1)} %attend.3), channel_id=1, replica_groups=mesh['z'=4,'xh'=2,'core'=2,'context'=2,'tensor'=4] {'z','xh','core'}, dimensions={0} | all-to-all | bytes 1048576 | tf_op jit(solution)/shard_map/all_to_all | solution.py:472
  217.9 2.3 collective-permute-done.7.refs_3_
  221.4 2.1 collective-permute-start.10
  225.0 3.2 %collective-permute-start.12 = (bf16[512,384]{1,0:T(8,128)(2,1)}, bf16[512,384]{1,0:T(8,128)(2,1)}, u32[]{:S(2)}, u32[]{:S(2)}) collective-permute-start(bf16[512,384]{1,0:T(8,128)(2,1)} %slice.57), channel_id=1, source_target_pairs={{0,3},{1,0},{2,1},{3,2},{4,7},{5,4},{6,5},{7,6},{8,11},{9,8},{10,9... | collective-permute-start | bytes 1179656 | tf_op jit(solution)/shard_map/ppermute | solution.py:27
  228.4 2.4 copy-done
  230.8 10.2 %mix_near.2.refs_8_ = f32[1024,1280]{1,0:T(8,128)S(1)} custom-call(s32[16]{0:T(128)S(1)} %select_reduce_fusion.4.refs_0_, s32[1]{0:T(128)} %bitcast.16.refs_1_, bf16[1024,384]{1,0:T(8,128)(2,1)} %bitcast.14.refs_2_, bf16[1024,384]{1,0:T(8,128)(2,1)S(1)} %collective-permute-done.7.refs_3_, bf16[1024,384]{1,0:T(8,128)(2,1)S(1)} %collective-permute-done.8.refs_4_, ...), custom_call_target="tpu_custom_call" | custom-call | flops 1024 | bytes 1024 | tf_op jit(solution)/shard_map/mix_near/pallas_call | solution.py:348
  241.1 2.4 copy-done.2
  243.7 3.2 %collective-permute-start.17 = (bf16[512,256]{1,0:T(8,128)(2,1)S(1)}, bf16[512,256]{1,0:T(8,128)(2,1)S(1)}, u32[]{:S(2)}, u32[]{:S(2)}) collective-permute-start(bf16[512,256]{1,0:T(8,128)(2,1)S(1)} %slice.59), channel_id=1, source_target_pairs={{0,3},{1,0},{2,1},{3,2},{4,7},{5,4},{6,5},{7,6},{8,11},{9,8},{10,9... | collective-permute-start | bytes 786440 | tf_op jit(solution)/shard_map/ppermute | solution.py:27
  246.9 8.9 %mix_near.3.refs_4_ = f32[1024,1280]{1,0:T(8,128)S(1)} custom-call(s32[16]{0:T(128)S(1)} %select_reduce_fusion.4.refs_0_, s32[1]{0:T(128)} %bitcast.16.refs_1_, bf16[512,384]{1,0:T(8,128)(2,1)S(1)} %collective-permute-done.11.refs_2_, bf16[512,384]{1,0:T(8,128)(2,1)} %collective-permute-done.12.refs_3_, ...), custom_call_target="tpu_custom_call" | custom-call | flops 1024 | bytes 1024 | tf_op jit(solution)/shard_map/mix_near/pallas_call | solution.py:348
  255.8 5.4 %mix_far.1 = bf16[16,64,1280]{2,1,0:T(8,128)(2,1)} custom-call(s32[16]{0:T(128)S(1)} %select_reduce_fusion.4.refs_0_, bf16[512,256]{1,0:T(8,128)(2,1)S(1)} %collective-permute-done.16.refs_1_, bf16[512,256]{1,0:T(8,128)(2,1)S(1)} %collective-permute-done.17.refs_2_, bf16[8,2,3,80,640]{4,3,2,1,0:T(8,128)(2,1)S(1)} %bitcast.31, f32[1024,1280]{1,0:T(8,128)S(1)} %mix_near.3.refs_4_), custom_call_target="tpu_custom_call" | custom-call | flops 1024 | bytes 1024 | tf_op jit(solution)/shard_map/mix_far/pallas_call | solution.py:388
  (90 shorter events, 23.1 us)
Async XLA Ops:
  6.5 221.9 %all-gather.3.cloned.1.call-start = ((), (), s32[]{:S(2)}) async-start(), calls=%async_computation.4 | async-start | bytes 5222400 | tf_op jit(solution)/shard_map/all_gather | solution.py:477
  10.0 41.7 %copy-start.10 = (bf16[5120]{0:T(1024)(128)(2,1)S(1)}, bf16[5120]{0:T(1024)(128)(2,1)}, u32[]{:S(2)}) copy-start(bf16[5120]{0:T(1024)(128)(2,1)} %param.13) | copy-start | bytes 30724
  10.0 41.8 %copy-start.8 = (bf16[5120,128]{1,0:T(8,128)(2,1)S(1)}, bf16[5120,128]{1,0:T(8,128)(2,1)}, u32[]{:S(2)}) copy-start(bf16[5120,128]{1,0:T(8,128)(2,1)} %param.17) | copy-start | bytes 3932164
  10.0 37.6 %collective-permute-start = (bf16[512,1280]{1,0:T(8,128)(2,1)}, bf16[512,1280]{1,0:T(8,128)(2,1)}, u32[]{:S(2)}, u32[]{:S(2)}) collective-permute-start(bf16[512,1280]{1,0:T(8,128)(2,1)} %get-tuple-element.40.refs_0_), channel_id=1, source_target_pairs={{0,1},{1,2},{2,3},{3,0},{4,5},{5,6},{6,7},{7,4},{8,9},{9,10},{10,1... | collective-permute-start | bytes 3932168 | tf_op jit(solution)/shard_map/ppermute | solution.py:23
  11.6 36.0 %collective-permute-start.3 = (bf16[512,1280]{1,0:T(8,128)(2,1)}, bf16[512,1280]{1,0:T(8,128)(2,1)}, u32[]{:S(2)}, u32[]{:S(2)}) collective-permute-start(bf16[512,1280]{1,0:T(8,128)(2,1)} %get-tuple-element.41.refs_1_), channel_id=1, source_target_pairs={{0,3},{1,0},{2,1},{3,2},{4,7},{5,4},{6,5},{7,6},{8,11},{9,8},{10,9... | collective-permute-start | bytes 3932168 | tf_op jit(solution)/shard_map/ppermute | solution.py:27
  15.3 36.6 %copy-start.9 = (bf16[5120,128]{1,0:T(8,128)(2,1)S(1)}, bf16[5120,128]{1,0:T(8,128)(2,1)}, u32[]{:S(2)}) copy-start(bf16[5120,128]{1,0:T(8,128)(2,1)} %param.16) | copy-start | bytes 3932164
  15.4 28.8 %collective-permute-start.13 = (bf16[80,640]{1,0:T(8,128)(2,1)S(1)}, bf16[80,640]{1,0:T(8,128)(2,1)S(1)}, u32[]{:S(2)}, u32[]{:S(2)}) collective-permute-start(bf16[80,640]{1,0:T(8,128)(2,1)S(1)} %get-tuple-element.94), channel_id=1, source_target_pairs={{0,1},{1,2},{2,3},{3,0},{4,5},{5,6},{6,7},{7,4},{8,9},{9,10},{10,1... | collective-permute-start | bytes 307208 | tf_op jit(solution)/shard_map/ppermute | solution.py:23
  15.8 30.0 %collective-permute-start.14 = (bf16[80,640]{1,0:T(8,128)(2,1)S(1)}, bf16[80,640]{1,0:T(8,128)(2,1)S(1)}, u32[]{:S(2)}, u32[]{:S(2)}) collective-permute-start(bf16[80,640]{1,0:T(8,128)(2,1)S(1)} %get-tuple-element.95), channel_id=1, source_target_pairs={{0,3},{1,0},{2,1},{3,2},{4,7},{5,4},{6,5},{7,6},{8,11},{9,8},{10,9... | collective-permute-start | bytes 307208 | tf_op jit(solution)/shard_map/ppermute | solution.py:27
  18.7 28.9 %collective-permute-start.15 = (bf16[80,640]{1,0:T(8,128)(2,1)S(1)}, bf16[80,640]{1,0:T(8,128)(2,1)S(1)}, u32[]{:S(2)}, u32[]{:S(2)}) collective-permute-start(bf16[80,640]{1,0:T(8,128)(2,1)S(1)} %get-tuple-element.93), channel_id=1, source_target_pairs={{0,2},{1,3},{2,0},{3,1},{4,6},{5,7},{6,4},{7,5},{8,10},{9,11},{10,... | collective-permute-start | bytes 307208 | tf_op jit(solution)/shard_map/ppermute | solution.py:424
  48.4 30.9 %collective-permute-start.1 = (bf16[512,1280]{1,0:T(8,128)(2,1)}, bf16[512,1280]{1,0:T(8,128)(2,1)}, u32[]{:S(2)}, u32[]{:S(2)}) collective-permute-start(bf16[512,1280]{1,0:T(8,128)(2,1)} %get-tuple-element.41.refs_1_), channel_id=1, source_target_pairs={{0,1},{1,2},{2,3},{3,0},{4,5},{5,6},{6,7},{7,4},{8,9},{9,10},{10,1... | collective-permute-start | bytes 3932168 | tf_op jit(solution)/shard_map/ppermute | solution.py:23
  49.6 29.7 %collective-permute-start.2 = (bf16[512,1280]{1,0:T(8,128)(2,1)}, bf16[512,1280]{1,0:T(8,128)(2,1)}, u32[]{:S(2)}, u32[]{:S(2)}) collective-permute-start(bf16[512,1280]{1,0:T(8,128)(2,1)} %get-tuple-element.40.refs_0_), channel_id=1, source_target_pairs={{0,3},{1,0},{2,1},{3,2},{4,7},{5,4},{6,5},{7,6},{8,11},{9,8},{10,9... | collective-permute-start | bytes 3932168 | tf_op jit(solution)/shard_map/ppermute | solution.py:27
  61.0 22.3 %copy-start.11 = (bf16[640]{0:T(1024)(128)(2,1)S(1)}, bf16[640]{0:T(1024)(128)(2,1)}, u32[]{:S(2)}) copy-start(bf16[640]{0:T(1024)(128)(2,1)} %param.15) | copy-start | bytes 3844
  61.0 22.4 %copy-start.13 = (s32[16]{0:T(128)S(1)}, s32[16]{0:T(128)}, u32[]{:S(2)}) copy-start(s32[16]{0:T(128)} %param.12) | copy-start | bytes 196
  61.0 22.5 %copy-start.12 = (bf16[128]{0:T(256)(128)(2,1)S(1)}, bf16[128]{0:T(256)(128)(2,1)}, u32[]{:S(2)}) copy-start(bf16[128]{0:T(256)(128)(2,1)} %param.18) | copy-start | bytes 772
  79.3 30.0 %collective-permute-start.4 = (bf16[512,1280]{1,0:T(8,128)(2,1)}, bf16[512,1280]{1,0:T(8,128)(2,1)}, u32[]{:S(2)}, u32[]{:S(2)}) collective-permute-start(bf16[512,1280]{1,0:T(8,128)(2,1)} %collective-permute-done.refs_2_), channel_id=1, source_target_pairs={{0,1},{1,2},{2,3},{3,0},{4,5},{5,6},{6,7},{7,4},{8,9},{9,10},{10,1... | collective-permute-start | bytes 3932168 | tf_op jit(solution)/shard_map/ppermute | solution.py:23
  79.3 30.0 %collective-permute-start.5 = (bf16[512,1280]{1,0:T(8,128)(2,1)}, bf16[512,1280]{1,0:T(8,128)(2,1)}, u32[]{:S(2)}, u32[]{:S(2)}) collective-permute-start(bf16[512,1280]{1,0:T(8,128)(2,1)} %collective-permute-done.3.refs_5_), channel_id=1, source_target_pairs={{0,3},{1,0},{2,1},{3,2},{4,7},{5,4},{6,5},{7,6},{8,11},{9,8},{10,9... | collective-permute-start | bytes 3932168 | tf_op jit(solution)/shard_map/ppermute | solution.py:27
  118.1 22.0 %copy-start.6 = (bf16[16,64,640]{2,1,0:T(8,128)(2,1)}, bf16[16,64,640]{2,1,0:T(8,128)(2,1)S(1)}, u32[]{:S(2)}) copy-start(bf16[16,64,640]{2,1,0:T(8,128)(2,1)S(1)} %get-tuple-element.58) | copy-start | bytes 3932164
  140.1 22.4 %collective-permute-start.6 = (bf16[16,64,384]{2,1,0:T(8,128)(2,1)S(1)}, bf16[16,64,384]{2,1,0:T(8,128)(2,1)S(1)}, u32[]{:S(2)}, u32[]{:S(2)}) collective-permute-start(bf16[16,64,384]{2,1,0:T(8,128)(2,1)S(1)} %all_to_all.20.refs_4_), channel_id=1, source_target_pairs={{0,4},{1,5},{2,6},{3,7},{8,12},{9,13},{10,14},{11,15},{16,20},{17,... | collective-permute-start | bytes 2359304 | tf_op jit(solution)/shard_map/ppermute | solution.py:486
  141.4 24.6 %all-to-all-start.1 = ((bf16[16,64,640]{2,1,0:T(8,128)(2,1)}), bf16[16,64,640]{2,1,0:T(8,128)(2,1)S(1)}, u32[]{:S(2)}, u32[]{:S(2)}) async-start(bf16[16,64,640]{2,1,0:T(8,128)(2,1)} %copy-done.6), calls=%async_computation.1 | async-start | bytes 2621440 | tf_op jit(solution)/shard_map/all_to_all | solution.py:472
  180.2 19.5 %all-to-all-start.2 = ((bf16[16,64,384]{2,1,0:T(8,128)(2,1)}), bf16[16,64,384]{2,1,0:T(8,128)(2,1)}, u32[]{:S(2)}, u32[]{:S(2)}) async-start(bf16[16,64,384]{2,1,0:T(8,128)(2,1)} %copy-done.5), calls=%async_computation.2 | async-start | bytes 1572864 | tf_op jit(solution)/shard_map/all_to_all | solution.py:472
  199.7 20.5 %collective-permute-start.7 = (bf16[1024,384]{1,0:T(8,128)(2,1)}, bf16[1024,384]{1,0:T(8,128)(2,1)S(1)}, u32[]{:S(2)}, u32[]{:S(2)}) collective-permute-start(bf16[1024,384]{1,0:T(8,128)(2,1)} %bitcast.14.refs_2_), channel_id=1, source_target_pairs={{0,1},{1,2},{2,3},{3,0},{4,5},{5,6},{6,7},{7,4},{8,9},{9,10},{10,1... | collective-permute-start | bytes 2359304 | tf_op jit(solution)/shard_map/ppermute | solution.py:23
  200.6 19.6 %collective-permute-start.8 = (bf16[1024,384]{1,0:T(8,128)(2,1)}, bf16[1024,384]{1,0:T(8,128)(2,1)S(1)}, u32[]{:S(2)}, u32[]{:S(2)}) collective-permute-start(bf16[1024,384]{1,0:T(8,128)(2,1)} %bitcast.14.refs_2_), channel_id=1, source_target_pairs={{0,3},{1,0},{2,1},{3,2},{4,7},{5,4},{6,5},{7,6},{8,11},{9,8},{10,9... | collective-permute-start | bytes 2359304 | tf_op jit(solution)/shard_map/ppermute | solution.py:27
  220.2 23.3 %collective-permute-start.9 = (bf16[1024,256]{1,0:T(8,128)(2,1)S(1)}, bf16[1024,256]{1,0:T(8,128)(2,1)S(1)}, u32[]{:S(2)}, u32[]{:S(2)}) collective-permute-start(bf16[1024,256]{1,0:T(8,128)(2,1)S(1)} %bitcast.33), channel_id=1, source_target_pairs={{0,1},{1,2},{2,3},{3,0},{4,5},{5,6},{6,7},{7,4},{8,9},{9,10},{10,1... | collective-permute-start | bytes 1572872 | tf_op jit(solution)/shard_map/ppermute | solution.py:23
  221.4 22.1 %collective-permute-start.10 = (bf16[1024,256]{1,0:T(8,128)(2,1)S(1)}, bf16[1024,256]{1,0:T(8,128)(2,1)S(1)}, u32[]{:S(2)}, u32[]{:S(2)}) collective-permute-start(bf16[1024,256]{1,0:T(8,128)(2,1)S(1)} %bitcast.34), channel_id=1, source_target_pairs={{0,3},{1,0},{2,1},{3,2},{4,7},{5,4},{6,5},{7,6},{8,11},{9,8},{10,9... | collective-permute-start | bytes 1572872 | tf_op jit(solution)/shard_map/ppermute | solution.py:27
  224.2 19.2 %collective-permute-start.11 = (bf16[512,384]{1,0:T(8,128)(2,1)}, bf16[512,384]{1,0:T(8,128)(2,1)S(1)}, u32[]{:S(2)}, u32[]{:S(2)}) collective-permute-start(bf16[512,384]{1,0:T(8,128)(2,1)} %slice.56), channel_id=1, source_target_pairs={{0,1},{1,2},{2,3},{3,0},{4,5},{5,6},{6,7},{7,4},{8,9},{9,10},{10,1... | collective-permute-start | bytes 1179656 | tf_op jit(solution)/shard_map/ppermute | solution.py:23
  225.0 18.4 %collective-permute-start.12 = (bf16[512,384]{1,0:T(8,128)(2,1)}, bf16[512,384]{1,0:T(8,128)(2,1)}, u32[]{:S(2)}, u32[]{:S(2)}) collective-permute-start(bf16[512,384]{1,0:T(8,128)(2,1)} %slice.57), channel_id=1, source_target_pairs={{0,3},{1,0},{2,1},{3,2},{4,7},{5,4},{6,5},{7,6},{8,11},{9,8},{10,9... | collective-permute-start | bytes 1179656 | tf_op jit(solution)/shard_map/ppermute | solution.py:27
  228.4 2.4 copy-start
  230.8 16.1 %copy-start.1 = (bf16[48,80,640]{2,1,0:T(8,128)(2,1)S(1)}, bf16[48,80,640]{2,1,0:T(8,128)(2,1)}, u32[]{:S(2)}) copy-start(bf16[48,80,640]{2,1,0:T(8,128)(2,1)} %all-gather.3.cloned.1.call-done) | copy-start | bytes 14745604
  230.8 16.1 %copy-start.3 = (bf16[1024,1280]{1,0:T(8,128)(2,1)S(1)}, bf16[1024,1280]{1,0:T(8,128)(2,1)}, u32[]{:S(2)}) copy-start(bf16[1024,1280]{1,0:T(8,128)(2,1)} %param.10) | copy-start | bytes 7864324
  241.1 2.4 copy-start.2
  243.5 12.3 %collective-permute-start.16 = (bf16[512,256]{1,0:T(8,128)(2,1)S(1)}, bf16[512,256]{1,0:T(8,128)(2,1)S(1)}, u32[]{:S(2)}, u32[]{:S(2)}) collective-permute-start(bf16[512,256]{1,0:T(8,128)(2,1)S(1)} %slice.58), channel_id=1, source_target_pairs={{0,1},{1,2},{2,3},{3,0},{4,5},{5,6},{6,7},{7,4},{8,9},{9,10},{10,1... | collective-permute-start | bytes 786440 | tf_op jit(solution)/shard_map/ppermute | solution.py:23
  243.7 12.1 %collective-permute-start.17 = (bf16[512,256]{1,0:T(8,128)(2,1)S(1)}, bf16[512,256]{1,0:T(8,128)(2,1)S(1)}, u32[]{:S(2)}, u32[]{:S(2)}) collective-permute-start(bf16[512,256]{1,0:T(8,128)(2,1)S(1)} %slice.59), channel_id=1, source_target_pairs={{0,3},{1,0},{2,1},{3,2},{4,7},{5,4},{6,5},{7,6},{8,11},{9,8},{10,9... | collective-permute-start | bytes 786440 | tf_op jit(solution)/shard_map/ppermute | solution.py:27
  (3 other events, 4.0 us)
Sparse Core Ops, SparseCore 0:
  48.5 55.9 all-gather.2

commit v2 on v1

--- a/solution.py
+++ b/solution.py
@@ -13,18 +13,18 @@
 EPSILON = 1e-06
 DP = ("z", "xh", "core")
 TENSOR = 4
-FACTS = 128
-DIGIT = 32
+RING = 4
+X = ("xh", "context")
 MIB = 1024 * 1024
 SMALL = pl.CostEstimate(flops=1024, bytes_accessed=1024, transcendentals=0)
 
 
-def to_right(block):
-    return lax.ppermute(block, "tensor", [(i, (i + 1) % TENSOR) for i in range(TENSOR)])
-
-
-def to_left(block):
-    return lax.ppermute(block, "tensor", [(i, (i - 1) % TENSOR) for i in range(TENSOR)])
+def to_right(block, axis="tensor"):
+    return lax.ppermute(block, axis, [(i, (i + 1) % RING) for i in range(RING)])
+
+
+def to_left(block, axis="tensor"):
+    return lax.ppermute(block, axis, [(i, (i - 1) % RING) for i in range(RING)])
 
 
 def ring_near(top, low):
@@ -87,10 +87,9 @@
     )(*pieces, *weights, gains)
 
 
-def project_far_kernel(blocks, page, top, low, weights, gain, bias, total, squares, queries, others):
+def project_far_kernel(blocks, group, top, low, weights, gain, bias, total, squares, *outs):
     step = pl.program_id(0)
-    pages, count, heads_wide = queries.shape
-    columns = weights.shape[1]
+    pages, count, _ = outs[0].shape
     features = TENSOR * top.shape[1]
 
     def finish(piece):
@@ -98,36 +97,30 @@
         scale = lax.rsqrt((squares[...] + square) * (1.0 / features) + EPSILON)
         result = ((total[...] + product) * scale + bias[...]).astype(jnp.bfloat16)
         for item in range(pages // blocks):
-            index = step * (pages // blocks) + item
-            target = page[index]
+            target = group[step * (pages // blocks) + item]
             rows = result[item * count : (item + 1) * count]
-            queries[target] = rows[:, :heads_wide]
-            others[target, :, : columns - heads_wide] = rows[:, heads_wide:]
-            lane = lax.broadcasted_iota(jnp.int32, (count, FACTS), 1)
-            fact = jnp.zeros_like(lane)
-            for place in range(3):
-                fact = jnp.where(lane == place, page[(place + 1) * pages + index], fact)
-            others[target, :, columns - heads_wide :] = fact.astype(jnp.float32).astype(jnp.bfloat16)
+            at = 0
+            for out in outs:
+                out[target] = rows[:, at : at + out.shape[2]]
+                at += out.shape[2]
 
     pl.when(step < blocks // 2)(lambda: finish(top))
     pl.when(step >= blocks // 2)(lambda: finish(low))
 
 
-def project_far(page, top, low, weights, gain, bias, carry, heads_wide):
+def project_far(group, top, low, weights, gain, bias, carry, split):
     blocks = 4
     half, width = carry[0].shape[0] // 2, top.shape[1]
     columns = weights.shape[1]
-    pages = page.shape[0] // 4
+    pages = group.shape[0]
     block = 2 * half // blocks
-    shapes = [
-        (pages, 2 * half // pages, wide) for wide in (heads_wide, columns - heads_wide + FACTS)
-    ]
+    shapes = [(pages, 2 * half // pages, wide) for wide in (split, columns - split)]
 
     def kernel(*refs):
         project_far_kernel(blocks, *refs)
 
     def whole(shape):
-        return pl.BlockSpec(shape, lambda r, page: (0,) * len(shape))
+        return pl.BlockSpec(shape, lambda r, group: (0,) * len(shape))
 
     return pl.pallas_call(
         kernel,
@@ -136,20 +129,20 @@
             num_scalar_prefetch=1,
             grid=(blocks,),
             in_specs=[
-                pl.BlockSpec((block, width), lambda r, page: (jnp.minimum(r, blocks // 2 - 1), 0)),
-                pl.BlockSpec((block, width), lambda r, page: (jnp.maximum(r - blocks // 2, 0), 0)),
+                pl.BlockSpec((block, width), lambda r, group: (jnp.minimum(r, blocks // 2 - 1), 0)),
+                pl.BlockSpec((block, width), lambda r, group: (jnp.maximum(r - blocks // 2, 0), 0)),
                 whole(weights.shape),
                 whole(gain.shape),
                 whole(bias.shape),
-                pl.BlockSpec((block, columns), lambda r, page: (r, 0)),
-                pl.BlockSpec((block, 1), lambda r, page: (r, 0)),
+                pl.BlockSpec((block, columns), lambda r, group: (r, 0)),
+                pl.BlockSpec((block, 1), lambda r, group: (r, 0)),
             ],
             out_specs=[whole(shape) for shape in shapes],
         ),
         compiler_params=pltpu.CompilerParams(vmem_limit_bytes=28 * MIB),
         cost_estimate=SMALL,
         name="project_far",
-    )(page, top, low, weights, gain, bias, *carry)
+    )(group, top, low, weights, gain, bias, *carry)
 
 
 def attend_kernel(heads, first, source, sequence, context, queries, own, other, out, *scratch):
@@ -178,7 +171,7 @@
         slot = index * per
         query = jnp.concatenate(
             [
-                queries[source[pages + slot + page], :, (first + head) * HEAD : (first + head + 1) * HEAD]
+                queries[source[pages + slot + page], :, first + head * HEAD : first + (head + 1) * HEAD]
                 for head in range(heads)
                 for page in range(per)
             ],
@@ -277,9 +270,9 @@
     )(source, sequence, context, queries, own, other)
 
 
-def rows_of(w_out, cut):
+def rows_of(w_out, place, cut):
     begin, end = cut
-    return w_out[:, 0, 0, begin:end, :].reshape(-1, w_out.shape[-1])
+    return w_out[:, 0, place, begin:end, :].reshape(-1, w_out.shape[-1])
 
 
 def mix_near_kernel(steps, counts, carried, paged, page_of, me, *refs):
@@ -289,52 +282,53 @@
     before = refs.pop(0) if carried else None
     hidden = refs.pop(0) if paged else None
     (total,) = refs
-    step = pl.program_id(1)
-
-    for index, (place, cut) in enumerate(steps):
-
-        @pl.when(step == index)
-        def _(index=index, place=place, cut=cut):
-            if place == 0:
-                band = w_own[8 * cut[0] : 8 * cut[1], :]
-            else:
-                band = rows_of(w_all, cut)
-            start = 0
-            for piece in pieces[index]:
-                count = piece.shape[0]
-                at = pl.ds(start, count)
-                product = jnp.dot(piece[...], band, preferred_element_type=jnp.float32)
-                if index > 0:
-                    product = total[at] + product
-                elif carried:
-                    product = before[at] + product
-                if index == len(steps) - 1 and paged:
-                    rows = [hidden[page_of[(start + k) // PAGE]] for k in range(0, count, PAGE)]
-                    product = product + jnp.concatenate(rows, axis=0).astype(jnp.float32)
-                total[at] = product
-                start += count
+    block = pl.program_id(1)
+    bands = [
+        w_own[8 * cut[0] : 8 * cut[1], :] if place == 0 else rows_of(w_all, place - 1, cut)
+        for place, cut in steps
+    ]
+    band = jnp.concatenate(bands, axis=0)
+
+    def finish(half):
+        rows = jnp.concatenate([piece[min(half, len(piece) - 1)][...] for piece in pieces], axis=1)
+        product = jnp.dot(rows, band, preferred_element_type=jnp.float32)
+        if carried:
+            product = before[...] + product
+        if paged:
+            count = rows.shape[0] // PAGE
+            added = [hidden[page_of[half * count + item]] for item in range(count)]
+            product = product + jnp.concatenate(added, axis=0).astype(jnp.float32)
+        total[...] = product
+
+    for half in range(2):
+        pl.when(block == half)(lambda half=half: finish(half))
 
 
 def mix_near(page_of, me, pieces, steps, w_out, w_all, before=None, hidden=None):
-    rows = sum(p.shape[0] for p in pieces[0])
-    outer, cuts, _, stored, columns = w_all.shape
-    counts = [len(group) for group in pieces]
+    outer, cuts, places, stored, columns = w_all.shape
+    counts = [len(piece) for piece in pieces]
+    half = sum(p.shape[0] for p in pieces[0]) // 2
 
     def kernel(*refs):
         mix_near_kernel(steps, counts, before is not None, hidden is not None, *refs)
 
-    def place_of(k):
-        return sum(jnp.where(k == i, max(place, 1) - 1, 0) for i, (place, _) in enumerate(steps))
-
-    flat = pl.BlockSpec((rows, columns), lambda n, k, page_of, me: (0, n))
-    operands = [p for group in pieces for p in group]
-    in_specs = [pl.BlockSpec(p.shape, lambda n, k, page_of, me: (0, 0)) for p in operands]
+    flat = pl.BlockSpec((half, columns), lambda n, r, page_of, me: (r, n))
+    operands, in_specs = [], []
+    for piece in pieces:
+        for array in piece:
+            operands.append(array)
+            whole = len(piece) > 1
+            in_specs.append(
+                pl.BlockSpec(
+                    (half, array.shape[1]),
+                    lambda n, r, page_of, me, whole=whole: (0 if whole else r, 0),
+                )
+            )
     operands += [w_out, w_all]
     in_specs += [
-        pl.BlockSpec((w_out.shape[0], columns), lambda n, k, page_of, me: (0, me[0] * cuts + n)),
+        pl.BlockSpec((w_out.shape[0], columns), lambda n, r, page_of, me: (0, me[0] * cuts + n)),
         pl.BlockSpec(
-            (outer, 1, 1, stored, columns),
-            lambda n, k, page_of, me: (0, n, place_of(k), 0, 0),
+            (outer, 1, places, stored, columns), lambda n, r, page_of, me: (0, n, 0, 0, 0)
         ),
     ]
     if before is not None:
@@ -343,14 +337,14 @@
     if hidden is not None:
         operands.append(hidden)
         in_specs.append(
-            pl.BlockSpec((rows // PAGE, PAGE, columns), lambda n, k, page_of, me: (0, 0, n))
+            pl.BlockSpec((2 * half // PAGE, PAGE, columns), lambda n, r, page_of, me: (0, 0, n))
         )
     return pl.pallas_call(
         kernel,
-        out_shape=jax.ShapeDtypeStruct((rows, cuts * columns), jnp.float32),
+        out_shape=jax.ShapeDtypeStruct((2 * half, cuts * columns), jnp.float32),
         grid_spec=pltpu.PrefetchScalarGridSpec(
             num_scalar_prefetch=2,
-            grid=(cuts, len(steps)),
+            grid=(cuts, 2),
             in_specs=in_specs,
             out_specs=flat,
         ),
@@ -362,7 +356,7 @@
 
 def mix_far_kernel(blocks, cut, page_of, top, low, w_all, before, out):
     step = pl.program_id(1)
-    band = rows_of(w_all, cut)
+    band = rows_of(w_all, 0, cut)
 
     def finish(piece):
         rows = before[...] + jnp.dot(piece[...], band, preferred_element_type=jnp.float32)
@@ -425,17 +419,36 @@
     return [to_right(right), to_left(left), far]
 
 
+def place_kernel(where, *refs):
+    sources, out = refs[:-1], refs[-1]
+    every = (0, 3, 1, 2)
+    for z_step, x_steps, source in zip((*every, 2), (every, every, every, every[:2], every[2:]), sources):
+        z = lax.rem(where[0] + z_step, RING)
+        for index, x_step in enumerate(x_steps):
+            x = lax.rem(where[1] + x_step, RING)
+            out[z * 2 + x // 2, lax.rem(x, 2)] = source[index]
+
+
+def place_shares(sources):
+    where = jnp.stack([lax.axis_index("z"), lax.axis_index(X)]).astype(jnp.int32)
+    vmem = pl.BlockSpec(memory_space=pltpu.VMEM)
+    return pl.pallas_call(
+        place_kernel,
+        out_shape=jax.ShapeDtypeStruct((8, 2) + sources[0].shape[1:], jnp.bfloat16),
+        in_specs=[pl.BlockSpec(memory_space=pltpu.SMEM)] + [vmem] * len(sources),
+        out_specs=vmem,
+        compiler_params=pltpu.CompilerParams(vmem_limit_bytes=24 * MIB),
+        cost_estimate=SMALL,
+        name="place_shares",
+    )(where, *sources)
+
+
 def places(local, sequence):
     pages = local.shape[0]
     ladder = jnp.arange(pages, dtype=jnp.int32)
     hit = local[None, :] == ladder[:, None]
     source = jnp.sum(jnp.where(hit, ladder[None, :], 0), axis=1)
     return jnp.stack([source, jnp.sum(jnp.where(hit, sequence[None, :], 0), axis=1)])
-
-
-def read_facts(facts):
-    facts = facts.astype(jnp.float32).astype(jnp.int32)
-    return places(facts[:, 0], facts[:, 1] * DIGIT + facts[:, 2])
 
 
 def body(hidden, seq_id, dest_page, norm_gain, w_query, q_bias, w_key, w_value, v_bias, w_out):
@@ -447,55 +460,74 @@
     order = jnp.stack([me, (me + 3) % TENSOR, (me + 1) % TENSOR, (me + 2) % TENSOR]).astype(jnp.int32)
     sequence = seq_id[::PAGE]
     group = dest_page // pages
-    page = jnp.concatenate([group, dest_page % pages, sequence // DIGIT, sequence % DIGIT])
     slots = jnp.arange(pages, dtype=jnp.int32)
     page_of = jnp.sum(jnp.where(group[None, :] == slots[:, None], slots[None, :], 0), axis=1)
 
     paged = hidden.reshape(pages, PAGE, hidden.shape[1])
     block = jnp.split(hidden, 2)
-    w_query, w_key, w_value, block = lax.optimization_barrier((w_query, w_key, w_value, block))
-    width, heads_wide = hidden.shape[1], w_query.shape[1]
+    width = hidden.shape[1]
 
     def band(array, index):
         return lax.dynamic_slice_in_dim(array, order[index] * width, width, 0)
 
+    hold = lax.optimization_barrier
+
+    def exchange(rows):
+        return lax.all_to_all(rows, DP, split_axis=0, concat_axis=0, tiled=True)
+
+    def beside(rows):
+        return lax.ppermute(rows, "context", [(0, 1)])
+
+    shares = w_out_shares(w_out, context, lax.axis_index(("z", "xh")), 8, cuts)
+    block, shares = hold((block, shares))
+    left, right = ring_near(*block)
+    shares = jnp.stack(shares)
+    x_left, x_right = to_right(shares, X), to_left(shares, X)
+    depth = (cuts[0][1] - cuts[0][0]) * HEAD // 8
+    x_top, x_low = to_right(x_left[:, :depth], X), to_left(x_right[:, depth:], X)
+    shares = jnp.stack([shares, x_left, x_right, jnp.concatenate([x_top, x_low], axis=1)])
+
+    w_query, w_key, w_value, block = hold((w_query, w_key, w_value, block))
     weights = [
-        jnp.concatenate([band(w, index) for w in (w_query, w_key, w_value)], axis=1)
+        jnp.concatenate([band(w, index) for w in (w_key, w_value, w_query)], axis=1)
         for index in range(TENSOR)
     ]
     gains = [band(norm_gain, index)[None, :] for index in range(TENSOR)]
     near_gains, far_gain = jnp.stack(gains[:3]), gains[3][None]
-    bias = jnp.concatenate([q_bias, jnp.zeros_like(v_bias), v_bias]).astype(jnp.float32)[None, :]
-    hold = lax.optimization_barrier
-
-    def exchange(rows):
-        return lax.all_to_all(rows, DP, split_axis=0, concat_axis=0, tiled=True)
-
-    left, right = ring_near(*block)
-    shares = w_out_shares(w_out, context, lax.axis_index(("z", "xh")), 8, cuts)
-    shares, _ = hold((shares, (left[0], right[1])))
-    w_all = lax.all_gather(jnp.stack(shares), ("z", "xh", "context"), axis=0, tiled=False)
-    w_all = w_all.reshape((8, 2) + w_all.shape[1:])
-    left, right, weights, near_gains = hold((left, right, weights, near_gains))
-    far = ring_far(left[0], right[1])
+    bias = jnp.concatenate([jnp.zeros_like(v_bias), v_bias, q_bias]).astype(jnp.float32)[None, :]
+
+    facts = jnp.stack([jnp.take(dest_page % pages, page_of), jnp.take(sequence, page_of)], axis=1)
+    facts, _ = hold((facts, block))
+    facts = exchange(facts)
+    facts = jnp.stack([facts, beside(facts)])
+    here = places(facts[0, :, 0], facts[0, :, 1])
+    there = jnp.where(context > 0, places(facts[1, :, 0], facts[1, :, 1]), here)
+    source = jnp.concatenate([there[0], here[0]])
+    sequence = jnp.concatenate([there[1], here[1]])
+
+    top, low, weights, near_gains, source, sequence, shares = hold(
+        (left[0], right[1], weights, near_gains, source, sequence, shares)
+    )
+    far = ring_far(top, low)
+    z_left, z_right = to_right(shares, "z"), to_left(shares, "z")
+    left, right, z_left, z_right = hold((left, right, z_left, z_right))
+    z_far = (to_right(z_left[:2], "z"), to_left(z_right[2:], "z"))
     carry = project_near((block, left, right), weights[:3], near_gains)
-    queries, own = project_far(page, *far, weights[3], far_gain, bias, carry, heads_wide)
+    (first, end), (start, stop) = cuts
+    split = (2 + end) * HEAD
+    far, z_far = hold((far, z_far))
+    w_all = place_shares([shares, z_left, z_right, *z_far])
+    own, queries = project_far(group, *far, weights[3], far_gain, bias, carry, split)
     own = exchange(own)
+    other = beside(own[:, :, : 2 * HEAD])
     queries, own = hold((queries, own))
     queries = exchange(queries)
-    other = lax.ppermute(own, "context", [(0, 1)])
-
-    here = read_facts(own[:, 0, 2 * HEAD : 2 * HEAD + 3])
-    there = read_facts(other[:, 0, 2 * HEAD : 2 * HEAD + 3])
-    there = jnp.where(context > 0, there, here)
-    source = jnp.concatenate([there[0], here[0]])
-    sequence = jnp.concatenate([there[1], here[1]])
 
     second = context.astype(jnp.int32).reshape(1)
-    (first, end), (start, stop) = cuts
-    part_a = attend(end - first, first, source, sequence, second, queries, own, other)
-    queries, part_a = hold((queries, part_a))
-    part_b = attend(stop - start, start, source, sequence, second, queries, own, other)
+    own, w_all = hold((own, w_all))
+    part_a = attend(end - first, 2 * HEAD, source, sequence, second, own, own, other)
+    own, part_a = hold((own, part_a))
+    part_b = attend(stop - start, 0, source, sequence, second, queries, own, other)
     part_a, part_b = hold((exchange(part_a), part_b))
     flat_a = part_a.reshape(pages * PAGE, -1)
     left, right = to_right(flat_a), to_left(flat_a)

time: 271 us -> 255 us (0.941)
  waiting for transfers between devices: 82.4 us -> 53.4 us
  starting transfers between devices: 36.4 us -> 55.6 us
  between operations: 13.7 us -> 0.57 us
  local copies, waits for them, and re-layouts: 20.7 us -> 30.1 us
  Pallas kernels: 70.8 us -> 61.7 us
  blocking collectives: 36.9 us -> 43.3 us
    ppermute x17 -> x26, waiting for transfers between devices: 73.1 us -> 47.5 us  [the longest x12 27.5 us: to_left(): return lax.ppermute(block, axis, [(i, (i - 1) % RING) for i in range(RING)])]
    all_to_all x2 -> x3, starting transfers between devices: 8.22 us -> 18.9 us  [exchange(): return lax.all_to_all(rows, DP, split_axis=0, concat_axis=0, tiled=True)]
    unnamed x28 -> x52, local copies, waits for them, and re-layouts: 8.78 us -> 16.4 us
    all_to_all x2, blocking collectives: 36.9 us -> 43.3 us  [exchange(): return lax.all_to_all(rows, DP, split_axis=0, concat_axis=0, tiled=True)]
    ppermute x17 -> x26, starting transfers between devices: 27.4 us -> 33.6 us  [the longest x12 20.6 us: to_left(): return lax.ppermute(block, axis, [(i, (i - 1) % RING) for i in range(RING)])]
    pallas_call x2, Pallas kernels: 24 us -> 18.6 us  [attend(): pl.pallas_call(kernel, out_shape=jax.ShapeDtypeStruct((pages, PAGE, heads...]
    pallas_call x2 -> x3, Pallas kernels: 19.1 us -> 16.9 us  [the longest x2 16 us: mix_near(): pl.pallas_call(kernel, out_shape=jax.ShapeDtypeStruct((2 * half, cuts * c...]
    all_to_all x2 -> x3, waiting for transfers between devices: 7.41 us -> 5.9 us  [exchange(): return lax.all_to_all(rows, DP, split_axis=0, concat_axis=0, tiled=True)]
  transfers between devices with their start and end apart: 21 -> 30, of which waited for: 9 -> 12; matrix products, arithmetic and copies ran while one was open for 5% -> 7% of each run, Pallas kernels for 24% -> 20%
where the time goes in v2:
time: 255 us; the launch traced here: 254 us
  Pallas kernels  61.7 us (24%)
  starting transfers between devices  55.6 us (22%)
  waiting for transfers between devices  53.4 us (21%)
  blocking collectives  43.3 us (17%)
  local copies, waits for them, and re-layouts  30.1 us (12%)
  other arithmetic  9.17 us (4%)
    all_to_all x2, blocking collectives, exchange(): return lax.all_to_all(rows, DP, split_axis=0, concat_axis=0, tiled=True)  43.3 us
    ppermute x12, waiting for transfers between devices, to_left(): return lax.ppermute(block, axis, [(i, (i - 1) % RING) for i in range(RING)])  27.5 us
    ppermute x12, starting transfers between devices, to_left(): return lax.ppermute(block, axis, [(i, (i - 1) % RING) for i in range(RING)])  20.6 us
    all_to_all x3, starting transfers between devices, exchange(): return lax.all_to_all(rows, DP, split_axis=0, concat_axis=0, tiled=True)  18.9 us
    pallas_call x2, Pallas kernels, attend(): pl.pallas_call(kernel, out_shape=jax.ShapeDtypeStruct((pages, PAGE, heads...  18.6 us
    unnamed x52, local copies, waits for them, and re-layouts  16.4 us
    pallas_call x1, Pallas kernels, project_near(): pl.pallas_call(kernel, out_shape=[jax.ShapeDtypeStruct(shape, jnp.float32...  16.4 us
    pallas_call x2, Pallas kernels, mix_near(): pl.pallas_call(kernel, out_shape=jax.ShapeDtypeStruct((2 * half, cuts * c...  16 us
  transfers between devices with their start and end apart: 30, of which 12 were waited for; matrix products, arithmetic and copies ran while one was open for 7% of the time, Pallas kernels for 20%

profile of v2, /device:TPU:2, one launch (start us, length us, event | category | flops | bytes accessed | tf_op | source)
XLA Modules:
  0.0 253.9 jit_solution(7438063082930555975)
XLA Ops:
  3.0 3.2 %collective-permute-start.2 = (bf16[80,640]{1,0:T(8,128)(2,1)}, bf16[80,640]{1,0:T(8,128)(2,1)S(1)}, u32[]{:S(2)}, u32[]{:S(2)}) collective-permute-start(bf16[80,640]{1,0:T(8,128)(2,1)} %get-tuple-element.126), channel_id=1, source_target_pairs={{0,2},{1,3},{2,0},{3,1},{4,6},{5,7},{6,4},{7,5},{8,10},{9,11},{10,... | collective-permute-start | bytes 307208 | tf_op jit(solution)/shard_map/ppermute | solution.py:418
  6.8 2.6 %collective-permute-start.1 = (bf16[80,640]{1,0:T(8,128)(2,1)S(1)}, bf16[80,640]{1,0:T(8,128)(2,1)S(1)}, u32[]{:S(2)}, u32[]{:S(2)}) collective-permute-start(bf16[80,640]{1,0:T(8,128)(2,1)S(1)} %get-tuple-element.128), channel_id=1, source_target_pairs={{0,3},{1,0},{2,1},{3,2},{4,7},{5,4},{6,5},{7,6},{8,11},{9,8},{10,9... | collective-permute-start | bytes 307208 | tf_op jit(solution)/shard_map/ppermute | solution.py:27
  17.9 3.2 %collective-permute-start.4 = (bf16[512,1280]{1,0:T(8,128)(2,1)}, bf16[512,1280]{1,0:T(8,128)(2,1)}, u32[]{:S(2)}, u32[]{:S(2)}) collective-permute-start(bf16[512,1280]{1,0:T(8,128)(2,1)} %get-tuple-element.63.refs_1_), channel_id=1, source_target_pairs={{0,3},{1,0},{2,1},{3,2},{4,7},{5,4},{6,5},{7,6},{8,11},{9,8},{10,9... | collective-permute-start | bytes 3932168 | tf_op jit(solution)/shard_map/ppermute | solution.py:27
  21.8 7.0 %all-to-all-start = ((s32[16,1,2]{2,1,0:T(1,128)}), s32[16,1,2]{2,1,0:T(1,128)S(1)}, u32[]{:S(2)}, u32[]{:S(2)}) async-start(s32[16,1,2]{2,1,0:T(1,128)} %copy.14), calls=%async_computation | async-start | bytes 16384 | tf_op jit(solution)/shard_map/all_to_all | solution.py:476
  28.8 3.6 %constant_dynamic-slice_fusion = (bf16[1280,640]{1,0:T(8,128)(2,1)S(1)}, bf16[1280,640]{1,0:T(8,128)(2,1)S(1)}, bf16[1280,640]{1,0:T(8,128)(2,1)S(1)}, bf16[1280,640]{1,0:T(8,128)(2,1)S(1)}) fusion(bf16[5120,640]{1,0:T(8,128)(2,1)} %param.16, s32[]{:T(128)S(6)} %select_n.114, s32[]{:T(128)S(6)} %select_n.113, s32[]{:T(128)S(6)} %select_n.112, s32[]{:T(128)S(6)} %select_n.111), kind=kLoop, calls=%fused_computation.27 | loop fusion | bytes 13107216 | tf_op jit(solution)/shard_map/dynamic_slice | solution.py:471
  39.2 4.2 %collective-permute-done.5 = s32[16,2]{0,1:T(2,128)S(1)} collective-permute-done((s32[16,2]{0,1:T(2,128)S(1)}, s32[16,2]{0,1:T(2,128)S(1)}, u32[]{:S(2)}, u32[]{:S(2)}) %collective-permute-start.5) | collective-permute-done | bytes 160 | tf_op jit(solution)/shard_map/ppermute | solution.py:479
  45.9 4.7 %collective-permute-done.9 = bf16[3,32,640]{2,1,0:T(8,128)(2,1)S(1)} collective-permute-done((bf16[3,32,640]{2,1,0:T(8,128)(2,1)S(1)}, bf16[3,32,640]{2,1,0:T(8,128)(2,1)S(1)}, u32[]{:S(2)}, u32[]{:S(2)}) %collective-permute-start.9) | collective-permute-done | bytes 122912 | tf_op jit(solution)/shard_map/ppermute | solution.py:27
  54.0 2.7 %collective-permute-start.15 = (bf16[4,3,80,640]{3,2,1,0:T(8,128)(2,1)S(1)}, bf16[4,3,80,640]{3,2,1,0:T(8,128)(2,1)S(1)}, u32[]{:S(2)}, u32[]{:S(2)}) collective-permute-start(bf16[4,3,80,640]{3,2,1,0:T(8,128)(2,1)S(1)} %pad_maximum_fusion.4.refs_0_), channel_id=1, source_target_pairs={{0,96},{32,0},{64,32},{96,64},{1,97},{33,1},{65,33},{97,65},{2,98}... | collective-permute-start | bytes 3686408 | tf_op jit(solution)/shard_map/ppermute | solution.py:27
  56.8 19.1 %collective-permute-done.13.refs_4_ = bf16[512,1280]{1,0:T(8,128)(2,1)} collective-permute-done((bf16[512,1280]{1,0:T(8,128)(2,1)}, bf16[512,1280]{1,0:T(8,128)(2,1)}, u32[]{:S(2)}, u32[]{:S(2)}) %collective-permute-start.13) | collective-permute-done | bytes 1310752 | tf_op jit(solution)/shard_map/ppermute | solution.py:27
  75.9 3.7 %collective-permute-start.11 = (bf16[512,1280]{1,0:T(8,128)(2,1)}, bf16[512,1280]{1,0:T(8,128)(2,1)S(1)}, u32[]{:S(2)}, u32[]{:S(2)}) collective-permute-start(bf16[512,1280]{1,0:T(8,128)(2,1)} %collective-permute-done.4.refs_5_), channel_id=1, source_target_pairs={{0,3},{1,0},{2,1},{3,2},{4,7},{5,4},{6,5},{7,6},{8,11},{9,8},{10,9... | collective-permute-start | bytes 3932168 | tf_op jit(solution)/shard_map/ppermute | solution.py:27
  79.6 4.1 %collective-permute-done.12.refs_3_ = bf16[512,1280]{1,0:T(8,128)(2,1)S(1)} collective-permute-done((bf16[512,1280]{1,0:T(8,128)(2,1)}, bf16[512,1280]{1,0:T(8,128)(2,1)S(1)}, u32[]{:S(2)}, u32[]{:S(2)}) %collective-permute-start.12) | collective-permute-done | bytes 1310752 | tf_op jit(solution)/shard_map/ppermute | solution.py:23
  86.0 2.4 collective-permute-start.17
  88.5 16.4 %project_near.1 = (f32[1024,896]{1,0:T(8,128)}, f32[1024,1]{1,0:T(8,128)}) custom-call(bf16[512,1280]{1,0:T(8,128)(2,1)} %get-tuple-element.62.refs_0_, bf16[512,1280]{1,0:T(8,128)(2,1)} %get-tuple-element.63.refs_1_, bf16[512,1280]{1,0:T(8,128)(2,1)} %collective-permute-done.3.refs_2_, bf16[512,1280]{1,0:T(8,128)(2,1)} %copy-done.20, ...), custom_call_target="tpu_custom_call" | custom-call | flops 1024 | bytes 1024 | tf_op jit(solution)/shard_map/project_near/pallas_call | solution.py:77
  104.9 4.5 %collective-permute-done.10.refs_1_ = bf16[512,1280]{1,0:T(8,128)(2,1)S(1)} collective-permute-done((bf16[512,1280]{1,0:T(8,128)(2,1)}, bf16[512,1280]{1,0:T(8,128)(2,1)S(1)}, u32[]{:S(2)}, u32[]{:S(2)}) %collective-permute-start.10) | collective-permute-done | bytes 1310752 | tf_op jit(solution)/shard_map/ppermute | solution.py:23
  109.5 2.5 copy-done.5
  113.0 4.5 %project_far.1 = (bf16[16,64,640]{2,1,0:T(8,128)(2,1)S(1)}, bf16[16,64,256]{2,1,0:T(8,128)(2,1)S(1)}) custom-call(s32[16]{0:T(128)S(1)} %get-tuple-element.144.refs_0_, bf16[512,1280]{1,0:T(8,128)(2,1)S(1)} %collective-permute-done.10.refs_1_, bf16[512,1280]{1,0:T(8,128)(2,1)S(1)} %collective-permute-done.11.refs_2_, ...), custom_call_target="tpu_custom_call" | custom-call | flops 1024 | bytes 1024 | tf_op jit(solution)/shard_map/project_far/pallas_call | solution.py:125
  117.5 26.8 %all_to_all.32.refs_3_.refs_4_ = bf16[16,64,640]{2,1,0:T(8,128)(2,1)S(1)} all-to-all(bf16[16,64,640]{2,1,0:T(8,128)(2,1)S(1)} %get-tuple-element.87), channel_id=1, replica_groups=mesh['z'=4,'xh'=2,'core'=2,'context'=2,'tensor'=4] {'z','xh','core'}, dimensions={0} | all-to-all | bytes 2621440 | tf_op jit(solution)/shard_map/all_to_all | solution.py:476
  146.5 4.3 %all-to-all-start.3 = ((bf16[16,64,256]{2,1,0:T(8,128)(2,1)}), bf16[16,64,256]{2,1,0:T(8,128)(2,1)}, u32[]{:S(2)}, u32[]{:S(2)}) async-start(bf16[16,64,256]{2,1,0:T(8,128)(2,1)} %copy-done.17), calls=%async_computation.3 | async-start | bytes 1048576 | tf_op jit(solution)/shard_map/all_to_all | solution.py:476
  156.5 2.2 copy-done
  158.7 3.4 %collective-permute-done.18.refs_5_ = bf16[16,64,256]{2,1,0:T(8,128)(2,1)S(1)} collective-permute-done((bf16[16,64,256]{2,1,0:T(8,128)(2,1)}, bf16[16,64,256]{2,1,0:T(8,128)(2,1)S(1)}, u32[]{:S(2)}, u32[]{:S(2)}) %collective-permute-start.18) | collective-permute-done | bytes 524320 | tf_op jit(solution)/shard_map/ppermute | solution.py:479
  162.1 10.3 %attend.2 = bf16[16,64,384]{2,1,0:T(8,128)(2,1)} custom-call(s32[32]{0:T(128)S(1)} %pad_add_fusion.1.refs_0_, s32[32]{0:T(128)S(1)} %pad_add_fusion.2.refs_1_, s32[1]{0:T(128)} %bitcast.26.refs_2_, bf16[16,64,640]{2,1,0:T(8,128)(2,1)S(1)} %all_to_all.32.refs_3_.refs_4_, bf16[16,64,640]{2,1,0:T(8,128)(2,1)S(1)} %all_to_all.32.refs_3_.refs_4_, ...), custom_call_target="tpu_custom_call" | custom-call | flops 1024 | bytes 1024 | tf_op jit(solution)/shard_map/attend/pallas_call | solution.py:254
  172.4 7.6 %all-to-all-start.2 = ((bf16[16,64,384]{2,1,0:T(8,128)(2,1)}), bf16[16,64,384]{2,1,0:T(8,128)(2,1)S(1)}, u32[]{:S(2)}, u32[]{:S(2)}) async-start(bf16[16,64,384]{2,1,0:T(8,128)(2,1)} %attend.2), calls=%async_computation.2 | async-start | bytes 1572864 | tf_op jit(solution)/shard_map/all_to_all | solution.py:476
  181.1 8.3 %attend.3 = bf16[16,64,256]{2,1,0:T(8,128)(2,1)S(1)} custom-call(s32[32]{0:T(128)S(1)} %pad_add_fusion.1.refs_0_, s32[32]{0:T(128)S(1)} %pad_add_fusion.2.refs_1_, s32[1]{0:T(128)} %bitcast.26.refs_2_, bf16[16,64,256]{2,1,0:T(8,128)(2,1)} %all-to-all-done.3.refs_3_, bf16[16,64,640]{2,1,0:T(8,128)(2,1)S(1)} %all_to_all.32.refs_3_.refs_4_, ...), custom_call_target="tpu_custom_call" | custom-call | flops 1024 | bytes 1024 | tf_op jit(solution)/shard_map/attend/pallas_call | solution.py:254
  189.4 5.9 %all-to-all-done.2 = bf16[16,64,384]{2,1,0:T(8,128)(2,1)S(1)} async-done(((bf16[16,64,384]{2,1,0:T(8,128)(2,1)}), bf16[16,64,384]{2,1,0:T(8,128)(2,1)S(1)}, u32[]{:S(2)}, u32[]{:S(2)}) %all-to-all-start.2) | async-done | bytes 786464 | tf_op jit(solution)/shard_map/all_to_all | solution.py:476
  197.3 16.4 %all_to_all.33 = bf16[16,64,256]{2,1,0:T(8,128)(2,1)S(1)} all-to-all(bf16[16,64,256]{2,1,0:T(8,128)(2,1)S(1)} %attend.3), channel_id=1, replica_groups=mesh['z'=4,'xh'=2,'core'=2,'context'=2,'tensor'=4] {'z','xh','core'}, dimensions={0} | all-to-all | bytes 1048576 | tf_op jit(solution)/shard_map/all_to_all | solution.py:476
  219.7 2.4 copy-done.1
  222.1 8.6 %mix_near.2.refs_8_ = f32[1024,1280]{1,0:T(8,128)S(1)} custom-call(s32[16]{0:T(128)S(1)} %select_reduce_fusion.4.refs_0_, s32[1]{0:T(128)} %bitcast.29.refs_1_, bf16[1024,384]{1,0:T(8,128)(2,1)S(1)} %bitcast.45, bf16[1024,384]{1,0:T(8,128)(2,1)S(1)} %collective-permute-done.19.refs_3_, bf16[1024,384]{1,0:T(8,128)(2,1)S(1)} %collective-permute-done.20.refs_4_, ...), custom_call_target="tpu_custom_call" | custom-call | flops 1024 | bytes 1024 | tf_op jit(solution)/shard_map/mix_near/pallas_call | solution.py:342
  230.7 2.3 copy-done.2
  233.1 3.2 %collective-permute-done.24.refs_3_ = bf16[512,384]{1,0:T(8,128)(2,1)S(1)} collective-permute-done((bf16[512,384]{1,0:T(8,128)(2,1)S(1)}, bf16[512,384]{1,0:T(8,128)(2,1)S(1)}, u32[]{:S(2)}, u32[]{:S(2)}) %collective-permute-start.24) | collective-permute-done | bytes 393248 | tf_op jit(solution)/shard_map/ppermute | solution.py:27
  238.1 3.0 %collective-permute-start.26 = (bf16[512,256]{1,0:T(8,128)(2,1)S(1)}, bf16[512,256]{1,0:T(8,128)(2,1)S(1)}, u32[]{:S(2)}, u32[]{:S(2)}) collective-permute-start(bf16[512,256]{1,0:T(8,128)(2,1)S(1)} %slice.63), channel_id=1, source_target_pairs={{0,3},{1,0},{2,1},{3,2},{4,7},{5,4},{6,5},{7,6},{8,11},{9,8},{10,9... | collective-permute-start | bytes 786440 | tf_op jit(solution)/shard_map/ppermute | solution.py:27
  241.1 7.4 %mix_near.3.refs_4_ = f32[1024,1280]{1,0:T(8,128)S(1)} custom-call(s32[16]{0:T(128)S(1)} %select_reduce_fusion.4.refs_0_, s32[1]{0:T(128)} %bitcast.29.refs_1_, bf16[512,384]{1,0:T(8,128)(2,1)S(1)} %collective-permute-done.23.refs_2_, bf16[512,384]{1,0:T(8,128)(2,1)S(1)} %collective-permute-done.24.refs_3_, ...), custom_call_target="tpu_custom_call" | custom-call | flops 1024 | bytes 1024 | tf_op jit(solution)/shard_map/mix_near/pallas_call | solution.py:342
  248.5 5.4 %mix_far.1 = bf16[16,64,1280]{2,1,0:T(8,128)(2,1)} custom-call(s32[16]{0:T(128)S(1)} %select_reduce_fusion.4.refs_0_, bf16[512,256]{1,0:T(8,128)(2,1)S(1)} %collective-permute-done.25.refs_1_, bf16[512,256]{1,0:T(8,128)(2,1)S(1)} %collective-permute-done.26.refs_2_, bf16[8,2,3,80,640]{4,3,2,1,0:T(8,128)(2,1)S(1)} %copy-done.1, f32[1024,1280]{1,0:T(8,128)S(1)} %mix_near.3.refs_4_), custom_call_target="tpu_custom_call" | custom-call | flops 1024 | bytes 1024 | tf_op jit(solution)/shard_map/mix_far/pallas_call | solution.py:382
  (141 shorter events, 47.5 us)
Async XLA Ops:
  3.0 12.1 %collective-permute-start.2 = (bf16[80,640]{1,0:T(8,128)(2,1)}, bf16[80,640]{1,0:T(8,128)(2,1)S(1)}, u32[]{:S(2)}, u32[]{:S(2)}) collective-permute-start(bf16[80,640]{1,0:T(8,128)(2,1)} %get-tuple-element.126), channel_id=1, source_target_pairs={{0,2},{1,3},{2,0},{3,1},{4,6},{5,7},{6,4},{7,5},{8,10},{9,11},{10,... | collective-permute-start | bytes 307208 | tf_op jit(solution)/shard_map/ppermute | solution.py:418
  6.2 8.9 %collective-permute-start = (bf16[80,640]{1,0:T(8,128)(2,1)}, bf16[80,640]{1,0:T(8,128)(2,1)S(1)}, u32[]{:S(2)}, u32[]{:S(2)}) collective-permute-start(bf16[80,640]{1,0:T(8,128)(2,1)} %get-tuple-element.127), channel_id=1, source_target_pairs={{0,1},{1,2},{2,3},{3,0},{4,5},{5,6},{6,7},{7,4},{8,9},{9,10},{10,1... | collective-permute-start | bytes 307208 | tf_op jit(solution)/shard_map/ppermute | solution.py:23
  6.8 8.2 %collective-permute-start.1 = (bf16[80,640]{1,0:T(8,128)(2,1)S(1)}, bf16[80,640]{1,0:T(8,128)(2,1)S(1)}, u32[]{:S(2)}, u32[]{:S(2)}) collective-permute-start(bf16[80,640]{1,0:T(8,128)(2,1)S(1)} %get-tuple-element.128), channel_id=1, source_target_pairs={{0,3},{1,0},{2,1},{3,2},{4,7},{5,4},{6,5},{7,6},{8,11},{9,8},{10,9... | collective-permute-start | bytes 307208 | tf_op jit(solution)/shard_map/ppermute | solution.py:27
  15.8 27.7 %collective-permute-start.6 = (bf16[3,80,640]{2,1,0:T(8,128)(2,1)S(1)}, bf16[3,80,640]{2,1,0:T(8,128)(2,1)S(1)}, u32[]{:S(2)}, u32[]{:S(2)}) collective-permute-start(bf16[3,80,640]{2,1,0:T(8,128)(2,1)S(1)} %get-tuple-element.130), channel_id=1, source_target_pairs={{0,4},{4,16},{16,20},{20,0},{1,5},{5,17},{17,21},{21,1},{2,6},{6,1... | collective-permute-start | bytes 921608 | tf_op jit(solution)/shard_map/ppermute | solution.py:23
  17.3 28.0 %collective-permute-start.7 = (bf16[3,80,640]{2,1,0:T(8,128)(2,1)S(1)}, bf16[3,80,640]{2,1,0:T(8,128)(2,1)S(1)}, u32[]{:S(2)}, u32[]{:S(2)}) collective-permute-start(bf16[3,80,640]{2,1,0:T(8,128)(2,1)S(1)} %get-tuple-element.130), channel_id=1, source_target_pairs={{0,20},{4,0},{16,4},{20,16},{1,21},{5,1},{17,5},{21,17},{2,22},{6,... | collective-permute-start | bytes 921608 | tf_op jit(solution)/shard_map/ppermute | solution.py:27
  17.9 36.1 %collective-permute-start.3 = (bf16[512,1280]{1,0:T(8,128)(2,1)}, bf16[512,1280]{1,0:T(8,128)(2,1)}, u32[]{:S(2)}, u32[]{:S(2)}) collective-permute-start(bf16[512,1280]{1,0:T(8,128)(2,1)} %get-tuple-element.62.refs_0_), channel_id=1, source_target_pairs={{0,1},{1,2},{2,3},{3,0},{4,5},{5,6},{6,7},{7,4},{8,9},{9,10},{10,1... | collective-permute-start | bytes 3932168 | tf_op jit(solution)/shard_map/ppermute | solution.py:23
  17.9 36.2 %collective-permute-start.4 = (bf16[512,1280]{1,0:T(8,128)(2,1)}, bf16[512,1280]{1,0:T(8,128)(2,1)}, u32[]{:S(2)}, u32[]{:S(2)}) collective-permute-start(bf16[512,1280]{1,0:T(8,128)(2,1)} %get-tuple-element.63.refs_1_), channel_id=1, source_target_pairs={{0,3},{1,0},{2,1},{3,2},{4,7},{5,4},{6,5},{7,6},{8,11},{9,8},{10,9... | collective-permute-start | bytes 3932168 | tf_op jit(solution)/shard_map/ppermute | solution.py:27
  21.8 16.0 %all-to-all-start = ((s32[16,1,2]{2,1,0:T(1,128)}), s32[16,1,2]{2,1,0:T(1,128)S(1)}, u32[]{:S(2)}, u32[]{:S(2)}) async-start(s32[16,1,2]{2,1,0:T(1,128)} %copy.14), calls=%async_computation | async-start | bytes 16384 | tf_op jit(solution)/shard_map/all_to_all | solution.py:476
  37.9 5.5 %collective-permute-start.5 = (s32[16,2]{0,1:T(2,128)S(1)}, s32[16,2]{0,1:T(2,128)S(1)}, u32[]{:S(2)}, u32[]{:S(2)}) collective-permute-start(s32[16,2]{0,1:T(2,128)S(1)} %bitcast.55), channel_id=1, source_target_pairs={{0,4},{1,5},{2,6},{3,7},{8,12},{9,13},{10,14},{11,15},{16,20},{17,... | collective-permute-start | bytes 392 | tf_op jit(solution)/shard_map/ppermute | solution.py:479
  43.3 32.5 %collective-permute-start.13 = (bf16[512,1280]{1,0:T(8,128)(2,1)}, bf16[512,1280]{1,0:T(8,128)(2,1)}, u32[]{:S(2)}, u32[]{:S(2)}) collective-permute-start(bf16[512,1280]{1,0:T(8,128)(2,1)} %get-tuple-element.62.refs_0_), channel_id=1, source_target_pairs={{0,3},{1,0},{2,1},{3,2},{4,7},{5,4},{6,5},{7,6},{8,11},{9,8},{10,9... | collective-permute-start | bytes 3932168 | tf_op jit(solution)/shard_map/ppermute | solution.py:27
  43.6 9.0 %collective-permute-start.8 = (bf16[3,48,640]{2,1,0:T(8,128)(2,1)S(1)}, bf16[3,48,640]{2,1,0:T(8,128)(2,1)S(1)}, u32[]{:S(2)}, u32[]{:S(2)}) collective-permute-start(bf16[3,48,640]{2,1,0:T(8,128)(2,1)S(1)} %slice.68), channel_id=1, source_target_pairs={{0,4},{4,16},{16,20},{20,0},{1,5},{5,17},{17,21},{21,1},{2,6},{6,1... | collective-permute-start | bytes 552968 | tf_op jit(solution)/shard_map/ppermute | solution.py:23
  45.4 5.2 %collective-permute-start.9 = (bf16[3,32,640]{2,1,0:T(8,128)(2,1)S(1)}, bf16[3,32,640]{2,1,0:T(8,128)(2,1)S(1)}, u32[]{:S(2)}, u32[]{:S(2)}) collective-permute-start(bf16[3,32,640]{2,1,0:T(8,128)(2,1)S(1)} %slice.69), channel_id=1, source_target_pairs={{0,20},{4,0},{16,4},{20,16},{1,21},{5,1},{17,5},{21,17},{2,22},{6,... | collective-permute-start | bytes 368648 | tf_op jit(solution)/shard_map/ppermute | solution.py:27
  50.6 33.1 %collective-permute-start.12 = (bf16[512,1280]{1,0:T(8,128)(2,1)}, bf16[512,1280]{1,0:T(8,128)(2,1)S(1)}, u32[]{:S(2)}, u32[]{:S(2)}) collective-permute-start(bf16[512,1280]{1,0:T(8,128)(2,1)} %get-tuple-element.63.refs_1_), channel_id=1, source_target_pairs={{0,1},{1,2},{2,3},{3,0},{4,5},{5,6},{6,7},{7,4},{8,9},{9,10},{10,1... | collective-permute-start | bytes 3932168 | tf_op jit(solution)/shard_map/ppermute | solution.py:23
  52.6 35.8 %copy-start.23 = (bf16[640]{0:T(1024)(128)(2,1)S(1)}, bf16[640]{0:T(1024)(128)(2,1)}, u32[]{:S(2)}) copy-start(bf16[640]{0:T(1024)(128)(2,1)} %param.17) | copy-start | bytes 3844
  52.7 35.8 %copy-start.24 = (bf16[128]{0:T(256)(128)(2,1)S(1)}, bf16[128]{0:T(256)(128)(2,1)}, u32[]{:S(2)}) copy-start(bf16[128]{0:T(256)(128)(2,1)} %param.20) | copy-start | bytes 772
  54.0 29.7 %collective-permute-start.15 = (bf16[4,3,80,640]{3,2,1,0:T(8,128)(2,1)S(1)}, bf16[4,3,80,640]{3,2,1,0:T(8,128)(2,1)S(1)}, u32[]{:S(2)}, u32[]{:S(2)}) collective-permute-start(bf16[4,3,80,640]{3,2,1,0:T(8,128)(2,1)S(1)} %pad_maximum_fusion.4.refs_0_), channel_id=1, source_target_pairs={{0,96},{32,0},{64,32},{96,64},{1,97},{33,1},{65,33},{97,65},{2,98}... | collective-permute-start | bytes 3686408 | tf_op jit(solution)/shard_map/ppermute | solution.py:27
  56.8 27.9 %collective-permute-start.14 = (bf16[4,3,80,640]{3,2,1,0:T(8,128)(2,1)S(1)}, bf16[4,3,80,640]{3,2,1,0:T(8,128)(2,1)S(1)}, u32[]{:S(2)}, u32[]{:S(2)}) collective-permute-start(bf16[4,3,80,640]{3,2,1,0:T(8,128)(2,1)S(1)} %pad_maximum_fusion.4.refs_0_), channel_id=1, source_target_pairs={{0,32},{32,64},{64,96},{96,0},{1,33},{33,65},{65,97},{97,1},{2,34}... | collective-permute-start | bytes 3686408 | tf_op jit(solution)/shard_map/ppermute | solution.py:23
  56.8 52.6 %collective-permute-start.10 = (bf16[512,1280]{1,0:T(8,128)(2,1)}, bf16[512,1280]{1,0:T(8,128)(2,1)S(1)}, u32[]{:S(2)}, u32[]{:S(2)}) collective-permute-start(bf16[512,1280]{1,0:T(8,128)(2,1)} %collective-permute-done.3.refs_2_), channel_id=1, source_target_pairs={{0,1},{1,2},{2,3},{3,0},{4,5},{5,6},{6,7},{7,4},{8,9},{9,10},{10,1... | collective-permute-start | bytes 3932168 | tf_op jit(solution)/shard_map/ppermute | solution.py:23
  75.9 33.5 %collective-permute-start.11 = (bf16[512,1280]{1,0:T(8,128)(2,1)}, bf16[512,1280]{1,0:T(8,128)(2,1)S(1)}, u32[]{:S(2)}, u32[]{:S(2)}) collective-permute-start(bf16[512,1280]{1,0:T(8,128)(2,1)} %collective-permute-done.4.refs_5_), channel_id=1, source_target_pairs={{0,3},{1,0},{2,1},{3,2},{4,7},{5,4},{6,5},{7,6},{8,11},{9,8},{10,9... | collective-permute-start | bytes 3932168 | tf_op jit(solution)/shard_map/ppermute | solution.py:27
  86.0 23.5 %collective-permute-start.17 = (bf16[2,3,80,640]{3,2,1,0:T(8,128)(2,1)}, bf16[2,3,80,640]{3,2,1,0:T(8,128)(2,1)S(1)}, u32[]{:S(2)}, u32[]{:S(2)}) collective-permute-start(bf16[2,3,80,640]{3,2,1,0:T(8,128)(2,1)} %slice.58), channel_id=1, source_target_pairs={{0,96},{32,0},{64,32},{96,64},{1,97},{33,1},{65,33},{97,65},{2,98}... | collective-permute-start | bytes 1843208 | tf_op jit(solution)/shard_map/ppermute | solution.py:27
  88.4 21.0 %collective-permute-start.16 = (bf16[2,3,80,640]{3,2,1,0:T(8,128)(2,1)S(1)}, bf16[2,3,80,640]{3,2,1,0:T(8,128)(2,1)S(1)}, u32[]{:S(2)}, u32[]{:S(2)}) collective-permute-start(bf16[2,3,80,640]{3,2,1,0:T(8,128)(2,1)S(1)} %slice.57), channel_id=1, source_target_pairs={{0,32},{32,64},{64,96},{96,0},{1,33},{33,65},{65,97},{97,1},{2,34}... | collective-permute-start | bytes 1843208 | tf_op jit(solution)/shard_map/ppermute | solution.py:23
  145.2 17.0 %collective-permute-start.18 = (bf16[16,64,256]{2,1,0:T(8,128)(2,1)}, bf16[16,64,256]{2,1,0:T(8,128)(2,1)S(1)}, u32[]{:S(2)}, u32[]{:S(2)}) collective-permute-start(bf16[16,64,256]{2,1,0:T(8,128)(2,1)} %slice.70), channel_id=1, source_target_pairs={{0,4},{1,5},{2,6},{3,7},{8,12},{9,13},{10,14},{11,15},{16,20},{17,... | collective-permute-start | bytes 1572872 | tf_op jit(solution)/shard_map/ppermute | solution.py:479
  146.5 26.0 %all-to-all-start.3 = ((bf16[16,64,256]{2,1,0:T(8,128)(2,1)}), bf16[16,64,256]{2,1,0:T(8,128)(2,1)}, u32[]{:S(2)}, u32[]{:S(2)}) async-start(bf16[16,64,256]{2,1,0:T(8,128)(2,1)} %copy-done.17), calls=%async_computation.3 | async-start | bytes 1048576 | tf_op jit(solution)/shard_map/all_to_all | solution.py:476
  172.4 22.8 %all-to-all-start.2 = ((bf16[16,64,384]{2,1,0:T(8,128)(2,1)}), bf16[16,64,384]{2,1,0:T(8,128)(2,1)S(1)}, u32[]{:S(2)}, u32[]{:S(2)}) async-start(bf16[16,64,384]{2,1,0:T(8,128)(2,1)} %attend.2), calls=%async_computation.2 | async-start | bytes 1572864 | tf_op jit(solution)/shard_map/all_to_all | solution.py:476
  195.3 19.0 %collective-permute-start.20 = (bf16[1024,384]{1,0:T(8,128)(2,1)S(1)}, bf16[1024,384]{1,0:T(8,128)(2,1)S(1)}, u32[]{:S(2)}, u32[]{:S(2)}) collective-permute-start(bf16[1024,384]{1,0:T(8,128)(2,1)S(1)} %bitcast.43), channel_id=1, source_target_pairs={{0,3},{1,0},{2,1},{3,2},{4,7},{5,4},{6,5},{7,6},{8,11},{9,8},{10,9... | collective-permute-start | bytes 2359304 | tf_op jit(solution)/shard_map/ppermute | solution.py:27
  195.5 20.0 %collective-permute-start.19 = (bf16[1024,384]{1,0:T(8,128)(2,1)S(1)}, bf16[1024,384]{1,0:T(8,128)(2,1)S(1)}, u32[]{:S(2)}, u32[]{:S(2)}) collective-permute-start(bf16[1024,384]{1,0:T(8,128)(2,1)S(1)} %bitcast.44), channel_id=1, source_target_pairs={{0,1},{1,2},{2,3},{3,0},{4,5},{5,6},{6,7},{7,4},{8,9},{9,10},{10,1... | collective-permute-start | bytes 2359304 | tf_op jit(solution)/shard_map/ppermute | solution.py:23
  215.5 22.2 %collective-permute-start.22 = (bf16[1024,256]{1,0:T(8,128)(2,1)S(1)}, bf16[1024,256]{1,0:T(8,128)(2,1)S(1)}, u32[]{:S(2)}, u32[]{:S(2)}) collective-permute-start(bf16[1024,256]{1,0:T(8,128)(2,1)S(1)} %bitcast.46), channel_id=1, source_target_pairs={{0,3},{1,0},{2,1},{3,2},{4,7},{5,4},{6,5},{7,6},{8,11},{9,8},{10,9... | collective-permute-start | bytes 1572872 | tf_op jit(solution)/shard_map/ppermute | solution.py:27
  215.8 22.0 %collective-permute-start.21 = (bf16[1024,256]{1,0:T(8,128)(2,1)S(1)}, bf16[1024,256]{1,0:T(8,128)(2,1)S(1)}, u32[]{:S(2)}, u32[]{:S(2)}) collective-permute-start(bf16[1024,256]{1,0:T(8,128)(2,1)S(1)} %bitcast.47), channel_id=1, source_target_pairs={{0,1},{1,2},{2,3},{3,0},{4,5},{5,6},{6,7},{7,4},{8,9},{9,10},{10,1... | collective-permute-start | bytes 1572872 | tf_op jit(solution)/shard_map/ppermute | solution.py:23
  217.6 18.6 %collective-permute-start.24 = (bf16[512,384]{1,0:T(8,128)(2,1)S(1)}, bf16[512,384]{1,0:T(8,128)(2,1)S(1)}, u32[]{:S(2)}, u32[]{:S(2)}) collective-permute-start(bf16[512,384]{1,0:T(8,128)(2,1)S(1)} %slice.61), channel_id=1, source_target_pairs={{0,3},{1,0},{2,1},{3,2},{4,7},{5,4},{6,5},{7,6},{8,11},{9,8},{10,9... | collective-permute-start | bytes 1179656 | tf_op jit(solution)/shard_map/ppermute | solution.py:27
  219.2 18.6 %collective-permute-start.23 = (bf16[512,384]{1,0:T(8,128)(2,1)S(1)}, bf16[512,384]{1,0:T(8,128)(2,1)S(1)}, u32[]{:S(2)}, u32[]{:S(2)}) collective-permute-start(bf16[512,384]{1,0:T(8,128)(2,1)S(1)} %slice.60), channel_id=1, source_target_pairs={{0,1},{1,2},{2,3},{3,0},{4,5},{5,6},{6,7},{7,4},{8,9},{9,10},{10,1... | collective-permute-start | bytes 1179656 | tf_op jit(solution)/shard_map/ppermute | solution.py:23
  237.8 10.7 %collective-permute-start.25 = (bf16[512,256]{1,0:T(8,128)(2,1)S(1)}, bf16[512,256]{1,0:T(8,128)(2,1)S(1)}, u32[]{:S(2)}, u32[]{:S(2)}) collective-permute-start(bf16[512,256]{1,0:T(8,128)(2,1)S(1)} %slice.62), channel_id=1, source_target_pairs={{0,1},{1,2},{2,3},{3,0},{4,5},{5,6},{6,7},{7,4},{8,9},{9,10},{10,1... | collective-permute-start | bytes 786440 | tf_op jit(solution)/shard_map/ppermute | solution.py:23
  238.1 10.4 %collective-permute-start.26 = (bf16[512,256]{1,0:T(8,128)(2,1)S(1)}, bf16[512,256]{1,0:T(8,128)(2,1)S(1)}, u32[]{:S(2)}, u32[]{:S(2)}) collective-permute-start(bf16[512,256]{1,0:T(8,128)(2,1)S(1)} %slice.63), channel_id=1, source_target_pairs={{0,3},{1,0},{2,1},{3,2},{4,7},{5,4},{6,5},{7,6},{8,11},{9,8},{10,9... | collective-permute-start | bytes 786440 | tf_op jit(solution)/shard_map/ppermute | solution.py:27
  (24 other events, 144.2 us)

commit v3 on v2

--- a/solution.py
+++ b/solution.py
@@ -145,8 +145,12 @@
     )(group, top, low, weights, gain, bias, *carry)
 
 
-def attend_kernel(heads, first, source, sequence, context, queries, own, other, out, *scratch):
-    keys, values, turned, best, total, summed = scratch
+def attend_kernel(heads, first, begins, ends, source, sequence, context, queries, own, *refs):
+    refs = list(refs)
+    other = refs.pop(0) if ends else None
+    state_in = [] if begins else [refs.pop(0) for _ in range(3)]
+    outs = [refs.pop(0) for _ in range(1 if ends else 3)]
+    keys, values, turned, best, total, summed = refs
     pages = own.shape[0]
     half = pages * PAGE
     per = 4
@@ -156,7 +160,7 @@
     factor = math.log2(math.e) / math.sqrt(HEAD)
 
     def place_page(slot, carry):
-        for base, lookup, array in ((0, 0, other), (half, pages, own)):
+        for base, lookup, array in [(0, 0, other)] * ends + [(half, pages, own)] * begins:
             page = source[lookup + slot]
             at = pl.ds(pl.multiple_of(base + slot * PAGE, PAGE), PAGE)
             keys[at, :] = array[page, :, :HEAD]
@@ -164,7 +168,7 @@
         return carry
 
     lax.fori_loop(0, pages, place_page, 0)
-    for block in range(2 * blocks):
+    for block in range(0 if ends else blocks, 2 * blocks if begins else blocks):
         turned[block] = values[pl.ds(block * rows, rows), :].astype(jnp.float32).T.astype(jnp.bfloat16)
 
     def query_block(index, carry):
@@ -203,12 +207,16 @@
             )
 
         last = blocks + index
-        scores = scores_of(last, True)
-        top = jnp.max(scores, axis=0, keepdims=True)
-        weight = jnp.exp2((scores - top) * factor)
-        best[...] = top
-        total[...] = jnp.sum(weight, axis=0, keepdims=True)
-        summed[...] = apply(last, weight)
+        if begins:
+            scores = scores_of(last, True)
+            top = jnp.max(scores, axis=0, keepdims=True)
+            weight = jnp.exp2((scores - top) * factor)
+            best[...] = top
+            total[...] = jnp.sum(weight, axis=0, keepdims=True)
+            summed[...] = apply(last, weight)
+        else:
+            for held, array in zip((best, total, summed), state_in):
+                held[...] = array[index]
 
         def key_block(block, carry):
             seen = False
@@ -228,12 +236,17 @@
 
             return carry
 
-        lax.fori_loop(jnp.where(context[0] > 0, 0, blocks), last, key_block, 0)
+        begin = jnp.where(context[0] > 0, 0, blocks) if ends else blocks
+        lax.fori_loop(begin, last if begins else blocks, key_block, 0)
+        if not ends:
+            for held, array in zip((best, total, summed), outs):
+                array[index] = held[...]
+            return carry
         result = (summed[...] / total[...]).T.astype(jnp.bfloat16)
         for head in range(heads):
             for page in range(per):
                 start = head * rows + page * PAGE
-                out[source[pages + slot + page], :, head * HEAD : (head + 1) * HEAD] = result[
+                outs[0][source[pages + slot + page], :, head * HEAD : (head + 1) * HEAD] = result[
                     start : start + PAGE
                 ]
         return carry
@@ -241,21 +254,29 @@
     lax.fori_loop(0, blocks, query_block, 0)
 
 
-def attend(heads, first, source, sequence, context, queries, own, other):
+def attend(heads, first, source, sequence, context, queries, own, other=None, state=None):
     pages = own.shape[0]
+    begins, ends = state is None, other is not None
 
     def kernel(*refs):
-        attend_kernel(heads, first, *refs)
+        attend_kernel(heads, first, begins, ends, *refs)
 
     half = pages * PAGE
     lanes = heads * 4 * PAGE
     vmem = pl.BlockSpec(memory_space=pltpu.VMEM)
     smem = pl.BlockSpec(memory_space=pltpu.SMEM)
-    return pl.pallas_call(
+    operands = [queries, own] + ([other] if ends else []) + list(state or [])
+    if ends:
+        out_shape = [jax.ShapeDtypeStruct((pages, PAGE, heads * HEAD), jnp.bfloat16)]
+    else:
+        out_shape = [
+            jax.ShapeDtypeStruct((pages // 4, rows, lanes), jnp.float32) for rows in (1, 1, HEAD)
+        ]
+    outs = pl.pallas_call(
         kernel,
-        out_shape=jax.ShapeDtypeStruct((pages, PAGE, heads * HEAD), jnp.bfloat16),
-        in_specs=[smem] * 3 + [vmem] * 3,
-        out_specs=vmem,
+        out_shape=out_shape,
+        in_specs=[smem] * 3 + [vmem] * len(operands),
+        out_specs=[vmem] * len(out_shape),
         scratch_shapes=[
             pltpu.VMEM((2 * half, HEAD), jnp.bfloat16),
             pltpu.VMEM((2 * half, HEAD), jnp.bfloat16),
@@ -267,7 +288,8 @@
         compiler_params=pltpu.CompilerParams(vmem_limit_bytes=20 * MIB),
         cost_estimate=SMALL,
         name="attend",
-    )(source, sequence, context, queries, own, other)
+    )(source, sequence, context, *operands)
+    return outs[0] if ends else outs
 
 
 def rows_of(w_out, place, cut):
@@ -524,15 +546,15 @@
     queries = exchange(queries)
 
     second = context.astype(jnp.int32).reshape(1)
-    own, w_all = hold((own, w_all))
-    part_a = attend(end - first, 2 * HEAD, source, sequence, second, own, own, other)
+    state = attend(end - first, 2 * HEAD, source, sequence, second, own, own)
+    part_a = attend(end - first, 2 * HEAD, source, sequence, second, own, own, other, state)
     own, part_a = hold((own, part_a))
     part_b = attend(stop - start, 0, source, sequence, second, queries, own, other)
     part_a, part_b = hold((exchange(part_a), part_b))
     flat_a = part_a.reshape(pages * PAGE, -1)
     left, right = to_right(flat_a), to_left(flat_a)
     flat_b = exchange(part_b).reshape(pages * PAGE, -1)
-    left, right, flat_b = hold((left, right, flat_b))
+    left, right, flat_b, w_all = hold((left, right, flat_b, w_all))
     bands = [(first * HEAD // 8, end * HEAD // 8) for first, end in cuts]
     here = me.astype(jnp.int32).reshape(1)
     half = pages * PAGE // 2

time: 255 us -> 249 us (0.976)
  blocking collectives: 43.3 us -> 26.8 us
  waiting for transfers between devices: 53.4 us -> 60.7 us
  Pallas kernels: 61.7 us -> 56.5 us
  local copies, waits for them, and re-layouts: 30.1 us -> 33.8 us
  starting transfers between devices: 55.6 us -> 58.9 us
    all_to_all x2 -> x1, blocking collectives: 43.3 us -> 26.8 us  [exchange(): return lax.all_to_all(rows, DP, split_axis=0, concat_axis=0, tiled=True)]
    all_to_all x3 -> x4, waiting for transfers between devices: 5.9 us -> 11.9 us  [exchange(): return lax.all_to_all(rows, DP, split_axis=0, concat_axis=0, tiled=True)]
    pallas_call x2 -> x3, Pallas kernels: 18.6 us -> 13 us  [attend(): pl.pallas_call(kernel, out_shape=out_shape, in_specs=[smem] * 3 + [vmem]...]
    ppermute x2, waiting for transfers between devices: 7.55 us -> 11 us  [beside(): return lax.ppermute(rows, 'context', [(0, 1)])]
    all_to_all x3 -> x4, starting transfers between devices: 18.9 us -> 22.2 us  [exchange(): return lax.all_to_all(rows, DP, split_axis=0, concat_axis=0, tiled=True)]
    unnamed x52 -> x56, local copies, waits for them, and re-layouts: 16.4 us -> 18.2 us
  transfers between devices with their start and end apart: 30 -> 31, of which waited for: 12 -> 13; matrix products, arithmetic and copies ran while one was open for 7% -> 8% of each run, Pallas kernels for 20% -> 19%
where the time goes in v3:
time: 249 us; the launch traced here: 246 us
  waiting for transfers between devices  60.7 us (24%)
  starting transfers between devices  58.9 us (24%)
  Pallas kernels  56.5 us (23%)
  local copies, waits for them, and re-layouts  33.8 us (14%)
  blocking collectives  26.8 us (11%)
  other arithmetic  9.18 us (4%)
    all_to_all x1, blocking collectives, exchange(): return lax.all_to_all(rows, DP, split_axis=0, concat_axis=0, tiled=True)  26.8 us
    ppermute x12, waiting for transfers between devices, to_left(): return lax.ppermute(block, axis, [(i, (i - 1) % RING) for i in range(RING)])  25.2 us
    all_to_all x4, starting transfers between devices, exchange(): return lax.all_to_all(rows, DP, split_axis=0, concat_axis=0, tiled=True)  22.2 us
    ppermute x12, starting transfers between devices, to_left(): return lax.ppermute(block, axis, [(i, (i - 1) % RING) for i in range(RING)])  20.7 us
    unnamed x56, local copies, waits for them, and re-layouts  18.2 us
    pallas_call x1, Pallas kernels, project_near(): pl.pallas_call(kernel, out_shape=[jax.ShapeDtypeStruct(shape, jnp.float32...  16.4 us
    pallas_call x2, Pallas kernels, mix_near(): pl.pallas_call(kernel, out_shape=jax.ShapeDtypeStruct((2 * half, cuts * c...  16.3 us
    pallas_call x3, Pallas kernels, attend(): pl.pallas_call(kernel, out_shape=out_shape, in_specs=[smem] * 3 + [vmem]...  13 us
  transfers between devices with their start and end apart: 31, of which 13 were waited for; matrix products, arithmetic and copies ran while one was open for 8% of the time, Pallas kernels for 19%

profile of v3, /device:TPU:2, one launch (start us, length us, event | category | flops | bytes accessed | tf_op | source)
XLA Modules:
  0.0 246.5 jit_solution(10026392612061859761)
XLA Ops:
  3.0 3.2 %collective-permute-start.2 = (bf16[80,640]{1,0:T(8,128)(2,1)}, bf16[80,640]{1,0:T(8,128)(2,1)S(1)}, u32[]{:S(2)}, u32[]{:S(2)}) collective-permute-start(bf16[80,640]{1,0:T(8,128)(2,1)} %get-tuple-element.130), channel_id=1, source_target_pairs={{0,2},{1,3},{2,0},{3,1},{4,6},{5,7},{6,4},{7,5},{8,10},{9,11},{10,... | collective-permute-start | bytes 307208 | tf_op jit(solution)/shard_map/ppermute | solution.py:440
  6.8 2.6 %collective-permute-start.1 = (bf16[80,640]{1,0:T(8,128)(2,1)S(1)}, bf16[80,640]{1,0:T(8,128)(2,1)S(1)}, u32[]{:S(2)}, u32[]{:S(2)}) collective-permute-start(bf16[80,640]{1,0:T(8,128)(2,1)S(1)} %get-tuple-element.132), channel_id=1, source_target_pairs={{0,3},{1,0},{2,1},{3,2},{4,7},{5,4},{6,5},{7,6},{8,11},{9,8},{10,9... | collective-permute-start | bytes 307208 | tf_op jit(solution)/shard_map/ppermute | solution.py:27
  17.8 3.2 %collective-permute-start.4 = (bf16[512,1280]{1,0:T(8,128)(2,1)}, bf16[512,1280]{1,0:T(8,128)(2,1)}, u32[]{:S(2)}, u32[]{:S(2)}) collective-permute-start(bf16[512,1280]{1,0:T(8,128)(2,1)} %get-tuple-element.65.refs_1_), channel_id=1, source_target_pairs={{0,3},{1,0},{2,1},{3,2},{4,7},{5,4},{6,5},{7,6},{8,11},{9,8},{10,9... | collective-permute-start | bytes 3932168 | tf_op jit(solution)/shard_map/ppermute | solution.py:27
  21.8 7.0 %all-to-all-start = ((s32[16,1,2]{2,1,0:T(1,128)}), s32[16,1,2]{2,1,0:T(1,128)S(1)}, u32[]{:S(2)}, u32[]{:S(2)}) async-start(s32[16,1,2]{2,1,0:T(1,128)} %copy.14), calls=%async_computation | async-start | bytes 16384 | tf_op jit(solution)/shard_map/all_to_all | solution.py:498
  28.8 3.6 %constant_dynamic-slice_fusion = (bf16[1280,640]{1,0:T(8,128)(2,1)S(1)}, bf16[1280,640]{1,0:T(8,128)(2,1)S(1)}, bf16[1280,640]{1,0:T(8,128)(2,1)S(1)}, bf16[1280,640]{1,0:T(8,128)(2,1)S(1)}) fusion(bf16[5120,640]{1,0:T(8,128)(2,1)} %param.16, s32[]{:T(128)S(6)} %select_n.114, s32[]{:T(128)S(6)} %select_n.113, s32[]{:T(128)S(6)} %select_n.112, s32[]{:T(128)S(6)} %select_n.111), kind=kLoop, calls=%fused_computation.27 | loop fusion | bytes 13107216 | tf_op jit(solution)/shard_map/dynamic_slice | solution.py:493
  39.2 4.2 %collective-permute-done.5 = s32[16,2]{0,1:T(2,128)S(1)} collective-permute-done((s32[16,2]{0,1:T(2,128)S(1)}, s32[16,2]{0,1:T(2,128)S(1)}, u32[]{:S(2)}, u32[]{:S(2)}) %collective-permute-start.5) | collective-permute-done | bytes 160 | tf_op jit(solution)/shard_map/ppermute | solution.py:501
  45.9 4.7 %collective-permute-done.9 = bf16[3,32,640]{2,1,0:T(8,128)(2,1)S(1)} collective-permute-done((bf16[3,32,640]{2,1,0:T(8,128)(2,1)S(1)}, bf16[3,32,640]{2,1,0:T(8,128)(2,1)S(1)}, u32[]{:S(2)}, u32[]{:S(2)}) %collective-permute-start.9) | collective-permute-done | bytes 122912 | tf_op jit(solution)/shard_map/ppermute | solution.py:27
  54.0 2.7 %collective-permute-start.15 = (bf16[4,3,80,640]{3,2,1,0:T(8,128)(2,1)S(1)}, bf16[4,3,80,640]{3,2,1,0:T(8,128)(2,1)S(1)}, u32[]{:S(2)}, u32[]{:S(2)}) collective-permute-start(bf16[4,3,80,640]{3,2,1,0:T(8,128)(2,1)S(1)} %pad_maximum_fusion.4.refs_0_), channel_id=1, source_target_pairs={{0,96},{32,0},{64,32},{96,64},{1,97},{33,1},{65,33},{97,65},{2,98}... | collective-permute-start | bytes 3686408 | tf_op jit(solution)/shard_map/ppermute | solution.py:27
  56.8 19.1 %collective-permute-done.13.refs_4_ = bf16[512,1280]{1,0:T(8,128)(2,1)} collective-permute-done((bf16[512,1280]{1,0:T(8,128)(2,1)}, bf16[512,1280]{1,0:T(8,128)(2,1)}, u32[]{:S(2)}, u32[]{:S(2)}) %collective-permute-start.13) | collective-permute-done | bytes 1310752 | tf_op jit(solution)/shard_map/ppermute | solution.py:27
  75.8 3.7 %collective-permute-start.11 = (bf16[512,1280]{1,0:T(8,128)(2,1)}, bf16[512,1280]{1,0:T(8,128)(2,1)S(1)}, u32[]{:S(2)}, u32[]{:S(2)}) collective-permute-start(bf16[512,1280]{1,0:T(8,128)(2,1)} %collective-permute-done.4.refs_5_), channel_id=1, source_target_pairs={{0,3},{1,0},{2,1},{3,2},{4,7},{5,4},{6,5},{7,6},{8,11},{9,8},{10,9... | collective-permute-start | bytes 3932168 | tf_op jit(solution)/shard_map/ppermute | solution.py:27
  79.5 4.2 %collective-permute-done.12.refs_3_ = bf16[512,1280]{1,0:T(8,128)(2,1)S(1)} collective-permute-done((bf16[512,1280]{1,0:T(8,128)(2,1)}, bf16[512,1280]{1,0:T(8,128)(2,1)S(1)}, u32[]{:S(2)}, u32[]{:S(2)}) %collective-permute-start.12) | collective-permute-done | bytes 1310752 | tf_op jit(solution)/shard_map/ppermute | solution.py:23
  85.9 2.4 collective-permute-start.17
  88.4 16.4 %project_near.1 = (f32[1024,896]{1,0:T(8,128)}, f32[1024,1]{1,0:T(8,128)}) custom-call(bf16[512,1280]{1,0:T(8,128)(2,1)} %get-tuple-element.64.refs_0_, bf16[512,1280]{1,0:T(8,128)(2,1)} %get-tuple-element.65.refs_1_, bf16[512,1280]{1,0:T(8,128)(2,1)} %collective-permute-done.3.refs_2_, bf16[512,1280]{1,0:T(8,128)(2,1)} %copy-done.22, ...), custom_call_target="tpu_custom_call" | custom-call | flops 1024 | bytes 1024 | tf_op jit(solution)/shard_map/project_near/pallas_call | solution.py:77
  104.8 4.6 %collective-permute-done.10.refs_1_ = bf16[512,1280]{1,0:T(8,128)(2,1)S(1)} collective-permute-done((bf16[512,1280]{1,0:T(8,128)(2,1)}, bf16[512,1280]{1,0:T(8,128)(2,1)S(1)}, u32[]{:S(2)}, u32[]{:S(2)}) %collective-permute-start.10) | collective-permute-done | bytes 1310752 | tf_op jit(solution)/shard_map/ppermute | solution.py:23
  109.4 2.5 %copy-done.5 = f32[1024,896]{1,0:T(8,128)S(1)} copy-done((f32[1024,896]{1,0:T(8,128)S(1)}, f32[1024,896]{1,0:T(8,128)}, u32[]{:S(2)}) %copy-start.5) | copy-done | bytes 3670040
  112.9 4.5 %project_far.1 = (bf16[16,64,640]{2,1,0:T(8,128)(2,1)S(1)}, bf16[16,64,256]{2,1,0:T(8,128)(2,1)S(1)}) custom-call(s32[16]{0:T(128)S(1)} %get-tuple-element.148.refs_0_, bf16[512,1280]{1,0:T(8,128)(2,1)S(1)} %collective-permute-done.10.refs_1_, bf16[512,1280]{1,0:T(8,128)(2,1)S(1)} %collective-permute-done.11.refs_2_, ...), custom_call_target="tpu_custom_call" | custom-call | flops 1024 | bytes 1024 | tf_op jit(solution)/shard_map/project_far/pallas_call | solution.py:125
  117.5 26.8 %all_to_all.32.refs_3_.refs_4_ = bf16[16,64,640]{2,1,0:T(8,128)(2,1)S(1)} all-to-all(bf16[16,64,640]{2,1,0:T(8,128)(2,1)S(1)} %get-tuple-element.89), channel_id=1, replica_groups=mesh['z'=4,'xh'=2,'core'=2,'context'=2,'tensor'=4] {'z','xh','core'}, dimensions={0} | all-to-all | bytes 2621440 | tf_op jit(solution)/shard_map/all_to_all | solution.py:498
  146.4 4.2 %all-to-all-start.3 = ((bf16[16,64,256]{2,1,0:T(8,128)(2,1)}), bf16[16,64,256]{2,1,0:T(8,128)(2,1)}, u32[]{:S(2)}, u32[]{:S(2)}) async-start(bf16[16,64,256]{2,1,0:T(8,128)(2,1)} %copy-done.19), calls=%async_computation.3 | async-start | bytes 1048576 | tf_op jit(solution)/shard_map/all_to_all | solution.py:498
  150.7 4.5 %attend.3 = (f32[4,1,768]{2,1,0:T(1,128)S(1)}, f32[4,1,768]{2,1,0:T(1,128)S(1)}, f32[4,128,768]{2,1,0:T(8,128)S(1)}) custom-call(s32[32]{0:T(128)S(1)} %pad_add_fusion.1.refs_0_, s32[32]{0:T(128)S(1)} %pad_add_fusion.2.refs_1_, s32[1]{0:T(128)} %bitcast.24.refs_2_, bf16[16,64,640]{2,1,0:T(8,128)(2,1)S(1)} %all_to_all.32.refs_3_.refs_4_, ...), custom_call_target="tpu_custom_call" | custom-call | flops 1024 | bytes 1024 | tf_op jit(solution)/shard_map/attend/pallas_call | solution.py:275
  155.2 6.9 %collective-permute-done.18.refs_5_ = bf16[16,64,256]{2,1,0:T(8,128)(2,1)S(1)} collective-permute-done((bf16[16,64,256]{2,1,0:T(8,128)(2,1)}, bf16[16,64,256]{2,1,0:T(8,128)(2,1)S(1)}, u32[]{:S(2)}, u32[]{:S(2)}) %collective-permute-start.18) | collective-permute-done | bytes 524320 | tf_op jit(solution)/shard_map/ppermute | solution.py:501
  162.1 2.7 %attend.4 = bf16[16,64,384]{2,1,0:T(8,128)(2,1)S(1)} custom-call(s32[32]{0:T(128)S(1)} %pad_add_fusion.1.refs_0_, s32[32]{0:T(128)S(1)} %pad_add_fusion.2.refs_1_, s32[1]{0:T(128)} %bitcast.24.refs_2_, bf16[16,64,640]{2,1,0:T(8,128)(2,1)S(1)} %all_to_all.32.refs_3_.refs_4_, bf16[16,64,640]{2,1,0:T(8,128)(2,1)S(1)} %all_to_all.32.refs_3_.refs_4_, ...), custom_call_target="tpu_custom_call" | custom-call | flops 1024 | bytes 1024 | tf_op jit(solution)/shard_map/attend/pallas_call | solution.py:275
  165.6 6.7 %all-to-all-start.2 = ((bf16[16,64,384]{2,1,0:T(8,128)(2,1)}), bf16[16,64,384]{2,1,0:T(8,128)(2,1)S(1)}, u32[]{:S(2)}, u32[]{:S(2)}) async-start(bf16[16,64,384]{2,1,0:T(8,128)(2,1)} %copy-done.6), calls=%async_computation.2 | async-start | bytes 1572864 | tf_op jit(solution)/shard_map/all_to_all | solution.py:498
  173.4 5.8 %attend.5 = bf16[16,64,256]{2,1,0:T(8,128)(2,1)S(1)} custom-call(s32[32]{0:T(128)S(1)} %pad_add_fusion.1.refs_0_, s32[32]{0:T(128)S(1)} %pad_add_fusion.2.refs_1_, s32[1]{0:T(128)} %bitcast.24.refs_2_, bf16[16,64,256]{2,1,0:T(8,128)(2,1)} %all-to-all-done.3.refs_3_, bf16[16,64,640]{2,1,0:T(8,128)(2,1)S(1)} %all_to_all.32.refs_3_.refs_4_, ...), custom_call_target="tpu_custom_call" | custom-call | flops 1024 | bytes 1024 | tf_op jit(solution)/shard_map/attend/pallas_call | solution.py:275
  180.1 7.5 %all-to-all-done.2 = bf16[16,64,384]{2,1,0:T(8,128)(2,1)S(1)} async-done(((bf16[16,64,384]{2,1,0:T(8,128)(2,1)}), bf16[16,64,384]{2,1,0:T(8,128)(2,1)S(1)}, u32[]{:S(2)}, u32[]{:S(2)}) %all-to-all-start.2) | async-done | bytes 786464 | tf_op jit(solution)/shard_map/all_to_all | solution.py:498
  189.6 4.2 %all-to-all-start.4 = ((bf16[16,64,256]{2,1,0:T(8,128)(2,1)}), bf16[16,64,256]{2,1,0:T(8,128)(2,1)}, u32[]{:S(2)}, u32[]{:S(2)}) async-start(bf16[16,64,256]{2,1,0:T(8,128)(2,1)} %copy-done.13), calls=%async_computation.4 | async-start | bytes 1048576 | tf_op jit(solution)/shard_map/all_to_all | solution.py:498
  201.8 4.4 %all-to-all-done.4 = bf16[16,64,256]{2,1,0:T(8,128)(2,1)} async-done(((bf16[16,64,256]{2,1,0:T(8,128)(2,1)}), bf16[16,64,256]{2,1,0:T(8,128)(2,1)}, u32[]{:S(2)}, u32[]{:S(2)}) %all-to-all-start.4) | async-done | bytes 524320 | tf_op jit(solution)/shard_map/all_to_all | solution.py:498
  214.1 2.4 copy-done.1
  216.5 9.0 %mix_near.2.refs_8_ = f32[1024,1280]{1,0:T(8,128)S(1)} custom-call(s32[16]{0:T(128)S(1)} %select_reduce_fusion.4.refs_0_, s32[1]{0:T(128)} %bitcast.29.refs_1_, bf16[1024,384]{1,0:T(8,128)(2,1)S(1)} %bitcast.45, bf16[1024,384]{1,0:T(8,128)(2,1)} %collective-permute-done.19.refs_3_, bf16[1024,384]{1,0:T(8,128)(2,1)} %collective-permute-done.20.refs_4_, ...), custom_call_target="tpu_custom_call" | custom-call | flops 1024 | bytes 1024 | tf_op jit(solution)/shard_map/mix_near/pallas_call | solution.py:364
  225.5 2.3 copy-done.2
  230.7 3.1 %collective-permute-start.26 = (bf16[512,256]{1,0:T(8,128)(2,1)S(1)}, bf16[512,256]{1,0:T(8,128)(2,1)S(1)}, u32[]{:S(2)}, u32[]{:S(2)}) collective-permute-start(bf16[512,256]{1,0:T(8,128)(2,1)S(1)} %slice.63), channel_id=1, source_target_pairs={{0,3},{1,0},{2,1},{3,2},{4,7},{5,4},{6,5},{7,6},{8,11},{9,8},{10,9... | collective-permute-start | bytes 786440 | tf_op jit(solution)/shard_map/ppermute | solution.py:27
  233.8 7.3 %mix_near.3.refs_4_ = f32[1024,1280]{1,0:T(8,128)S(1)} custom-call(s32[16]{0:T(128)S(1)} %select_reduce_fusion.4.refs_0_, s32[1]{0:T(128)} %bitcast.29.refs_1_, bf16[512,384]{1,0:T(8,128)(2,1)S(1)} %collective-permute-done.23.refs_2_, bf16[512,384]{1,0:T(8,128)(2,1)S(1)} %collective-permute-done.24.refs_3_, ...), custom_call_target="tpu_custom_call" | custom-call | flops 1024 | bytes 1024 | tf_op jit(solution)/shard_map/mix_near/pallas_call | solution.py:364
  241.1 5.4 %mix_far.1 = bf16[16,64,1280]{2,1,0:T(8,128)(2,1)} custom-call(s32[16]{0:T(128)S(1)} %select_reduce_fusion.4.refs_0_, bf16[512,256]{1,0:T(8,128)(2,1)S(1)} %collective-permute-done.25.refs_1_, bf16[512,256]{1,0:T(8,128)(2,1)S(1)} %collective-permute-done.26.refs_2_, bf16[8,2,3,80,640]{4,3,2,1,0:T(8,128)(2,1)S(1)} %copy-done.1, f32[1024,1280]{1,0:T(8,128)S(1)} %mix_near.3.refs_4_), custom_call_target="tpu_custom_call" | custom-call | flops 1024 | bytes 1024 | tf_op jit(solution)/shard_map/mix_far/pallas_call | solution.py:404
  (147 shorter events, 54.2 us)
Async XLA Ops:
  3.0 12.0 %collective-permute-start.2 = (bf16[80,640]{1,0:T(8,128)(2,1)}, bf16[80,640]{1,0:T(8,128)(2,1)S(1)}, u32[]{:S(2)}, u32[]{:S(2)}) collective-permute-start(bf16[80,640]{1,0:T(8,128)(2,1)} %get-tuple-element.130), channel_id=1, source_target_pairs={{0,2},{1,3},{2,0},{3,1},{4,6},{5,7},{6,4},{7,5},{8,10},{9,11},{10,... | collective-permute-start | bytes 307208 | tf_op jit(solution)/shard_map/ppermute | solution.py:440
  6.2 8.8 %collective-permute-start = (bf16[80,640]{1,0:T(8,128)(2,1)}, bf16[80,640]{1,0:T(8,128)(2,1)S(1)}, u32[]{:S(2)}, u32[]{:S(2)}) collective-permute-start(bf16[80,640]{1,0:T(8,128)(2,1)} %get-tuple-element.131), channel_id=1, source_target_pairs={{0,1},{1,2},{2,3},{3,0},{4,5},{5,6},{6,7},{7,4},{8,9},{9,10},{10,1... | collective-permute-start | bytes 307208 | tf_op jit(solution)/shard_map/ppermute | solution.py:23
  6.8 8.2 %collective-permute-start.1 = (bf16[80,640]{1,0:T(8,128)(2,1)S(1)}, bf16[80,640]{1,0:T(8,128)(2,1)S(1)}, u32[]{:S(2)}, u32[]{:S(2)}) collective-permute-start(bf16[80,640]{1,0:T(8,128)(2,1)S(1)} %get-tuple-element.132), channel_id=1, source_target_pairs={{0,3},{1,0},{2,1},{3,2},{4,7},{5,4},{6,5},{7,6},{8,11},{9,8},{10,9... | collective-permute-start | bytes 307208 | tf_op jit(solution)/shard_map/ppermute | solution.py:27
  15.8 27.7 %collective-permute-start.6 = (bf16[3,80,640]{2,1,0:T(8,128)(2,1)S(1)}, bf16[3,80,640]{2,1,0:T(8,128)(2,1)S(1)}, u32[]{:S(2)}, u32[]{:S(2)}) collective-permute-start(bf16[3,80,640]{2,1,0:T(8,128)(2,1)S(1)} %get-tuple-element.134), channel_id=1, source_target_pairs={{0,4},{4,16},{16,20},{20,0},{1,5},{5,17},{17,21},{21,1},{2,6},{6,1... | collective-permute-start | bytes 921608 | tf_op jit(solution)/shard_map/ppermute | solution.py:23
  17.3 28.0 %collective-permute-start.7 = (bf16[3,80,640]{2,1,0:T(8,128)(2,1)S(1)}, bf16[3,80,640]{2,1,0:T(8,128)(2,1)S(1)}, u32[]{:S(2)}, u32[]{:S(2)}) collective-permute-start(bf16[3,80,640]{2,1,0:T(8,128)(2,1)S(1)} %get-tuple-element.134), channel_id=1, source_target_pairs={{0,20},{4,0},{16,4},{20,16},{1,21},{5,1},{17,5},{21,17},{2,22},{6,... | collective-permute-start | bytes 921608 | tf_op jit(solution)/shard_map/ppermute | solution.py:27
  17.8 36.2 %collective-permute-start.3 = (bf16[512,1280]{1,0:T(8,128)(2,1)}, bf16[512,1280]{1,0:T(8,128)(2,1)}, u32[]{:S(2)}, u32[]{:S(2)}) collective-permute-start(bf16[512,1280]{1,0:T(8,128)(2,1)} %get-tuple-element.64.refs_0_), channel_id=1, source_target_pairs={{0,1},{1,2},{2,3},{3,0},{4,5},{5,6},{6,7},{7,4},{8,9},{9,10},{10,1... | collective-permute-start | bytes 3932168 | tf_op jit(solution)/shard_map/ppermute | solution.py:23
  17.8 36.2 %collective-permute-start.4 = (bf16[512,1280]{1,0:T(8,128)(2,1)}, bf16[512,1280]{1,0:T(8,128)(2,1)}, u32[]{:S(2)}, u32[]{:S(2)}) collective-permute-start(bf16[512,1280]{1,0:T(8,128)(2,1)} %get-tuple-element.65.refs_1_), channel_id=1, source_target_pairs={{0,3},{1,0},{2,1},{3,2},{4,7},{5,4},{6,5},{7,6},{8,11},{9,8},{10,9... | collective-permute-start | bytes 3932168 | tf_op jit(solution)/shard_map/ppermute | solution.py:27
  21.8 16.0 %all-to-all-start = ((s32[16,1,2]{2,1,0:T(1,128)}), s32[16,1,2]{2,1,0:T(1,128)S(1)}, u32[]{:S(2)}, u32[]{:S(2)}) async-start(s32[16,1,2]{2,1,0:T(1,128)} %copy.14), calls=%async_computation | async-start | bytes 16384 | tf_op jit(solution)/shard_map/all_to_all | solution.py:498
  37.9 5.5 %collective-permute-start.5 = (s32[16,2]{0,1:T(2,128)S(1)}, s32[16,2]{0,1:T(2,128)S(1)}, u32[]{:S(2)}, u32[]{:S(2)}) collective-permute-start(s32[16,2]{0,1:T(2,128)S(1)} %bitcast.52), channel_id=1, source_target_pairs={{0,4},{1,5},{2,6},{3,7},{8,12},{9,13},{10,14},{11,15},{16,20},{17,... | collective-permute-start | bytes 392 | tf_op jit(solution)/shard_map/ppermute | solution.py:501
  43.3 32.5 %collective-permute-start.13 = (bf16[512,1280]{1,0:T(8,128)(2,1)}, bf16[512,1280]{1,0:T(8,128)(2,1)}, u32[]{:S(2)}, u32[]{:S(2)}) collective-permute-start(bf16[512,1280]{1,0:T(8,128)(2,1)} %get-tuple-element.64.refs_0_), channel_id=1, source_target_pairs={{0,3},{1,0},{2,1},{3,2},{4,7},{5,4},{6,5},{7,6},{8,11},{9,8},{10,9... | collective-permute-start | bytes 3932168 | tf_op jit(solution)/shard_map/ppermute | solution.py:27
  43.5 9.0 %collective-permute-start.8 = (bf16[3,48,640]{2,1,0:T(8,128)(2,1)S(1)}, bf16[3,48,640]{2,1,0:T(8,128)(2,1)S(1)}, u32[]{:S(2)}, u32[]{:S(2)}) collective-permute-start(bf16[3,48,640]{2,1,0:T(8,128)(2,1)S(1)} %slice.68), channel_id=1, source_target_pairs={{0,4},{4,16},{16,20},{20,0},{1,5},{5,17},{17,21},{21,1},{2,6},{6,1... | collective-permute-start | bytes 552968 | tf_op jit(solution)/shard_map/ppermute | solution.py:23
  45.3 5.2 %collective-permute-start.9 = (bf16[3,32,640]{2,1,0:T(8,128)(2,1)S(1)}, bf16[3,32,640]{2,1,0:T(8,128)(2,1)S(1)}, u32[]{:S(2)}, u32[]{:S(2)}) collective-permute-start(bf16[3,32,640]{2,1,0:T(8,128)(2,1)S(1)} %slice.69), channel_id=1, source_target_pairs={{0,20},{4,0},{16,4},{20,16},{1,21},{5,1},{17,5},{21,17},{2,22},{6,... | collective-permute-start | bytes 368648 | tf_op jit(solution)/shard_map/ppermute | solution.py:27
  50.5 33.1 %collective-permute-start.12 = (bf16[512,1280]{1,0:T(8,128)(2,1)}, bf16[512,1280]{1,0:T(8,128)(2,1)S(1)}, u32[]{:S(2)}, u32[]{:S(2)}) collective-permute-start(bf16[512,1280]{1,0:T(8,128)(2,1)} %get-tuple-element.65.refs_1_), channel_id=1, source_target_pairs={{0,1},{1,2},{2,3},{3,0},{4,5},{5,6},{6,7},{7,4},{8,9},{9,10},{10,1... | collective-permute-start | bytes 3932168 | tf_op jit(solution)/shard_map/ppermute | solution.py:23
  52.6 35.8 %copy-start.26 = (bf16[128]{0:T(256)(128)(2,1)S(1)}, bf16[128]{0:T(256)(128)(2,1)}, u32[]{:S(2)}) copy-start(bf16[128]{0:T(256)(128)(2,1)} %param.20) | copy-start | bytes 772
  54.0 29.7 %collective-permute-start.15 = (bf16[4,3,80,640]{3,2,1,0:T(8,128)(2,1)S(1)}, bf16[4,3,80,640]{3,2,1,0:T(8,128)(2,1)S(1)}, u32[]{:S(2)}, u32[]{:S(2)}) collective-permute-start(bf16[4,3,80,640]{3,2,1,0:T(8,128)(2,1)S(1)} %pad_maximum_fusion.4.refs_0_), channel_id=1, source_target_pairs={{0,96},{32,0},{64,32},{96,64},{1,97},{33,1},{65,33},{97,65},{2,98}... | collective-permute-start | bytes 3686408 | tf_op jit(solution)/shard_map/ppermute | solution.py:27
  56.8 27.9 %collective-permute-start.14 = (bf16[4,3,80,640]{3,2,1,0:T(8,128)(2,1)S(1)}, bf16[4,3,80,640]{3,2,1,0:T(8,128)(2,1)S(1)}, u32[]{:S(2)}, u32[]{:S(2)}) collective-permute-start(bf16[4,3,80,640]{3,2,1,0:T(8,128)(2,1)S(1)} %pad_maximum_fusion.4.refs_0_), channel_id=1, source_target_pairs={{0,32},{32,64},{64,96},{96,0},{1,33},{33,65},{65,97},{97,1},{2,34}... | collective-permute-start | bytes 3686408 | tf_op jit(solution)/shard_map/ppermute | solution.py:23
  56.8 52.6 %collective-permute-start.10 = (bf16[512,1280]{1,0:T(8,128)(2,1)}, bf16[512,1280]{1,0:T(8,128)(2,1)S(1)}, u32[]{:S(2)}, u32[]{:S(2)}) collective-permute-start(bf16[512,1280]{1,0:T(8,128)(2,1)} %collective-permute-done.3.refs_2_), channel_id=1, source_target_pairs={{0,1},{1,2},{2,3},{3,0},{4,5},{5,6},{6,7},{7,4},{8,9},{9,10},{10,1... | collective-permute-start | bytes 3932168 | tf_op jit(solution)/shard_map/ppermute | solution.py:23
  75.8 33.6 %collective-permute-start.11 = (bf16[512,1280]{1,0:T(8,128)(2,1)}, bf16[512,1280]{1,0:T(8,128)(2,1)S(1)}, u32[]{:S(2)}, u32[]{:S(2)}) collective-permute-start(bf16[512,1280]{1,0:T(8,128)(2,1)} %collective-permute-done.4.refs_5_), channel_id=1, source_target_pairs={{0,3},{1,0},{2,1},{3,2},{4,7},{5,4},{6,5},{7,6},{8,11},{9,8},{10,9... | collective-permute-start | bytes 3932168 | tf_op jit(solution)/shard_map/ppermute | solution.py:27
  85.9 23.5 %collective-permute-start.17 = (bf16[2,3,80,640]{3,2,1,0:T(8,128)(2,1)}, bf16[2,3,80,640]{3,2,1,0:T(8,128)(2,1)S(1)}, u32[]{:S(2)}, u32[]{:S(2)}) collective-permute-start(bf16[2,3,80,640]{3,2,1,0:T(8,128)(2,1)} %slice.58), channel_id=1, source_target_pairs={{0,96},{32,0},{64,32},{96,64},{1,97},{33,1},{65,33},{97,65},{2,98}... | collective-permute-start | bytes 1843208 | tf_op jit(solution)/shard_map/ppermute | solution.py:27
  88.4 21.0 %collective-permute-start.16 = (bf16[2,3,80,640]{3,2,1,0:T(8,128)(2,1)S(1)}, bf16[2,3,80,640]{3,2,1,0:T(8,128)(2,1)S(1)}, u32[]{:S(2)}, u32[]{:S(2)}) collective-permute-start(bf16[2,3,80,640]{3,2,1,0:T(8,128)(2,1)S(1)} %slice.57), channel_id=1, source_target_pairs={{0,32},{32,64},{64,96},{96,0},{1,33},{33,65},{65,97},{97,1},{2,34}... | collective-permute-start | bytes 1843208 | tf_op jit(solution)/shard_map/ppermute | solution.py:23
  145.1 17.0 %collective-permute-start.18 = (bf16[16,64,256]{2,1,0:T(8,128)(2,1)}, bf16[16,64,256]{2,1,0:T(8,128)(2,1)S(1)}, u32[]{:S(2)}, u32[]{:S(2)}) collective-permute-start(bf16[16,64,256]{2,1,0:T(8,128)(2,1)} %slice.70), channel_id=1, source_target_pairs={{0,4},{1,5},{2,6},{3,7},{8,12},{9,13},{10,14},{11,15},{16,20},{17,... | collective-permute-start | bytes 1572872 | tf_op jit(solution)/shard_map/ppermute | solution.py:501
  146.4 19.2 %all-to-all-start.3 = ((bf16[16,64,256]{2,1,0:T(8,128)(2,1)}), bf16[16,64,256]{2,1,0:T(8,128)(2,1)}, u32[]{:S(2)}, u32[]{:S(2)}) async-start(bf16[16,64,256]{2,1,0:T(8,128)(2,1)} %copy-done.19), calls=%async_computation.3 | async-start | bytes 1048576 | tf_op jit(solution)/shard_map/all_to_all | solution.py:498
  165.6 21.9 %all-to-all-start.2 = ((bf16[16,64,384]{2,1,0:T(8,128)(2,1)}), bf16[16,64,384]{2,1,0:T(8,128)(2,1)S(1)}, u32[]{:S(2)}, u32[]{:S(2)}) async-start(bf16[16,64,384]{2,1,0:T(8,128)(2,1)} %copy-done.6), calls=%async_computation.2 | async-start | bytes 1572864 | tf_op jit(solution)/shard_map/all_to_all | solution.py:498
  187.6 19.1 %collective-permute-start.20 = (bf16[1024,384]{1,0:T(8,128)(2,1)S(1)}, bf16[1024,384]{1,0:T(8,128)(2,1)}, u32[]{:S(2)}, u32[]{:S(2)}) collective-permute-start(bf16[1024,384]{1,0:T(8,128)(2,1)S(1)} %bitcast.43), channel_id=1, source_target_pairs={{0,3},{1,0},{2,1},{3,2},{4,7},{5,4},{6,5},{7,6},{8,11},{9,8},{10,9... | collective-permute-start | bytes 2359304 | tf_op jit(solution)/shard_map/ppermute | solution.py:27
  187.8 20.1 %collective-permute-start.19 = (bf16[1024,384]{1,0:T(8,128)(2,1)S(1)}, bf16[1024,384]{1,0:T(8,128)(2,1)}, u32[]{:S(2)}, u32[]{:S(2)}) collective-permute-start(bf16[1024,384]{1,0:T(8,128)(2,1)S(1)} %bitcast.44), channel_id=1, source_target_pairs={{0,1},{1,2},{2,3},{3,0},{4,5},{5,6},{6,7},{7,4},{8,9},{9,10},{10,1... | collective-permute-start | bytes 2359304 | tf_op jit(solution)/shard_map/ppermute | solution.py:23
  189.6 16.6 %all-to-all-start.4 = ((bf16[16,64,256]{2,1,0:T(8,128)(2,1)}), bf16[16,64,256]{2,1,0:T(8,128)(2,1)}, u32[]{:S(2)}, u32[]{:S(2)}) async-start(bf16[16,64,256]{2,1,0:T(8,128)(2,1)} %copy-done.13), calls=%async_computation.4 | async-start | bytes 1048576 | tf_op jit(solution)/shard_map/all_to_all | solution.py:498
  207.9 22.5 %collective-permute-start.22 = (bf16[1024,256]{1,0:T(8,128)(2,1)}, bf16[1024,256]{1,0:T(8,128)(2,1)S(1)}, u32[]{:S(2)}, u32[]{:S(2)}) collective-permute-start(bf16[1024,256]{1,0:T(8,128)(2,1)} %bitcast.26.refs_5_), channel_id=1, source_target_pairs={{0,3},{1,0},{2,1},{3,2},{4,7},{5,4},{6,5},{7,6},{8,11},{9,8},{10,9... | collective-permute-start | bytes 1572872 | tf_op jit(solution)/shard_map/ppermute | solution.py:27
  208.2 22.2 %collective-permute-start.21 = (bf16[1024,256]{1,0:T(8,128)(2,1)}, bf16[1024,256]{1,0:T(8,128)(2,1)S(1)}, u32[]{:S(2)}, u32[]{:S(2)}) collective-permute-start(bf16[1024,256]{1,0:T(8,128)(2,1)} %bitcast.26.refs_5_), channel_id=1, source_target_pairs={{0,1},{1,2},{2,3},{3,0},{4,5},{5,6},{6,7},{7,4},{8,9},{9,10},{10,1... | collective-permute-start | bytes 1572872 | tf_op jit(solution)/shard_map/ppermute | solution.py:23
  212.0 16.8 %collective-permute-start.24 = (bf16[512,384]{1,0:T(8,128)(2,1)S(1)}, bf16[512,384]{1,0:T(8,128)(2,1)S(1)}, u32[]{:S(2)}, u32[]{:S(2)}) collective-permute-start(bf16[512,384]{1,0:T(8,128)(2,1)S(1)} %slice.61), channel_id=1, source_target_pairs={{0,3},{1,0},{2,1},{3,2},{4,7},{5,4},{6,5},{7,6},{8,11},{9,8},{10,9... | collective-permute-start | bytes 1179656 | tf_op jit(solution)/shard_map/ppermute | solution.py:27
  213.6 16.8 %collective-permute-start.23 = (bf16[512,384]{1,0:T(8,128)(2,1)S(1)}, bf16[512,384]{1,0:T(8,128)(2,1)S(1)}, u32[]{:S(2)}, u32[]{:S(2)}) collective-permute-start(bf16[512,384]{1,0:T(8,128)(2,1)S(1)} %slice.60), channel_id=1, source_target_pairs={{0,1},{1,2},{2,3},{3,0},{4,5},{5,6},{6,7},{7,4},{8,9},{9,10},{10,1... | collective-permute-start | bytes 1179656 | tf_op jit(solution)/shard_map/ppermute | solution.py:23
  230.4 10.7 %collective-permute-start.25 = (bf16[512,256]{1,0:T(8,128)(2,1)S(1)}, bf16[512,256]{1,0:T(8,128)(2,1)S(1)}, u32[]{:S(2)}, u32[]{:S(2)}) collective-permute-start(bf16[512,256]{1,0:T(8,128)(2,1)S(1)} %slice.62), channel_id=1, source_target_pairs={{0,1},{1,2},{2,3},{3,0},{4,5},{5,6},{6,7},{7,4},{8,9},{9,10},{10,1... | collective-permute-start | bytes 786440 | tf_op jit(solution)/shard_map/ppermute | solution.py:23
  230.7 10.4 %collective-permute-start.26 = (bf16[512,256]{1,0:T(8,128)(2,1)S(1)}, bf16[512,256]{1,0:T(8,128)(2,1)S(1)}, u32[]{:S(2)}, u32[]{:S(2)}) collective-permute-start(bf16[512,256]{1,0:T(8,128)(2,1)S(1)} %slice.63), channel_id=1, source_target_pairs={{0,3},{1,0},{2,1},{3,2},{4,7},{5,4},{6,5},{7,6},{8,11},{9,8},{10,9... | collective-permute-start | bytes 786440 | tf_op jit(solution)/shard_map/ppermute | solution.py:27
  (27 other events, 172.2 us)

commit v4 on v3

--- a/solution.py
+++ b/solution.py
@@ -392,7 +392,7 @@
 
 
 def mix_far(page_of, top, low, cut, w_all, before):
-    blocks = 4
+    blocks = 2
     half, width = top.shape
     outer, cuts, places, stored, columns = w_all.shape
     block = 2 * half // blocks
@@ -459,7 +459,7 @@
         out_shape=jax.ShapeDtypeStruct((8, 2) + sources[0].shape[1:], jnp.bfloat16),
         in_specs=[pl.BlockSpec(memory_space=pltpu.SMEM)] + [vmem] * len(sources),
         out_specs=vmem,
-        compiler_params=pltpu.CompilerParams(vmem_limit_bytes=24 * MIB),
+        compiler_params=pltpu.CompilerParams(vmem_limit_bytes=60 * MIB),
         cost_estimate=SMALL,
         name="place_shares",
     )(where, *sources)

time: 249 us -> 246 us (0.988)
  Pallas kernels: 56.5 us -> 72.8 us
  local copies, waits for them, and re-layouts: 33.8 us -> 21.5 us
  starting transfers between devices: 58.9 us -> 55.1 us
    pallas_call x3, Pallas kernels: 13 us -> 26.7 us  [attend(): pl.pallas_call(kernel, out_shape=out_shape, in_specs=[smem] * 3 + [vmem]...]
    unnamed x56 -> x36, local copies, waits for them, and re-layouts: 18.2 us -> 8.68 us
    all_to_all x4, starting transfers between devices: 22.2 us -> 18 us  [exchange(): return lax.all_to_all(rows, DP, split_axis=0, concat_axis=0, tiled=True)]
    pallas_call x1, Pallas kernels: 0.94 us -> 5 us  [place_shares(): pl.pallas_call(place_kernel, out_shape=jax.ShapeDtypeStruct((8, 2) + sour...]
    ppermute x12, waiting for transfers between devices: 25.2 us -> 29.2 us  [to_left(): return lax.ppermute(block, axis, [(i, (i - 1) % RING) for i in range(RING)])]
  transfers between devices with their start and end apart: 31 -> 31, of which waited for: 13 -> 12; matrix products, arithmetic and copies ran while one was open for 8% -> 7% of each run, Pallas kernels for 19% -> 26%
where the time goes in v4:
time: 246 us; the launch traced here: 245 us
  Pallas kernels  72.8 us (30%)
  waiting for transfers between devices  60.8 us (25%)
  starting transfers between devices  55.1 us (22%)
  blocking collectives  26.9 us (11%)
  local copies, waits for them, and re-layouts  21.5 us (9%)
  other arithmetic  7.85 us (3%)
    ppermute x12, waiting for transfers between devices, to_left(): return lax.ppermute(block, axis, [(i, (i - 1) % RING) for i in range(RING)])  29.2 us
    all_to_all x1, blocking collectives, exchange(): return lax.all_to_all(rows, DP, split_axis=0, concat_axis=0, tiled=True)  26.9 us
    pallas_call x3, Pallas kernels, attend(): pl.pallas_call(kernel, out_shape=out_shape, in_specs=[smem] * 3 + [vmem]...  26.7 us
    ppermute x12, starting transfers between devices, to_left(): return lax.ppermute(block, axis, [(i, (i - 1) % RING) for i in range(RING)])  20.9 us
    all_to_all x4, starting transfers between devices, exchange(): return lax.all_to_all(rows, DP, split_axis=0, concat_axis=0, tiled=True)  18 us
    pallas_call x1, Pallas kernels, project_near(): pl.pallas_call(kernel, out_shape=[jax.ShapeDtypeStruct(shape, jnp.float32...  16.4 us
    pallas_call x2, Pallas kernels, mix_near(): pl.pallas_call(kernel, out_shape=jax.ShapeDtypeStruct((2 * half, cuts * c...  15.9 us
    ppermute x12, waiting for transfers between devices, to_right(): return lax.ppermute(block, axis, [(i, (i + 1) % RING) for i in range(RING)])  12.3 us
  transfers between devices with their start and end apart: 31, of which 12 were waited for; matrix products, arithmetic and copies ran while one was open for 7% of the time, Pallas kernels for 26%

profile of v4, /device:TPU:2, one launch (start us, length us, event | category | flops | bytes accessed | tf_op | source)
XLA Modules:
  0.0 245.5 jit_solution(17647443253836131664)
XLA Ops:
  3.0 3.2 %collective-permute-start.2 = (bf16[80,640]{1,0:T(8,128)(2,1)}, bf16[80,640]{1,0:T(8,128)(2,1)S(1)}, u32[]{:S(2)}, u32[]{:S(2)}) collective-permute-start(bf16[80,640]{1,0:T(8,128)(2,1)} %get-tuple-element.130), channel_id=1, source_target_pairs={{0,2},{1,3},{2,0},{3,1},{4,6},{5,7},{6,4},{7,5},{8,10},{9,11},{10,... | collective-permute-start | bytes 307208 | tf_op jit(solution)/shard_map/ppermute | solution.py:440
  6.8 2.6 %collective-permute-start.1 = (bf16[80,640]{1,0:T(8,128)(2,1)S(1)}, bf16[80,640]{1,0:T(8,128)(2,1)S(1)}, u32[]{:S(2)}, u32[]{:S(2)}) collective-permute-start(bf16[80,640]{1,0:T(8,128)(2,1)S(1)} %get-tuple-element.132), channel_id=1, source_target_pairs={{0,3},{1,0},{2,1},{3,2},{4,7},{5,4},{6,5},{7,6},{8,11},{9,8},{10,9... | collective-permute-start | bytes 307208 | tf_op jit(solution)/shard_map/ppermute | solution.py:27
  17.2 3.2 %collective-permute-start.4 = (bf16[512,1280]{1,0:T(8,128)(2,1)}, bf16[512,1280]{1,0:T(8,128)(2,1)}, u32[]{:S(2)}, u32[]{:S(2)}) collective-permute-start(bf16[512,1280]{1,0:T(8,128)(2,1)} %get-tuple-element.65.refs_1_), channel_id=1, source_target_pairs={{0,3},{1,0},{2,1},{3,2},{4,7},{5,4},{6,5},{7,6},{8,11},{9,8},{10,9... | collective-permute-start | bytes 3932168 | tf_op jit(solution)/shard_map/ppermute | solution.py:27
  21.1 7.0 %all-to-all-start = ((s32[16,1,2]{2,1,0:T(1,128)}), s32[16,1,2]{2,1,0:T(1,128)S(1)}, u32[]{:S(2)}, u32[]{:S(2)}) async-start(s32[16,1,2]{2,1,0:T(1,128)} %copy.14), calls=%async_computation | async-start | bytes 16384 | tf_op jit(solution)/shard_map/all_to_all | solution.py:498
  28.1 3.6 %constant_dynamic-slice_fusion = (bf16[1280,640]{1,0:T(8,128)(2,1)S(1)}, bf16[1280,640]{1,0:T(8,128)(2,1)S(1)}, bf16[1280,640]{1,0:T(8,128)(2,1)S(1)}, bf16[1280,640]{1,0:T(8,128)(2,1)S(1)}) fusion(bf16[5120,640]{1,0:T(8,128)(2,1)} %param.16, s32[]{:T(128)S(6)} %select_n.114, s32[]{:T(128)S(6)} %select_n.113, s32[]{:T(128)S(6)} %select_n.112, s32[]{:T(128)S(6)} %select_n.111), kind=kLoop, calls=%fused_computation.27 | loop fusion | bytes 13107216 | tf_op jit(solution)/shard_map/dynamic_slice | solution.py:493
  38.5 4.2 %collective-permute-done.5 = s32[16,2]{0,1:T(2,128)S(1)} collective-permute-done((s32[16,2]{0,1:T(2,128)S(1)}, s32[16,2]{0,1:T(2,128)S(1)}, u32[]{:S(2)}, u32[]{:S(2)}) %collective-permute-start.5) | collective-permute-done | bytes 160 | tf_op jit(solution)/shard_map/ppermute | solution.py:501
  45.2 4.7 %collective-permute-done.9 = bf16[3,32,640]{2,1,0:T(8,128)(2,1)S(1)} collective-permute-done((bf16[3,32,640]{2,1,0:T(8,128)(2,1)S(1)}, bf16[3,32,640]{2,1,0:T(8,128)(2,1)S(1)}, u32[]{:S(2)}, u32[]{:S(2)}) %collective-permute-start.9) | collective-permute-done | bytes 122912 | tf_op jit(solution)/shard_map/ppermute | solution.py:27
  52.2 2.7 %collective-permute-start.15 = (bf16[4,3,80,640]{3,2,1,0:T(8,128)(2,1)S(1)}, bf16[4,3,80,640]{3,2,1,0:T(8,128)(2,1)S(1)}, u32[]{:S(2)}, u32[]{:S(2)}) collective-permute-start(bf16[4,3,80,640]{3,2,1,0:T(8,128)(2,1)S(1)} %pad_maximum_fusion.4.refs_0_), channel_id=1, source_target_pairs={{0,96},{32,0},{64,32},{96,64},{1,97},{33,1},{65,33},{97,65},{2,98}... | collective-permute-start | bytes 3686408 | tf_op jit(solution)/shard_map/ppermute | solution.py:27
  54.9 20.2 %collective-permute-done.13.refs_4_ = bf16[512,1280]{1,0:T(8,128)(2,1)} collective-permute-done((bf16[512,1280]{1,0:T(8,128)(2,1)}, bf16[512,1280]{1,0:T(8,128)(2,1)}, u32[]{:S(2)}, u32[]{:S(2)}) %collective-permute-start.13) | collective-permute-done | bytes 1310752 | tf_op jit(solution)/shard_map/ppermute | solution.py:27
  75.2 3.7 %collective-permute-start.11 = (bf16[512,1280]{1,0:T(8,128)(2,1)}, bf16[512,1280]{1,0:T(8,128)(2,1)S(1)}, u32[]{:S(2)}, u32[]{:S(2)}) collective-permute-start(bf16[512,1280]{1,0:T(8,128)(2,1)} %collective-permute-done.4.refs_5_), channel_id=1, source_target_pairs={{0,3},{1,0},{2,1},{3,2},{4,7},{5,4},{6,5},{7,6},{8,11},{9,8},{10,9... | collective-permute-start | bytes 3932168 | tf_op jit(solution)/shard_map/ppermute | solution.py:27
  78.9 4.1 %collective-permute-done.12.refs_3_ = bf16[512,1280]{1,0:T(8,128)(2,1)S(1)} collective-permute-done((bf16[512,1280]{1,0:T(8,128)(2,1)}, bf16[512,1280]{1,0:T(8,128)(2,1)S(1)}, u32[]{:S(2)}, u32[]{:S(2)}) %collective-permute-start.12) | collective-permute-done | bytes 1310752 | tf_op jit(solution)/shard_map/ppermute | solution.py:23
  84.1 2.7 %collective-permute-start.17 = (bf16[2,3,80,640]{3,2,1,0:T(8,128)(2,1)}, bf16[2,3,80,640]{3,2,1,0:T(8,128)(2,1)S(1)}, u32[]{:S(2)}, u32[]{:S(2)}) collective-permute-start(bf16[2,3,80,640]{3,2,1,0:T(8,128)(2,1)} %slice.58), channel_id=1, source_target_pairs={{0,96},{32,0},{64,32},{96,64},{1,97},{33,1},{65,33},{97,65},{2,98}... | collective-permute-start | bytes 1843208 | tf_op jit(solution)/shard_map/ppermute | solution.py:27
  86.9 16.4 %project_near.1 = (f32[1024,896]{1,0:T(8,128)}, f32[1024,1]{1,0:T(8,128)}) custom-call(bf16[512,1280]{1,0:T(8,128)(2,1)} %get-tuple-element.64.refs_0_, bf16[512,1280]{1,0:T(8,128)(2,1)} %get-tuple-element.65.refs_1_, bf16[512,1280]{1,0:T(8,128)(2,1)} %collective-permute-done.3.refs_2_, bf16[512,1280]{1,0:T(8,128)(2,1)} %copy-done.12, ...), custom_call_target="tpu_custom_call" | custom-call | flops 1024 | bytes 1024 | tf_op jit(solution)/shard_map/project_near/pallas_call | solution.py:77
  103.3 5.4 %collective-permute-done.10.refs_1_ = bf16[512,1280]{1,0:T(8,128)(2,1)S(1)} collective-permute-done((bf16[512,1280]{1,0:T(8,128)(2,1)}, bf16[512,1280]{1,0:T(8,128)(2,1)S(1)}, u32[]{:S(2)}, u32[]{:S(2)}) %collective-permute-start.10) | collective-permute-done | bytes 1310752 | tf_op jit(solution)/shard_map/ppermute | solution.py:23
  112.6 4.5 %project_far.1 = (bf16[16,64,640]{2,1,0:T(8,128)(2,1)S(1)}, bf16[16,64,256]{2,1,0:T(8,128)(2,1)S(1)}) custom-call(s32[16]{0:T(128)S(1)} %get-tuple-element.148.refs_0_, bf16[512,1280]{1,0:T(8,128)(2,1)S(1)} %collective-permute-done.10.refs_1_, bf16[512,1280]{1,0:T(8,128)(2,1)S(1)} %collective-permute-done.11.refs_2_, ...), custom_call_target="tpu_custom_call" | custom-call | flops 1024 | bytes 1024 | tf_op jit(solution)/shard_map/project_far/pallas_call | solution.py:125
  117.1 26.9 %all_to_all.32.refs_3_.refs_4_ = bf16[16,64,640]{2,1,0:T(8,128)(2,1)S(1)} all-to-all(bf16[16,64,640]{2,1,0:T(8,128)(2,1)S(1)} %get-tuple-element.89), channel_id=1, replica_groups=mesh['z'=4,'xh'=2,'core'=2,'context'=2,'tensor'=4] {'z','xh','core'}, dimensions={0} | all-to-all | bytes 2621440 | tf_op jit(solution)/shard_map/all_to_all | solution.py:498
  145.3 3.6 %all-to-all-start.3 = ((bf16[16,64,256]{2,1,0:T(8,128)(2,1)}), bf16[16,64,256]{2,1,0:T(8,128)(2,1)S(1)}, u32[]{:S(2)}, u32[]{:S(2)}) async-start(bf16[16,64,256]{2,1,0:T(8,128)(2,1)} %copy-done.6), calls=%async_computation.3 | async-start | bytes 1048576 | tf_op jit(solution)/shard_map/all_to_all | solution.py:498
  148.9 7.1 %attend.3 = (f32[4,1,768]{2,1,0:T(1,128)S(1)}, f32[4,1,768]{2,1,0:T(1,128)S(1)}, f32[4,128,768]{2,1,0:T(8,128)S(1)}) custom-call(s32[32]{0:T(128)S(1)} %pad_add_fusion.1.refs_0_, s32[32]{0:T(128)S(1)} %pad_add_fusion.2.refs_1_, s32[1]{0:T(128)} %bitcast.24.refs_2_, bf16[16,64,640]{2,1,0:T(8,128)(2,1)S(1)} %all_to_all.32.refs_3_.refs_4_, ...), custom_call_target="tpu_custom_call" | custom-call | flops 1024 | bytes 1024 | tf_op jit(solution)/shard_map/attend/pallas_call | solution.py:275
  156.1 4.7 %collective-permute-done.18.refs_5_ = bf16[16,64,256]{2,1,0:T(8,128)(2,1)S(1)} collective-permute-done((bf16[16,64,256]{2,1,0:T(8,128)(2,1)S(1)}, bf16[16,64,256]{2,1,0:T(8,128)(2,1)S(1)}, u32[]{:S(2)}, u32[]{:S(2)}) %collective-permute-start.18) | collective-permute-done | bytes 524320 | tf_op jit(solution)/shard_map/ppermute | solution.py:501
  160.8 8.1 %attend.4 = bf16[16,64,384]{2,1,0:T(8,128)(2,1)} custom-call(s32[32]{0:T(128)S(1)} %pad_add_fusion.1.refs_0_, s32[32]{0:T(128)S(1)} %pad_add_fusion.2.refs_1_, s32[1]{0:T(128)} %bitcast.24.refs_2_, bf16[16,64,640]{2,1,0:T(8,128)(2,1)S(1)} %all_to_all.32.refs_3_.refs_4_, bf16[16,64,640]{2,1,0:T(8,128)(2,1)S(1)} %all_to_all.32.refs_3_.refs_4_, ...), custom_call_target="tpu_custom_call" | custom-call | flops 1024 | bytes 1024 | tf_op jit(solution)/shard_map/attend/pallas_call | solution.py:275
  168.9 3.8 %all-to-all-start.2 = ((bf16[16,64,384]{2,1,0:T(8,128)(2,1)}), bf16[16,64,384]{2,1,0:T(8,128)(2,1)S(1)}, u32[]{:S(2)}, u32[]{:S(2)}) async-start(bf16[16,64,384]{2,1,0:T(8,128)(2,1)} %attend.4), calls=%async_computation.2 | async-start | bytes 1572864 | tf_op jit(solution)/shard_map/all_to_all | solution.py:498
  172.7 11.4 %attend.5 = bf16[16,64,256]{2,1,0:T(8,128)(2,1)} custom-call(s32[32]{0:T(128)S(1)} %pad_add_fusion.1.refs_0_, s32[32]{0:T(128)S(1)} %pad_add_fusion.2.refs_1_, s32[1]{0:T(128)} %bitcast.24.refs_2_, bf16[16,64,256]{2,1,0:T(8,128)(2,1)S(1)} %all-to-all-done.3.refs_3_, bf16[16,64,640]{2,1,0:T(8,128)(2,1)S(1)} %all_to_all.32.refs_3_.refs_4_, ...), custom_call_target="tpu_custom_call" | custom-call | flops 1024 | bytes 1024 | tf_op jit(solution)/shard_map/attend/pallas_call | solution.py:275
  184.2 3.7 %all-to-all-done.2 = bf16[16,64,384]{2,1,0:T(8,128)(2,1)S(1)} async-done(((bf16[16,64,384]{2,1,0:T(8,128)(2,1)}), bf16[16,64,384]{2,1,0:T(8,128)(2,1)S(1)}, u32[]{:S(2)}, u32[]{:S(2)}) %all-to-all-start.2) | async-done | bytes 786464 | tf_op jit(solution)/shard_map/all_to_all | solution.py:498
  189.9 3.6 %all-to-all-start.4 = ((bf16[16,64,256]{2,1,0:T(8,128)(2,1)}), bf16[16,64,256]{2,1,0:T(8,128)(2,1)S(1)}, u32[]{:S(2)}, u32[]{:S(2)}) async-start(bf16[16,64,256]{2,1,0:T(8,128)(2,1)} %attend.5), calls=%async_computation.4 | async-start | bytes 1048576 | tf_op jit(solution)/shard_map/all_to_all | solution.py:498
  194.2 5.0 %place_shares.1.refs_7_.refs_3_ = bf16[8,2,3,80,640]{4,3,2,1,0:T(8,128)(2,1)} custom-call(s32[2]{0:T(128)} %pad_add_fusion.3.where, bf16[4,3,80,640]{3,2,1,0:T(8,128)(2,1)} %copy-done.7, bf16[4,3,80,640]{3,2,1,0:T(8,128)(2,1)} %copy-done.9, bf16[4,3,80,640]{3,2,1,0:T(8,128)(2,1)} %copy-done.8, bf16[2,3,80,640]{3,2,1,0:T(8,128)(2,1)} %copy-done.14, ...), custom_call_target="tpu_custom_call" | custom-call | flops 1024 | bytes 1024 | tf_op jit(solution)/shard_map/place_shares/pallas_call | solution.py:457
  199.2 6.7 %all-to-all-done.4 = bf16[16,64,256]{2,1,0:T(8,128)(2,1)S(1)} async-done(((bf16[16,64,256]{2,1,0:T(8,128)(2,1)}), bf16[16,64,256]{2,1,0:T(8,128)(2,1)S(1)}, u32[]{:S(2)}, u32[]{:S(2)}) %all-to-all-start.4) | async-done | bytes 524320 | tf_op jit(solution)/shard_map/all_to_all | solution.py:498
  212.4 2.4 copy-done
  214.8 8.6 %mix_near.2.refs_8_ = f32[1024,1280]{1,0:T(8,128)S(1)} custom-call(s32[16]{0:T(128)S(1)} %select_reduce_fusion.4.refs_0_, s32[1]{0:T(128)} %bitcast.29.refs_1_, bf16[1024,384]{1,0:T(8,128)(2,1)S(1)} %bitcast.45, bf16[1024,384]{1,0:T(8,128)(2,1)S(1)} %collective-permute-done.19.refs_3_, bf16[1024,384]{1,0:T(8,128)(2,1)S(1)} %collective-permute-done.20.refs_4_, ...), custom_call_target="tpu_custom_call" | custom-call | flops 1024 | bytes 1024 | tf_op jit(solution)/shard_map/mix_near/pallas_call | solution.py:364
  225.7 3.2 %collective-permute-done.24.refs_3_ = bf16[512,384]{1,0:T(8,128)(2,1)S(1)} collective-permute-done((bf16[512,384]{1,0:T(8,128)(2,1)S(1)}, bf16[512,384]{1,0:T(8,128)(2,1)S(1)}, u32[]{:S(2)}, u32[]{:S(2)}) %collective-permute-start.24) | collective-permute-done | bytes 393248 | tf_op jit(solution)/shard_map/ppermute | solution.py:27
  230.7 3.0 %collective-permute-start.26 = (bf16[512,256]{1,0:T(8,128)(2,1)S(1)}, bf16[512,256]{1,0:T(8,128)(2,1)S(1)}, u32[]{:S(2)}, u32[]{:S(2)}) collective-permute-start(bf16[512,256]{1,0:T(8,128)(2,1)S(1)} %slice.63), channel_id=1, source_target_pairs={{0,3},{1,0},{2,1},{3,2},{4,7},{5,4},{6,5},{7,6},{8,11},{9,8},{10,9... | collective-permute-start | bytes 786440 | tf_op jit(solution)/shard_map/ppermute | solution.py:27
  233.7 7.3 %mix_near.3.refs_4_ = f32[1024,1280]{1,0:T(8,128)S(1)} custom-call(s32[16]{0:T(128)S(1)} %select_reduce_fusion.4.refs_0_, s32[1]{0:T(128)} %bitcast.29.refs_1_, bf16[512,384]{1,0:T(8,128)(2,1)S(1)} %collective-permute-done.23.refs_2_, bf16[512,384]{1,0:T(8,128)(2,1)S(1)} %collective-permute-done.24.refs_3_, ...), custom_call_target="tpu_custom_call" | custom-call | flops 1024 | bytes 1024 | tf_op jit(solution)/shard_map/mix_near/pallas_call | solution.py:364
  241.1 4.3 %mix_far.1 = bf16[16,64,1280]{2,1,0:T(8,128)(2,1)} custom-call(s32[16]{0:T(128)S(1)} %select_reduce_fusion.4.refs_0_, bf16[512,256]{1,0:T(8,128)(2,1)S(1)} %collective-permute-done.25.refs_1_, bf16[512,256]{1,0:T(8,128)(2,1)S(1)} %collective-permute-done.26.refs_2_, bf16[8,2,3,80,640]{4,3,2,1,0:T(8,128)(2,1)S(1)} %copy-done, f32[1024,1280]{1,0:T(8,128)S(1)} %mix_near.3.refs_4_), custom_call_target="tpu_custom_call" | custom-call | flops 1024 | bytes 1024 | tf_op jit(solution)/shard_map/mix_far/pallas_call | solution.py:404
  (127 shorter events, 43.2 us)
Async XLA Ops:
  3.0 12.0 %collective-permute-start.2 = (bf16[80,640]{1,0:T(8,128)(2,1)}, bf16[80,640]{1,0:T(8,128)(2,1)S(1)}, u32[]{:S(2)}, u32[]{:S(2)}) collective-permute-start(bf16[80,640]{1,0:T(8,128)(2,1)} %get-tuple-element.130), channel_id=1, source_target_pairs={{0,2},{1,3},{2,0},{3,1},{4,6},{5,7},{6,4},{7,5},{8,10},{9,11},{10,... | collective-permute-start | bytes 307208 | tf_op jit(solution)/shard_map/ppermute | solution.py:440
  6.2 8.8 %collective-permute-start = (bf16[80,640]{1,0:T(8,128)(2,1)}, bf16[80,640]{1,0:T(8,128)(2,1)S(1)}, u32[]{:S(2)}, u32[]{:S(2)}) collective-permute-start(bf16[80,640]{1,0:T(8,128)(2,1)} %get-tuple-element.131), channel_id=1, source_target_pairs={{0,1},{1,2},{2,3},{3,0},{4,5},{5,6},{6,7},{7,4},{8,9},{9,10},{10,1... | collective-permute-start | bytes 307208 | tf_op jit(solution)/shard_map/ppermute | solution.py:23
  6.8 8.2 %collective-permute-start.1 = (bf16[80,640]{1,0:T(8,128)(2,1)S(1)}, bf16[80,640]{1,0:T(8,128)(2,1)S(1)}, u32[]{:S(2)}, u32[]{:S(2)}) collective-permute-start(bf16[80,640]{1,0:T(8,128)(2,1)S(1)} %get-tuple-element.132), channel_id=1, source_target_pairs={{0,3},{1,0},{2,1},{3,2},{4,7},{5,4},{6,5},{7,6},{8,11},{9,8},{10,9... | collective-permute-start | bytes 307208 | tf_op jit(solution)/shard_map/ppermute | solution.py:27
  15.1 27.8 %collective-permute-start.6 = (bf16[3,80,640]{2,1,0:T(8,128)(2,1)S(1)}, bf16[3,80,640]{2,1,0:T(8,128)(2,1)S(1)}, u32[]{:S(2)}, u32[]{:S(2)}) collective-permute-start(bf16[3,80,640]{2,1,0:T(8,128)(2,1)S(1)} %get-tuple-element.134), channel_id=1, source_target_pairs={{0,4},{4,16},{16,20},{20,0},{1,5},{5,17},{17,21},{21,1},{2,6},{6,1... | collective-permute-start | bytes 921608 | tf_op jit(solution)/shard_map/ppermute | solution.py:23
  16.6 28.0 %collective-permute-start.7 = (bf16[3,80,640]{2,1,0:T(8,128)(2,1)S(1)}, bf16[3,80,640]{2,1,0:T(8,128)(2,1)S(1)}, u32[]{:S(2)}, u32[]{:S(2)}) collective-permute-start(bf16[3,80,640]{2,1,0:T(8,128)(2,1)S(1)} %get-tuple-element.134), channel_id=1, source_target_pairs={{0,20},{4,0},{16,4},{20,16},{1,21},{5,1},{17,5},{21,17},{2,22},{6,... | collective-permute-start | bytes 921608 | tf_op jit(solution)/shard_map/ppermute | solution.py:27
  17.2 35.0 %collective-permute-start.3 = (bf16[512,1280]{1,0:T(8,128)(2,1)}, bf16[512,1280]{1,0:T(8,128)(2,1)}, u32[]{:S(2)}, u32[]{:S(2)}) collective-permute-start(bf16[512,1280]{1,0:T(8,128)(2,1)} %get-tuple-element.64.refs_0_), channel_id=1, source_target_pairs={{0,1},{1,2},{2,3},{3,0},{4,5},{5,6},{6,7},{7,4},{8,9},{9,10},{10,1... | collective-permute-start | bytes 3932168 | tf_op jit(solution)/shard_map/ppermute | solution.py:23
  17.2 35.0 %collective-permute-start.4 = (bf16[512,1280]{1,0:T(8,128)(2,1)}, bf16[512,1280]{1,0:T(8,128)(2,1)}, u32[]{:S(2)}, u32[]{:S(2)}) collective-permute-start(bf16[512,1280]{1,0:T(8,128)(2,1)} %get-tuple-element.65.refs_1_), channel_id=1, source_target_pairs={{0,3},{1,0},{2,1},{3,2},{4,7},{5,4},{6,5},{7,6},{8,11},{9,8},{10,9... | collective-permute-start | bytes 3932168 | tf_op jit(solution)/shard_map/ppermute | solution.py:27
  21.1 16.0 %all-to-all-start = ((s32[16,1,2]{2,1,0:T(1,128)}), s32[16,1,2]{2,1,0:T(1,128)S(1)}, u32[]{:S(2)}, u32[]{:S(2)}) async-start(s32[16,1,2]{2,1,0:T(1,128)} %copy.14), calls=%async_computation | async-start | bytes 16384 | tf_op jit(solution)/shard_map/all_to_all | solution.py:498
  37.2 5.5 %collective-permute-start.5 = (s32[16,2]{0,1:T(2,128)S(1)}, s32[16,2]{0,1:T(2,128)S(1)}, u32[]{:S(2)}, u32[]{:S(2)}) collective-permute-start(s32[16,2]{0,1:T(2,128)S(1)} %bitcast.55), channel_id=1, source_target_pairs={{0,4},{1,5},{2,6},{3,7},{8,12},{9,13},{10,14},{11,15},{16,20},{17,... | collective-permute-start | bytes 392 | tf_op jit(solution)/shard_map/ppermute | solution.py:501
  42.7 32.5 %collective-permute-start.13 = (bf16[512,1280]{1,0:T(8,128)(2,1)}, bf16[512,1280]{1,0:T(8,128)(2,1)}, u32[]{:S(2)}, u32[]{:S(2)}) collective-permute-start(bf16[512,1280]{1,0:T(8,128)(2,1)} %get-tuple-element.64.refs_0_), channel_id=1, source_target_pairs={{0,3},{1,0},{2,1},{3,2},{4,7},{5,4},{6,5},{7,6},{8,11},{9,8},{10,9... | collective-permute-start | bytes 3932168 | tf_op jit(solution)/shard_map/ppermute | solution.py:27
  42.9 9.0 %collective-permute-start.8 = (bf16[3,48,640]{2,1,0:T(8,128)(2,1)S(1)}, bf16[3,48,640]{2,1,0:T(8,128)(2,1)S(1)}, u32[]{:S(2)}, u32[]{:S(2)}) collective-permute-start(bf16[3,48,640]{2,1,0:T(8,128)(2,1)S(1)} %slice.68), channel_id=1, source_target_pairs={{0,4},{4,16},{16,20},{20,0},{1,5},{5,17},{17,21},{21,1},{2,6},{6,1... | collective-permute-start | bytes 552968 | tf_op jit(solution)/shard_map/ppermute | solution.py:23
  44.7 5.2 %collective-permute-start.9 = (bf16[3,32,640]{2,1,0:T(8,128)(2,1)S(1)}, bf16[3,32,640]{2,1,0:T(8,128)(2,1)S(1)}, u32[]{:S(2)}, u32[]{:S(2)}) collective-permute-start(bf16[3,32,640]{2,1,0:T(8,128)(2,1)S(1)} %slice.69), channel_id=1, source_target_pairs={{0,20},{4,0},{16,4},{20,16},{1,21},{5,1},{17,5},{21,17},{2,22},{6,... | collective-permute-start | bytes 368648 | tf_op jit(solution)/shard_map/ppermute | solution.py:27
  49.9 33.1 %collective-permute-start.12 = (bf16[512,1280]{1,0:T(8,128)(2,1)}, bf16[512,1280]{1,0:T(8,128)(2,1)S(1)}, u32[]{:S(2)}, u32[]{:S(2)}) collective-permute-start(bf16[512,1280]{1,0:T(8,128)(2,1)} %get-tuple-element.65.refs_1_), channel_id=1, source_target_pairs={{0,1},{1,2},{2,3},{3,0},{4,5},{5,6},{6,7},{7,4},{8,9},{9,10},{10,1... | collective-permute-start | bytes 3932168 | tf_op jit(solution)/shard_map/ppermute | solution.py:23
  52.0 34.9 %copy-start.16 = (bf16[128]{0:T(256)(128)(2,1)S(1)}, bf16[128]{0:T(256)(128)(2,1)}, u32[]{:S(2)}) copy-start(bf16[128]{0:T(256)(128)(2,1)} %param.20) | copy-start | bytes 772
  52.2 30.8 %collective-permute-start.15 = (bf16[4,3,80,640]{3,2,1,0:T(8,128)(2,1)S(1)}, bf16[4,3,80,640]{3,2,1,0:T(8,128)(2,1)S(1)}, u32[]{:S(2)}, u32[]{:S(2)}) collective-permute-start(bf16[4,3,80,640]{3,2,1,0:T(8,128)(2,1)S(1)} %pad_maximum_fusion.4.refs_0_), channel_id=1, source_target_pairs={{0,96},{32,0},{64,32},{96,64},{1,97},{33,1},{65,33},{97,65},{2,98}... | collective-permute-start | bytes 3686408 | tf_op jit(solution)/shard_map/ppermute | solution.py:27
  54.9 28.1 %collective-permute-start.14 = (bf16[4,3,80,640]{3,2,1,0:T(8,128)(2,1)S(1)}, bf16[4,3,80,640]{3,2,1,0:T(8,128)(2,1)S(1)}, u32[]{:S(2)}, u32[]{:S(2)}) collective-permute-start(bf16[4,3,80,640]{3,2,1,0:T(8,128)(2,1)S(1)} %pad_maximum_fusion.4.refs_0_), channel_id=1, source_target_pairs={{0,32},{32,64},{64,96},{96,0},{1,33},{33,65},{65,97},{97,1},{2,34}... | collective-permute-start | bytes 3686408 | tf_op jit(solution)/shard_map/ppermute | solution.py:23
  54.9 53.8 %collective-permute-start.10 = (bf16[512,1280]{1,0:T(8,128)(2,1)}, bf16[512,1280]{1,0:T(8,128)(2,1)S(1)}, u32[]{:S(2)}, u32[]{:S(2)}) collective-permute-start(bf16[512,1280]{1,0:T(8,128)(2,1)} %collective-permute-done.3.refs_2_), channel_id=1, source_target_pairs={{0,1},{1,2},{2,3},{3,0},{4,5},{5,6},{6,7},{7,4},{8,9},{9,10},{10,1... | collective-permute-start | bytes 3932168 | tf_op jit(solution)/shard_map/ppermute | solution.py:23
  75.2 33.5 %collective-permute-start.11 = (bf16[512,1280]{1,0:T(8,128)(2,1)}, bf16[512,1280]{1,0:T(8,128)(2,1)S(1)}, u32[]{:S(2)}, u32[]{:S(2)}) collective-permute-start(bf16[512,1280]{1,0:T(8,128)(2,1)} %collective-permute-done.4.refs_5_), channel_id=1, source_target_pairs={{0,3},{1,0},{2,1},{3,2},{4,7},{5,4},{6,5},{7,6},{8,11},{9,8},{10,9... | collective-permute-start | bytes 3932168 | tf_op jit(solution)/shard_map/ppermute | solution.py:27
  84.1 24.6 %collective-permute-start.17 = (bf16[2,3,80,640]{3,2,1,0:T(8,128)(2,1)}, bf16[2,3,80,640]{3,2,1,0:T(8,128)(2,1)S(1)}, u32[]{:S(2)}, u32[]{:S(2)}) collective-permute-start(bf16[2,3,80,640]{3,2,1,0:T(8,128)(2,1)} %slice.58), channel_id=1, source_target_pairs={{0,96},{32,0},{64,32},{96,64},{1,97},{33,1},{65,33},{97,65},{2,98}... | collective-permute-start | bytes 1843208 | tf_op jit(solution)/shard_map/ppermute | solution.py:27
  86.8 21.9 %collective-permute-start.16 = (bf16[2,3,80,640]{3,2,1,0:T(8,128)(2,1)S(1)}, bf16[2,3,80,640]{3,2,1,0:T(8,128)(2,1)S(1)}, u32[]{:S(2)}, u32[]{:S(2)}) collective-permute-start(bf16[2,3,80,640]{3,2,1,0:T(8,128)(2,1)S(1)} %slice.57), channel_id=1, source_target_pairs={{0,32},{32,64},{64,96},{96,0},{1,33},{33,65},{65,97},{97,1},{2,34}... | collective-permute-start | bytes 1843208 | tf_op jit(solution)/shard_map/ppermute | solution.py:23
  144.0 16.8 %collective-permute-start.18 = (bf16[16,64,256]{2,1,0:T(8,128)(2,1)S(1)}, bf16[16,64,256]{2,1,0:T(8,128)(2,1)S(1)}, u32[]{:S(2)}, u32[]{:S(2)}) collective-permute-start(bf16[16,64,256]{2,1,0:T(8,128)(2,1)S(1)} %slice.70), channel_id=1, source_target_pairs={{0,4},{1,5},{2,6},{3,7},{8,12},{9,13},{10,14},{11,15},{16,20},{17,... | collective-permute-start | bytes 1572872 | tf_op jit(solution)/shard_map/ppermute | solution.py:501
  145.3 23.5 %all-to-all-start.3 = ((bf16[16,64,256]{2,1,0:T(8,128)(2,1)}), bf16[16,64,256]{2,1,0:T(8,128)(2,1)S(1)}, u32[]{:S(2)}, u32[]{:S(2)}) async-start(bf16[16,64,256]{2,1,0:T(8,128)(2,1)} %copy-done.6), calls=%async_computation.3 | async-start | bytes 1048576 | tf_op jit(solution)/shard_map/all_to_all | solution.py:498
  168.9 19.0 %all-to-all-start.2 = ((bf16[16,64,384]{2,1,0:T(8,128)(2,1)}), bf16[16,64,384]{2,1,0:T(8,128)(2,1)S(1)}, u32[]{:S(2)}, u32[]{:S(2)}) async-start(bf16[16,64,384]{2,1,0:T(8,128)(2,1)} %attend.4), calls=%async_computation.2 | async-start | bytes 1572864 | tf_op jit(solution)/shard_map/all_to_all | solution.py:498
  187.9 19.0 %collective-permute-start.20 = (bf16[1024,384]{1,0:T(8,128)(2,1)S(1)}, bf16[1024,384]{1,0:T(8,128)(2,1)S(1)}, u32[]{:S(2)}, u32[]{:S(2)}) collective-permute-start(bf16[1024,384]{1,0:T(8,128)(2,1)S(1)} %bitcast.43), channel_id=1, source_target_pairs={{0,3},{1,0},{2,1},{3,2},{4,7},{5,4},{6,5},{7,6},{8,11},{9,8},{10,9... | collective-permute-start | bytes 2359304 | tf_op jit(solution)/shard_map/ppermute | solution.py:27
  188.1 20.0 %collective-permute-start.19 = (bf16[1024,384]{1,0:T(8,128)(2,1)S(1)}, bf16[1024,384]{1,0:T(8,128)(2,1)S(1)}, u32[]{:S(2)}, u32[]{:S(2)}) collective-permute-start(bf16[1024,384]{1,0:T(8,128)(2,1)S(1)} %bitcast.44), channel_id=1, source_target_pairs={{0,1},{1,2},{2,3},{3,0},{4,5},{5,6},{6,7},{7,4},{8,9},{9,10},{10,1... | collective-permute-start | bytes 2359304 | tf_op jit(solution)/shard_map/ppermute | solution.py:23
  189.9 15.9 %all-to-all-start.4 = ((bf16[16,64,256]{2,1,0:T(8,128)(2,1)}), bf16[16,64,256]{2,1,0:T(8,128)(2,1)S(1)}, u32[]{:S(2)}, u32[]{:S(2)}) async-start(bf16[16,64,256]{2,1,0:T(8,128)(2,1)} %attend.5), calls=%async_computation.4 | async-start | bytes 1048576 | tf_op jit(solution)/shard_map/all_to_all | solution.py:498
  208.2 22.2 %collective-permute-start.22 = (bf16[1024,256]{1,0:T(8,128)(2,1)S(1)}, bf16[1024,256]{1,0:T(8,128)(2,1)S(1)}, u32[]{:S(2)}, u32[]{:S(2)}) collective-permute-start(bf16[1024,256]{1,0:T(8,128)(2,1)S(1)} %bitcast.46), channel_id=1, source_target_pairs={{0,3},{1,0},{2,1},{3,2},{4,7},{5,4},{6,5},{7,6},{8,11},{9,8},{10,9... | collective-permute-start | bytes 1572872 | tf_op jit(solution)/shard_map/ppermute | solution.py:27
  208.4 21.9 %collective-permute-start.21 = (bf16[1024,256]{1,0:T(8,128)(2,1)S(1)}, bf16[1024,256]{1,0:T(8,128)(2,1)S(1)}, u32[]{:S(2)}, u32[]{:S(2)}) collective-permute-start(bf16[1024,256]{1,0:T(8,128)(2,1)S(1)} %bitcast.47), channel_id=1, source_target_pairs={{0,1},{1,2},{2,3},{3,0},{4,5},{5,6},{6,7},{7,4},{8,9},{9,10},{10,1... | collective-permute-start | bytes 1572872 | tf_op jit(solution)/shard_map/ppermute | solution.py:23
  210.3 18.6 %collective-permute-start.24 = (bf16[512,384]{1,0:T(8,128)(2,1)S(1)}, bf16[512,384]{1,0:T(8,128)(2,1)S(1)}, u32[]{:S(2)}, u32[]{:S(2)}) collective-permute-start(bf16[512,384]{1,0:T(8,128)(2,1)S(1)} %slice.61), channel_id=1, source_target_pairs={{0,3},{1,0},{2,1},{3,2},{4,7},{5,4},{6,5},{7,6},{8,11},{9,8},{10,9... | collective-permute-start | bytes 1179656 | tf_op jit(solution)/shard_map/ppermute | solution.py:27
  211.8 18.5 %collective-permute-start.23 = (bf16[512,384]{1,0:T(8,128)(2,1)S(1)}, bf16[512,384]{1,0:T(8,128)(2,1)S(1)}, u32[]{:S(2)}, u32[]{:S(2)}) collective-permute-start(bf16[512,384]{1,0:T(8,128)(2,1)S(1)} %slice.60), channel_id=1, source_target_pairs={{0,1},{1,2},{2,3},{3,0},{4,5},{5,6},{6,7},{7,4},{8,9},{9,10},{10,1... | collective-permute-start | bytes 1179656 | tf_op jit(solution)/shard_map/ppermute | solution.py:23
  230.4 10.7 %collective-permute-start.25 = (bf16[512,256]{1,0:T(8,128)(2,1)S(1)}, bf16[512,256]{1,0:T(8,128)(2,1)S(1)}, u32[]{:S(2)}, u32[]{:S(2)}) collective-permute-start(bf16[512,256]{1,0:T(8,128)(2,1)S(1)} %slice.62), channel_id=1, source_target_pairs={{0,1},{1,2},{2,3},{3,0},{4,5},{5,6},{6,7},{7,4},{8,9},{9,10},{10,1... | collective-permute-start | bytes 786440 | tf_op jit(solution)/shard_map/ppermute | solution.py:23
  230.7 10.4 %collective-permute-start.26 = (bf16[512,256]{1,0:T(8,128)(2,1)S(1)}, bf16[512,256]{1,0:T(8,128)(2,1)S(1)}, u32[]{:S(2)}, u32[]{:S(2)}) collective-permute-start(bf16[512,256]{1,0:T(8,128)(2,1)S(1)} %slice.63), channel_id=1, source_target_pairs={{0,3},{1,0},{2,1},{3,2},{4,7},{5,4},{6,5},{7,6},{8,11},{9,8},{10,9... | collective-permute-start | bytes 786440 | tf_op jit(solution)/shard_map/ppermute | solution.py:27
  (17 other events, 175.4 us)

commit v5 on v4

--- a/solution.py
+++ b/solution.py
@@ -561,12 +561,12 @@
     far = ring_far(left[:half], right[half:])
     steps = [(0, bands[0]), (1, bands[0]), (2, bands[0]), (0, bands[1])]
     pieces = [(flat_a,), (left,), (right,), (flat_b,)]
-    total = mix_near(page_of, here, pieces, steps, w_out, w_all)
+    total = mix_near(page_of, here, pieces, steps, w_out, w_all, None, paged)
     left, right = to_right(flat_b), to_left(flat_b)
     left, right, far, total = hold((left, right, far, total))
     last = ring_far(left[:half], right[half:])
     steps = [(3, bands[0]), (1, bands[1]), (2, bands[1])]
-    total = mix_near(page_of, here, [far, (left,), (right,)], steps, w_out, w_all, total, paged)
+    total = mix_near(page_of, here, [far, (left,), (right,)], steps, w_out, w_all, total)
     result = mix_far(page_of, *last, bands[1], w_all, total)
     return result.reshape(hidden.shape)
 

time: 246 us -> 246 us (level)
    unnamed x36 -> x32, local copies, waits for them, and re-layouts: 8.68 us -> 6.39 us
  transfers between devices with their start and end apart: 31 -> 31, of which waited for: 12 -> 12; matrix products, arithmetic and copies ran while one was open for 7% -> 8% of each run, Pallas kernels for 26% -> 26%
where the time goes in v5:
time: 246 us
  Pallas kernels  73.4 us (30%)
  waiting for transfers between devices  60.4 us (25%)
  starting transfers between devices  55.7 us (23%)
  blocking collectives  26.8 us (11%)
  local copies, waits for them, and re-layouts  21.2 us (9%)
  other arithmetic  7.8 us (3%)
    ppermute x12, waiting for transfers between devices, to_left(): return lax.ppermute(block, axis, [(i, (i - 1) % RING) for i in range(RING)])  28.9 us
    all_to_all x1, blocking collectives, exchange(): return lax.all_to_all(rows, DP, split_axis=0, concat_axis=0, tiled=True)  26.8 us
    pallas_call x3, Pallas kernels, attend(): pl.pallas_call(kernel, out_shape=out_shape, in_specs=[smem] * 3 + [vmem]...  26.7 us
    ppermute x12, starting transfers between devices, to_left(): return lax.ppermute(block, axis, [(i, (i - 1) % RING) for i in range(RING)])  20.9 us
    all_to_all x4, starting transfers between devices, exchange(): return lax.all_to_all(rows, DP, split_axis=0, concat_axis=0, tiled=True)  18.6 us
    pallas_call x1, Pallas kernels, project_near(): pl.pallas_call(kernel, out_shape=[jax.ShapeDtypeStruct(shape, jnp.float32...  16.4 us
    pallas_call x2, Pallas kernels, mix_near(): pl.pallas_call(kernel, out_shape=jax.ShapeDtypeStruct((2 * half, cuts * c...  15.6 us
    ppermute x12, waiting for transfers between devices, to_right(): return lax.ppermute(block, axis, [(i, (i + 1) % RING) for i in range(RING)])  12.4 us
  transfers between devices with their start and end apart: 31, of which 12 were waited for; matrix products, arithmetic and copies ran while one was open for 8% of the time, Pallas kernels for 26%

profile of v5, /device:TPU:2, one launch (start us, length us, event | category | flops | bytes accessed | tf_op | source)
XLA Modules:
  0.0 246.0 jit_solution(8353001892398868163)
XLA Ops:
  3.0 3.2 %collective-permute-start.2 = (bf16[80,640]{1,0:T(8,128)(2,1)}, bf16[80,640]{1,0:T(8,128)(2,1)S(1)}, u32[]{:S(2)}, u32[]{:S(2)}) collective-permute-start(bf16[80,640]{1,0:T(8,128)(2,1)} %get-tuple-element.130), channel_id=1, source_target_pairs={{0,2},{1,3},{2,0},{3,1},{4,6},{5,7},{6,4},{7,5},{8,10},{9,11},{10,... | collective-permute-start | bytes 307208 | tf_op jit(solution)/shard_map/ppermute | solution.py:440
  6.8 2.6 %collective-permute-start.1 = (bf16[80,640]{1,0:T(8,128)(2,1)S(1)}, bf16[80,640]{1,0:T(8,128)(2,1)S(1)}, u32[]{:S(2)}, u32[]{:S(2)}) collective-permute-start(bf16[80,640]{1,0:T(8,128)(2,1)S(1)} %get-tuple-element.132), channel_id=1, source_target_pairs={{0,3},{1,0},{2,1},{3,2},{4,7},{5,4},{6,5},{7,6},{8,11},{9,8},{10,9... | collective-permute-start | bytes 307208 | tf_op jit(solution)/shard_map/ppermute | solution.py:27
  17.2 3.2 %collective-permute-start.4 = (bf16[512,1280]{1,0:T(8,128)(2,1)}, bf16[512,1280]{1,0:T(8,128)(2,1)}, u32[]{:S(2)}, u32[]{:S(2)}) collective-permute-start(bf16[512,1280]{1,0:T(8,128)(2,1)} %get-tuple-element.65.refs_1_), channel_id=1, source_target_pairs={{0,3},{1,0},{2,1},{3,2},{4,7},{5,4},{6,5},{7,6},{8,11},{9,8},{10,9... | collective-permute-start | bytes 3932168 | tf_op jit(solution)/shard_map/ppermute | solution.py:27
  21.1 7.0 %all-to-all-start = ((s32[16,1,2]{2,1,0:T(1,128)}), s32[16,1,2]{2,1,0:T(1,128)S(1)}, u32[]{:S(2)}, u32[]{:S(2)}) async-start(s32[16,1,2]{2,1,0:T(1,128)} %copy.14), calls=%async_computation | async-start | bytes 16384 | tf_op jit(solution)/shard_map/all_to_all | solution.py:498
  28.1 3.6 %constant_dynamic-slice_fusion = (bf16[1280,640]{1,0:T(8,128)(2,1)S(1)}, bf16[1280,640]{1,0:T(8,128)(2,1)S(1)}, bf16[1280,640]{1,0:T(8,128)(2,1)S(1)}, bf16[1280,640]{1,0:T(8,128)(2,1)S(1)}) fusion(bf16[5120,640]{1,0:T(8,128)(2,1)} %param.16, s32[]{:T(128)S(6)} %select_n.114, s32[]{:T(128)S(6)} %select_n.113, s32[]{:T(128)S(6)} %select_n.112, s32[]{:T(128)S(6)} %select_n.111), kind=kLoop, calls=%fused_computation.27 | loop fusion | bytes 13107216 | tf_op jit(solution)/shard_map/dynamic_slice | solution.py:493
  38.5 4.2 %collective-permute-done.5 = s32[16,2]{0,1:T(2,128)S(1)} collective-permute-done((s32[16,2]{0,1:T(2,128)S(1)}, s32[16,2]{0,1:T(2,128)S(1)}, u32[]{:S(2)}, u32[]{:S(2)}) %collective-permute-start.5) | collective-permute-done | bytes 160 | tf_op jit(solution)/shard_map/ppermute | solution.py:501
  45.2 4.7 %collective-permute-done.9 = bf16[3,32,640]{2,1,0:T(8,128)(2,1)S(1)} collective-permute-done((bf16[3,32,640]{2,1,0:T(8,128)(2,1)S(1)}, bf16[3,32,640]{2,1,0:T(8,128)(2,1)S(1)}, u32[]{:S(2)}, u32[]{:S(2)}) %collective-permute-start.9) | collective-permute-done | bytes 122912 | tf_op jit(solution)/shard_map/ppermute | solution.py:27
  52.2 2.7 %collective-permute-start.15 = (bf16[4,3,80,640]{3,2,1,0:T(8,128)(2,1)S(1)}, bf16[4,3,80,640]{3,2,1,0:T(8,128)(2,1)S(1)}, u32[]{:S(2)}, u32[]{:S(2)}) collective-permute-start(bf16[4,3,80,640]{3,2,1,0:T(8,128)(2,1)S(1)} %pad_maximum_fusion.4.refs_0_), channel_id=1, source_target_pairs={{0,96},{32,0},{64,32},{96,64},{1,97},{33,1},{65,33},{97,65},{2,98}... | collective-permute-start | bytes 3686408 | tf_op jit(solution)/shard_map/ppermute | solution.py:27
  54.9 20.2 %collective-permute-done.13.refs_4_ = bf16[512,1280]{1,0:T(8,128)(2,1)} collective-permute-done((bf16[512,1280]{1,0:T(8,128)(2,1)}, bf16[512,1280]{1,0:T(8,128)(2,1)}, u32[]{:S(2)}, u32[]{:S(2)}) %collective-permute-start.13) | collective-permute-done | bytes 1310752 | tf_op jit(solution)/shard_map/ppermute | solution.py:27
  75.2 3.7 %collective-permute-start.11 = (bf16[512,1280]{1,0:T(8,128)(2,1)}, bf16[512,1280]{1,0:T(8,128)(2,1)S(1)}, u32[]{:S(2)}, u32[]{:S(2)}) collective-permute-start(bf16[512,1280]{1,0:T(8,128)(2,1)} %collective-permute-done.4.refs_5_), channel_id=1, source_target_pairs={{0,3},{1,0},{2,1},{3,2},{4,7},{5,4},{6,5},{7,6},{8,11},{9,8},{10,9... | collective-permute-start | bytes 3932168 | tf_op jit(solution)/shard_map/ppermute | solution.py:27
  78.9 4.1 %collective-permute-done.12.refs_3_ = bf16[512,1280]{1,0:T(8,128)(2,1)S(1)} collective-permute-done((bf16[512,1280]{1,0:T(8,128)(2,1)}, bf16[512,1280]{1,0:T(8,128)(2,1)S(1)}, u32[]{:S(2)}, u32[]{:S(2)}) %collective-permute-start.12) | collective-permute-done | bytes 1310752 | tf_op jit(solution)/shard_map/ppermute | solution.py:23
  84.1 2.7 %collective-permute-start.17 = (bf16[2,3,80,640]{3,2,1,0:T(8,128)(2,1)}, bf16[2,3,80,640]{3,2,1,0:T(8,128)(2,1)S(1)}, u32[]{:S(2)}, u32[]{:S(2)}) collective-permute-start(bf16[2,3,80,640]{3,2,1,0:T(8,128)(2,1)} %slice.58), channel_id=1, source_target_pairs={{0,96},{32,0},{64,32},{96,64},{1,97},{33,1},{65,33},{97,65},{2,98}... | collective-permute-start | bytes 1843208 | tf_op jit(solution)/shard_map/ppermute | solution.py:27
  86.9 16.4 %project_near.1 = (f32[1024,896]{1,0:T(8,128)}, f32[1024,1]{1,0:T(8,128)}) custom-call(bf16[512,1280]{1,0:T(8,128)(2,1)} %get-tuple-element.64.refs_0_, bf16[512,1280]{1,0:T(8,128)(2,1)} %get-tuple-element.65.refs_1_, bf16[512,1280]{1,0:T(8,128)(2,1)} %collective-permute-done.3.refs_2_, bf16[512,1280]{1,0:T(8,128)(2,1)} %copy-done.10, ...), custom_call_target="tpu_custom_call" | custom-call | flops 1024 | bytes 1024 | tf_op jit(solution)/shard_map/project_near/pallas_call | solution.py:77
  103.3 5.4 %collective-permute-done.10.refs_1_ = bf16[512,1280]{1,0:T(8,128)(2,1)S(1)} collective-permute-done((bf16[512,1280]{1,0:T(8,128)(2,1)}, bf16[512,1280]{1,0:T(8,128)(2,1)S(1)}, u32[]{:S(2)}, u32[]{:S(2)}) %collective-permute-start.10) | collective-permute-done | bytes 1310752 | tf_op jit(solution)/shard_map/ppermute | solution.py:23
  112.7 5.3 %project_far.1 = (bf16[16,64,640]{2,1,0:T(8,128)(2,1)S(1)}, bf16[16,64,256]{2,1,0:T(8,128)(2,1)}) custom-call(s32[16]{0:T(128)S(1)} %get-tuple-element.148.refs_0_, bf16[512,1280]{1,0:T(8,128)(2,1)S(1)} %collective-permute-done.10.refs_1_, bf16[512,1280]{1,0:T(8,128)(2,1)S(1)} %collective-permute-done.11.refs_2_, ...), custom_call_target="tpu_custom_call" | custom-call | flops 1024 | bytes 1024 | tf_op jit(solution)/shard_map/project_far/pallas_call | solution.py:125
  117.9 26.8 %all_to_all.32.refs_3_.refs_4_ = bf16[16,64,640]{2,1,0:T(8,128)(2,1)S(1)} all-to-all(bf16[16,64,640]{2,1,0:T(8,128)(2,1)S(1)} %get-tuple-element.89), channel_id=1, replica_groups=mesh['z'=4,'xh'=2,'core'=2,'context'=2,'tensor'=4] {'z','xh','core'}, dimensions={0} | all-to-all | bytes 2621440 | tf_op jit(solution)/shard_map/all_to_all | solution.py:498
  146.1 3.6 %all-to-all-start.3 = ((bf16[16,64,256]{2,1,0:T(8,128)(2,1)}), bf16[16,64,256]{2,1,0:T(8,128)(2,1)S(1)}, u32[]{:S(2)}, u32[]{:S(2)}) async-start(bf16[16,64,256]{2,1,0:T(8,128)(2,1)} %get-tuple-element.97), calls=%async_computation.3 | async-start | bytes 1048576 | tf_op jit(solution)/shard_map/all_to_all | solution.py:498
  149.7 7.1 %attend.3 = (f32[4,1,768]{2,1,0:T(1,128)S(1)}, f32[4,1,768]{2,1,0:T(1,128)S(1)}, f32[4,128,768]{2,1,0:T(8,128)S(1)}) custom-call(s32[32]{0:T(128)S(1)} %pad_add_fusion.1.refs_0_, s32[32]{0:T(128)S(1)} %pad_add_fusion.2.refs_1_, s32[1]{0:T(128)} %bitcast.24.refs_2_, bf16[16,64,640]{2,1,0:T(8,128)(2,1)S(1)} %all_to_all.32.refs_3_.refs_4_, ...), custom_call_target="tpu_custom_call" | custom-call | flops 1024 | bytes 1024 | tf_op jit(solution)/shard_map/attend/pallas_call | solution.py:275
  156.8 4.7 %collective-permute-done.18.refs_5_ = bf16[16,64,256]{2,1,0:T(8,128)(2,1)S(1)} collective-permute-done((bf16[16,64,256]{2,1,0:T(8,128)(2,1)S(1)}, bf16[16,64,256]{2,1,0:T(8,128)(2,1)S(1)}, u32[]{:S(2)}, u32[]{:S(2)}) %collective-permute-start.18) | collective-permute-done | bytes 524320 | tf_op jit(solution)/shard_map/ppermute | solution.py:501
  161.6 8.1 %attend.4 = bf16[16,64,384]{2,1,0:T(8,128)(2,1)} custom-call(s32[32]{0:T(128)S(1)} %pad_add_fusion.1.refs_0_, s32[32]{0:T(128)S(1)} %pad_add_fusion.2.refs_1_, s32[1]{0:T(128)} %bitcast.24.refs_2_, bf16[16,64,640]{2,1,0:T(8,128)(2,1)S(1)} %all_to_all.32.refs_3_.refs_4_, bf16[16,64,640]{2,1,0:T(8,128)(2,1)S(1)} %all_to_all.32.refs_3_.refs_4_, ...), custom_call_target="tpu_custom_call" | custom-call | flops 1024 | bytes 1024 | tf_op jit(solution)/shard_map/attend/pallas_call | solution.py:275
  169.7 3.8 %all-to-all-start.2 = ((bf16[16,64,384]{2,1,0:T(8,128)(2,1)}), bf16[16,64,384]{2,1,0:T(8,128)(2,1)S(1)}, u32[]{:S(2)}, u32[]{:S(2)}) async-start(bf16[16,64,384]{2,1,0:T(8,128)(2,1)} %attend.4), calls=%async_computation.2 | async-start | bytes 1572864 | tf_op jit(solution)/shard_map/all_to_all | solution.py:498
  173.5 11.5 %attend.5 = bf16[16,64,256]{2,1,0:T(8,128)(2,1)} custom-call(s32[32]{0:T(128)S(1)} %pad_add_fusion.1.refs_0_, s32[32]{0:T(128)S(1)} %pad_add_fusion.2.refs_1_, s32[1]{0:T(128)} %bitcast.24.refs_2_, bf16[16,64,256]{2,1,0:T(8,128)(2,1)S(1)} %all-to-all-done.3.refs_3_, bf16[16,64,640]{2,1,0:T(8,128)(2,1)S(1)} %all_to_all.32.refs_3_.refs_4_, ...), custom_call_target="tpu_custom_call" | custom-call | flops 1024 | bytes 1024 | tf_op jit(solution)/shard_map/attend/pallas_call | solution.py:275
  185.0 3.7 %all-to-all-done.2 = bf16[16,64,384]{2,1,0:T(8,128)(2,1)S(1)} async-done(((bf16[16,64,384]{2,1,0:T(8,128)(2,1)}), bf16[16,64,384]{2,1,0:T(8,128)(2,1)S(1)}, u32[]{:S(2)}, u32[]{:S(2)}) %all-to-all-start.2) | async-done | bytes 786464 | tf_op jit(solution)/shard_map/all_to_all | solution.py:498
  190.7 4.2 %all-to-all-start.4 = ((bf16[16,64,256]{2,1,0:T(8,128)(2,1)}), bf16[16,64,256]{2,1,0:T(8,128)(2,1)}, u32[]{:S(2)}, u32[]{:S(2)}) async-start(bf16[16,64,256]{2,1,0:T(8,128)(2,1)} %attend.5), calls=%async_computation.4 | async-start | bytes 1048576 | tf_op jit(solution)/shard_map/all_to_all | solution.py:498
  195.6 5.1 %place_shares.1.refs_7_.refs_3_ = bf16[8,2,3,80,640]{4,3,2,1,0:T(8,128)(2,1)} custom-call(s32[2]{0:T(128)} %pad_add_fusion.3.where, bf16[4,3,80,640]{3,2,1,0:T(8,128)(2,1)} %copy-done.5, bf16[4,3,80,640]{3,2,1,0:T(8,128)(2,1)} %copy-done.7, bf16[4,3,80,640]{3,2,1,0:T(8,128)(2,1)} %copy-done.6, bf16[2,3,80,640]{3,2,1,0:T(8,128)(2,1)} %copy-done.12, ...), custom_call_target="tpu_custom_call" | custom-call | flops 1024 | bytes 1024 | tf_op jit(solution)/shard_map/place_shares/pallas_call | solution.py:457
  200.7 6.6 %all-to-all-done.4 = bf16[16,64,256]{2,1,0:T(8,128)(2,1)} async-done(((bf16[16,64,256]{2,1,0:T(8,128)(2,1)}), bf16[16,64,256]{2,1,0:T(8,128)(2,1)}, u32[]{:S(2)}, u32[]{:S(2)}) %all-to-all-start.4) | async-done | bytes 524320 | tf_op jit(solution)/shard_map/all_to_all | solution.py:498
  215.3 2.4 copy-done
  217.7 8.9 %mix_near.2.refs_8_ = f32[1024,1280]{1,0:T(8,128)S(1)} custom-call(s32[16]{0:T(128)S(1)} %select_reduce_fusion.4.refs_0_, s32[1]{0:T(128)} %bitcast.29.refs_1_, bf16[1024,384]{1,0:T(8,128)(2,1)S(1)} %bitcast.45, bf16[1024,384]{1,0:T(8,128)(2,1)} %collective-permute-done.19.refs_3_, bf16[1024,384]{1,0:T(8,128)(2,1)} %collective-permute-done.20.refs_4_, ...), custom_call_target="tpu_custom_call" | custom-call | flops 1024 | bytes 1024 | tf_op jit(solution)/shard_map/mix_near/pallas_call | solution.py:364
  226.6 3.4 %collective-permute-done.24.refs_3_ = bf16[512,384]{1,0:T(8,128)(2,1)S(1)} collective-permute-done((bf16[512,384]{1,0:T(8,128)(2,1)S(1)}, bf16[512,384]{1,0:T(8,128)(2,1)S(1)}, u32[]{:S(2)}, u32[]{:S(2)}) %collective-permute-start.24) | collective-permute-done | bytes 393248 | tf_op jit(solution)/shard_map/ppermute | solution.py:27
  231.9 3.0 %collective-permute-start.26 = (bf16[512,256]{1,0:T(8,128)(2,1)S(1)}, bf16[512,256]{1,0:T(8,128)(2,1)S(1)}, u32[]{:S(2)}, u32[]{:S(2)}) collective-permute-start(bf16[512,256]{1,0:T(8,128)(2,1)S(1)} %slice.63), channel_id=1, source_target_pairs={{0,3},{1,0},{2,1},{3,2},{4,7},{5,4},{6,5},{7,6},{8,11},{9,8},{10,9... | collective-permute-start | bytes 786440 | tf_op jit(solution)/shard_map/ppermute | solution.py:27
  234.9 6.7 %mix_near.3.refs_4_ = f32[1024,1280]{1,0:T(8,128)S(1)} custom-call(s32[16]{0:T(128)S(1)} %select_reduce_fusion.4.refs_0_, s32[1]{0:T(128)} %bitcast.29.refs_1_, bf16[512,384]{1,0:T(8,128)(2,1)S(1)} %collective-permute-done.23.refs_2_, bf16[512,384]{1,0:T(8,128)(2,1)S(1)} %collective-permute-done.24.refs_3_, ...), custom_call_target="tpu_custom_call" | custom-call | flops 1024 | bytes 1024 | tf_op jit(solution)/shard_map/mix_near/pallas_call | solution.py:364
  241.6 4.3 %mix_far.1 = bf16[16,64,1280]{2,1,0:T(8,128)(2,1)} custom-call(s32[16]{0:T(128)S(1)} %select_reduce_fusion.4.refs_0_, bf16[512,256]{1,0:T(8,128)(2,1)S(1)} %collective-permute-done.25.refs_1_, bf16[512,256]{1,0:T(8,128)(2,1)S(1)} %collective-permute-done.26.refs_2_, bf16[8,2,3,80,640]{4,3,2,1,0:T(8,128)(2,1)S(1)} %copy-done, f32[1024,1280]{1,0:T(8,128)S(1)} %mix_near.3.refs_4_), custom_call_target="tpu_custom_call" | custom-call | flops 1024 | bytes 1024 | tf_op jit(solution)/shard_map/mix_far/pallas_call | solution.py:404
  (123 shorter events, 42.3 us)
Async XLA Ops:
  3.0 12.0 %collective-permute-start.2 = (bf16[80,640]{1,0:T(8,128)(2,1)}, bf16[80,640]{1,0:T(8,128)(2,1)S(1)}, u32[]{:S(2)}, u32[]{:S(2)}) collective-permute-start(bf16[80,640]{1,0:T(8,128)(2,1)} %get-tuple-element.130), channel_id=1, source_target_pairs={{0,2},{1,3},{2,0},{3,1},{4,6},{5,7},{6,4},{7,5},{8,10},{9,11},{10,... | collective-permute-start | bytes 307208 | tf_op jit(solution)/shard_map/ppermute | solution.py:440
  6.1 8.8 %collective-permute-start = (bf16[80,640]{1,0:T(8,128)(2,1)}, bf16[80,640]{1,0:T(8,128)(2,1)S(1)}, u32[]{:S(2)}, u32[]{:S(2)}) collective-permute-start(bf16[80,640]{1,0:T(8,128)(2,1)} %get-tuple-element.131), channel_id=1, source_target_pairs={{0,1},{1,2},{2,3},{3,0},{4,5},{5,6},{6,7},{7,4},{8,9},{9,10},{10,1... | collective-permute-start | bytes 307208 | tf_op jit(solution)/shard_map/ppermute | solution.py:23
  6.8 8.2 %collective-permute-start.1 = (bf16[80,640]{1,0:T(8,128)(2,1)S(1)}, bf16[80,640]{1,0:T(8,128)(2,1)S(1)}, u32[]{:S(2)}, u32[]{:S(2)}) collective-permute-start(bf16[80,640]{1,0:T(8,128)(2,1)S(1)} %get-tuple-element.132), channel_id=1, source_target_pairs={{0,3},{1,0},{2,1},{3,2},{4,7},{5,4},{6,5},{7,6},{8,11},{9,8},{10,9... | collective-permute-start | bytes 307208 | tf_op jit(solution)/shard_map/ppermute | solution.py:27
  15.1 27.8 %collective-permute-start.6 = (bf16[3,80,640]{2,1,0:T(8,128)(2,1)S(1)}, bf16[3,80,640]{2,1,0:T(8,128)(2,1)S(1)}, u32[]{:S(2)}, u32[]{:S(2)}) collective-permute-start(bf16[3,80,640]{2,1,0:T(8,128)(2,1)S(1)} %get-tuple-element.134), channel_id=1, source_target_pairs={{0,4},{4,16},{16,20},{20,0},{1,5},{5,17},{17,21},{21,1},{2,6},{6,1... | collective-permute-start | bytes 921608 | tf_op jit(solution)/shard_map/ppermute | solution.py:23
  16.6 28.0 %collective-permute-start.7 = (bf16[3,80,640]{2,1,0:T(8,128)(2,1)S(1)}, bf16[3,80,640]{2,1,0:T(8,128)(2,1)S(1)}, u32[]{:S(2)}, u32[]{:S(2)}) collective-permute-start(bf16[3,80,640]{2,1,0:T(8,128)(2,1)S(1)} %get-tuple-element.134), channel_id=1, source_target_pairs={{0,20},{4,0},{16,4},{20,16},{1,21},{5,1},{17,5},{21,17},{2,22},{6,... | collective-permute-start | bytes 921608 | tf_op jit(solution)/shard_map/ppermute | solution.py:27
  17.2 35.0 %collective-permute-start.3 = (bf16[512,1280]{1,0:T(8,128)(2,1)}, bf16[512,1280]{1,0:T(8,128)(2,1)}, u32[]{:S(2)}, u32[]{:S(2)}) collective-permute-start(bf16[512,1280]{1,0:T(8,128)(2,1)} %get-tuple-element.64.refs_0_), channel_id=1, source_target_pairs={{0,1},{1,2},{2,3},{3,0},{4,5},{5,6},{6,7},{7,4},{8,9},{9,10},{10,1... | collective-permute-start | bytes 3932168 | tf_op jit(solution)/shard_map/ppermute | solution.py:23
  17.2 35.0 %collective-permute-start.4 = (bf16[512,1280]{1,0:T(8,128)(2,1)}, bf16[512,1280]{1,0:T(8,128)(2,1)}, u32[]{:S(2)}, u32[]{:S(2)}) collective-permute-start(bf16[512,1280]{1,0:T(8,128)(2,1)} %get-tuple-element.65.refs_1_), channel_id=1, source_target_pairs={{0,3},{1,0},{2,1},{3,2},{4,7},{5,4},{6,5},{7,6},{8,11},{9,8},{10,9... | collective-permute-start | bytes 3932168 | tf_op jit(solution)/shard_map/ppermute | solution.py:27
  21.1 16.0 %all-to-all-start = ((s32[16,1,2]{2,1,0:T(1,128)}), s32[16,1,2]{2,1,0:T(1,128)S(1)}, u32[]{:S(2)}, u32[]{:S(2)}) async-start(s32[16,1,2]{2,1,0:T(1,128)} %copy.14), calls=%async_computation | async-start | bytes 16384 | tf_op jit(solution)/shard_map/all_to_all | solution.py:498
  37.2 5.5 %collective-permute-start.5 = (s32[16,2]{0,1:T(2,128)S(1)}, s32[16,2]{0,1:T(2,128)S(1)}, u32[]{:S(2)}, u32[]{:S(2)}) collective-permute-start(s32[16,2]{0,1:T(2,128)S(1)} %bitcast.52), channel_id=1, source_target_pairs={{0,4},{1,5},{2,6},{3,7},{8,12},{9,13},{10,14},{11,15},{16,20},{17,... | collective-permute-start | bytes 392 | tf_op jit(solution)/shard_map/ppermute | solution.py:501
  42.6 32.5 %collective-permute-start.13 = (bf16[512,1280]{1,0:T(8,128)(2,1)}, bf16[512,1280]{1,0:T(8,128)(2,1)}, u32[]{:S(2)}, u32[]{:S(2)}) collective-permute-start(bf16[512,1280]{1,0:T(8,128)(2,1)} %get-tuple-element.64.refs_0_), channel_id=1, source_target_pairs={{0,3},{1,0},{2,1},{3,2},{4,7},{5,4},{6,5},{7,6},{8,11},{9,8},{10,9... | collective-permute-start | bytes 3932168 | tf_op jit(solution)/shard_map/ppermute | solution.py:27
  42.9 9.0 %collective-permute-start.8 = (bf16[3,48,640]{2,1,0:T(8,128)(2,1)S(1)}, bf16[3,48,640]{2,1,0:T(8,128)(2,1)S(1)}, u32[]{:S(2)}, u32[]{:S(2)}) collective-permute-start(bf16[3,48,640]{2,1,0:T(8,128)(2,1)S(1)} %slice.68), channel_id=1, source_target_pairs={{0,4},{4,16},{16,20},{20,0},{1,5},{5,17},{17,21},{21,1},{2,6},{6,1... | collective-permute-start | bytes 552968 | tf_op jit(solution)/shard_map/ppermute | solution.py:23
  44.7 5.2 %collective-permute-start.9 = (bf16[3,32,640]{2,1,0:T(8,128)(2,1)S(1)}, bf16[3,32,640]{2,1,0:T(8,128)(2,1)S(1)}, u32[]{:S(2)}, u32[]{:S(2)}) collective-permute-start(bf16[3,32,640]{2,1,0:T(8,128)(2,1)S(1)} %slice.69), channel_id=1, source_target_pairs={{0,20},{4,0},{16,4},{20,16},{1,21},{5,1},{17,5},{21,17},{2,22},{6,... | collective-permute-start | bytes 368648 | tf_op jit(solution)/shard_map/ppermute | solution.py:27
  49.9 33.1 %collective-permute-start.12 = (bf16[512,1280]{1,0:T(8,128)(2,1)}, bf16[512,1280]{1,0:T(8,128)(2,1)S(1)}, u32[]{:S(2)}, u32[]{:S(2)}) collective-permute-start(bf16[512,1280]{1,0:T(8,128)(2,1)} %get-tuple-element.65.refs_1_), channel_id=1, source_target_pairs={{0,1},{1,2},{2,3},{3,0},{4,5},{5,6},{6,7},{7,4},{8,9},{9,10},{10,1... | collective-permute-start | bytes 3932168 | tf_op jit(solution)/shard_map/ppermute | solution.py:23
  51.9 34.9 %copy-start.14 = (bf16[128]{0:T(256)(128)(2,1)S(1)}, bf16[128]{0:T(256)(128)(2,1)}, u32[]{:S(2)}) copy-start(bf16[128]{0:T(256)(128)(2,1)} %param.20) | copy-start | bytes 772
  52.2 30.8 %collective-permute-start.15 = (bf16[4,3,80,640]{3,2,1,0:T(8,128)(2,1)S(1)}, bf16[4,3,80,640]{3,2,1,0:T(8,128)(2,1)S(1)}, u32[]{:S(2)}, u32[]{:S(2)}) collective-permute-start(bf16[4,3,80,640]{3,2,1,0:T(8,128)(2,1)S(1)} %pad_maximum_fusion.4.refs_0_), channel_id=1, source_target_pairs={{0,96},{32,0},{64,32},{96,64},{1,97},{33,1},{65,33},{97,65},{2,98}... | collective-permute-start | bytes 3686408 | tf_op jit(solution)/shard_map/ppermute | solution.py:27
  54.9 28.1 %collective-permute-start.14 = (bf16[4,3,80,640]{3,2,1,0:T(8,128)(2,1)S(1)}, bf16[4,3,80,640]{3,2,1,0:T(8,128)(2,1)S(1)}, u32[]{:S(2)}, u32[]{:S(2)}) collective-permute-start(bf16[4,3,80,640]{3,2,1,0:T(8,128)(2,1)S(1)} %pad_maximum_fusion.4.refs_0_), channel_id=1, source_target_pairs={{0,32},{32,64},{64,96},{96,0},{1,33},{33,65},{65,97},{97,1},{2,34}... | collective-permute-start | bytes 3686408 | tf_op jit(solution)/shard_map/ppermute | solution.py:23
  54.9 53.8 %collective-permute-start.10 = (bf16[512,1280]{1,0:T(8,128)(2,1)}, bf16[512,1280]{1,0:T(8,128)(2,1)S(1)}, u32[]{:S(2)}, u32[]{:S(2)}) collective-permute-start(bf16[512,1280]{1,0:T(8,128)(2,1)} %collective-permute-done.3.refs_2_), channel_id=1, source_target_pairs={{0,1},{1,2},{2,3},{3,0},{4,5},{5,6},{6,7},{7,4},{8,9},{9,10},{10,1... | collective-permute-start | bytes 3932168 | tf_op jit(solution)/shard_map/ppermute | solution.py:23
  75.2 33.5 %collective-permute-start.11 = (bf16[512,1280]{1,0:T(8,128)(2,1)}, bf16[512,1280]{1,0:T(8,128)(2,1)S(1)}, u32[]{:S(2)}, u32[]{:S(2)}) collective-permute-start(bf16[512,1280]{1,0:T(8,128)(2,1)} %collective-permute-done.4.refs_5_), channel_id=1, source_target_pairs={{0,3},{1,0},{2,1},{3,2},{4,7},{5,4},{6,5},{7,6},{8,11},{9,8},{10,9... | collective-permute-start | bytes 3932168 | tf_op jit(solution)/shard_map/ppermute | solution.py:27
  84.1 24.6 %collective-permute-start.17 = (bf16[2,3,80,640]{3,2,1,0:T(8,128)(2,1)}, bf16[2,3,80,640]{3,2,1,0:T(8,128)(2,1)S(1)}, u32[]{:S(2)}, u32[]{:S(2)}) collective-permute-start(bf16[2,3,80,640]{3,2,1,0:T(8,128)(2,1)} %slice.58), channel_id=1, source_target_pairs={{0,96},{32,0},{64,32},{96,64},{1,97},{33,1},{65,33},{97,65},{2,98}... | collective-permute-start | bytes 1843208 | tf_op jit(solution)/shard_map/ppermute | solution.py:27
  86.8 21.9 %collective-permute-start.16 = (bf16[2,3,80,640]{3,2,1,0:T(8,128)(2,1)S(1)}, bf16[2,3,80,640]{3,2,1,0:T(8,128)(2,1)S(1)}, u32[]{:S(2)}, u32[]{:S(2)}) collective-permute-start(bf16[2,3,80,640]{3,2,1,0:T(8,128)(2,1)S(1)} %slice.57), channel_id=1, source_target_pairs={{0,32},{32,64},{64,96},{96,0},{1,33},{33,65},{65,97},{97,1},{2,34}... | collective-permute-start | bytes 1843208 | tf_op jit(solution)/shard_map/ppermute | solution.py:23
  144.8 16.8 %collective-permute-start.18 = (bf16[16,64,256]{2,1,0:T(8,128)(2,1)S(1)}, bf16[16,64,256]{2,1,0:T(8,128)(2,1)S(1)}, u32[]{:S(2)}, u32[]{:S(2)}) collective-permute-start(bf16[16,64,256]{2,1,0:T(8,128)(2,1)S(1)} %slice.70), channel_id=1, source_target_pairs={{0,4},{1,5},{2,6},{3,7},{8,12},{9,13},{10,14},{11,15},{16,20},{17,... | collective-permute-start | bytes 1572872 | tf_op jit(solution)/shard_map/ppermute | solution.py:501
  146.1 23.6 %all-to-all-start.3 = ((bf16[16,64,256]{2,1,0:T(8,128)(2,1)}), bf16[16,64,256]{2,1,0:T(8,128)(2,1)S(1)}, u32[]{:S(2)}, u32[]{:S(2)}) async-start(bf16[16,64,256]{2,1,0:T(8,128)(2,1)} %get-tuple-element.97), calls=%async_computation.3 | async-start | bytes 1048576 | tf_op jit(solution)/shard_map/all_to_all | solution.py:498
  169.7 19.0 %all-to-all-start.2 = ((bf16[16,64,384]{2,1,0:T(8,128)(2,1)}), bf16[16,64,384]{2,1,0:T(8,128)(2,1)S(1)}, u32[]{:S(2)}, u32[]{:S(2)}) async-start(bf16[16,64,384]{2,1,0:T(8,128)(2,1)} %attend.4), calls=%async_computation.2 | async-start | bytes 1572864 | tf_op jit(solution)/shard_map/all_to_all | solution.py:498
  188.7 19.1 %collective-permute-start.20 = (bf16[1024,384]{1,0:T(8,128)(2,1)S(1)}, bf16[1024,384]{1,0:T(8,128)(2,1)}, u32[]{:S(2)}, u32[]{:S(2)}) collective-permute-start(bf16[1024,384]{1,0:T(8,128)(2,1)S(1)} %bitcast.43), channel_id=1, source_target_pairs={{0,3},{1,0},{2,1},{3,2},{4,7},{5,4},{6,5},{7,6},{8,11},{9,8},{10,9... | collective-permute-start | bytes 2359304 | tf_op jit(solution)/shard_map/ppermute | solution.py:27
  188.9 20.2 %collective-permute-start.19 = (bf16[1024,384]{1,0:T(8,128)(2,1)S(1)}, bf16[1024,384]{1,0:T(8,128)(2,1)}, u32[]{:S(2)}, u32[]{:S(2)}) collective-permute-start(bf16[1024,384]{1,0:T(8,128)(2,1)S(1)} %bitcast.44), channel_id=1, source_target_pairs={{0,1},{1,2},{2,3},{3,0},{4,5},{5,6},{6,7},{7,4},{8,9},{9,10},{10,1... | collective-permute-start | bytes 2359304 | tf_op jit(solution)/shard_map/ppermute | solution.py:23
  190.7 16.6 %all-to-all-start.4 = ((bf16[16,64,256]{2,1,0:T(8,128)(2,1)}), bf16[16,64,256]{2,1,0:T(8,128)(2,1)}, u32[]{:S(2)}, u32[]{:S(2)}) async-start(bf16[16,64,256]{2,1,0:T(8,128)(2,1)} %attend.5), calls=%async_computation.4 | async-start | bytes 1048576 | tf_op jit(solution)/shard_map/all_to_all | solution.py:498
  209.1 22.5 %collective-permute-start.22 = (bf16[1024,256]{1,0:T(8,128)(2,1)}, bf16[1024,256]{1,0:T(8,128)(2,1)S(1)}, u32[]{:S(2)}, u32[]{:S(2)}) collective-permute-start(bf16[1024,256]{1,0:T(8,128)(2,1)} %bitcast.26.refs_5_), channel_id=1, source_target_pairs={{0,3},{1,0},{2,1},{3,2},{4,7},{5,4},{6,5},{7,6},{8,11},{9,8},{10,9... | collective-permute-start | bytes 1572872 | tf_op jit(solution)/shard_map/ppermute | solution.py:27
  209.3 22.2 %collective-permute-start.21 = (bf16[1024,256]{1,0:T(8,128)(2,1)}, bf16[1024,256]{1,0:T(8,128)(2,1)S(1)}, u32[]{:S(2)}, u32[]{:S(2)}) collective-permute-start(bf16[1024,256]{1,0:T(8,128)(2,1)} %bitcast.26.refs_5_), channel_id=1, source_target_pairs={{0,1},{1,2},{2,3},{3,0},{4,5},{5,6},{6,7},{7,4},{8,9},{9,10},{10,1... | collective-permute-start | bytes 1572872 | tf_op jit(solution)/shard_map/ppermute | solution.py:23
  213.2 16.8 %collective-permute-start.24 = (bf16[512,384]{1,0:T(8,128)(2,1)S(1)}, bf16[512,384]{1,0:T(8,128)(2,1)S(1)}, u32[]{:S(2)}, u32[]{:S(2)}) collective-permute-start(bf16[512,384]{1,0:T(8,128)(2,1)S(1)} %slice.61), channel_id=1, source_target_pairs={{0,3},{1,0},{2,1},{3,2},{4,7},{5,4},{6,5},{7,6},{8,11},{9,8},{10,9... | collective-permute-start | bytes 1179656 | tf_op jit(solution)/shard_map/ppermute | solution.py:27
  214.7 16.8 %collective-permute-start.23 = (bf16[512,384]{1,0:T(8,128)(2,1)S(1)}, bf16[512,384]{1,0:T(8,128)(2,1)S(1)}, u32[]{:S(2)}, u32[]{:S(2)}) collective-permute-start(bf16[512,384]{1,0:T(8,128)(2,1)S(1)} %slice.60), channel_id=1, source_target_pairs={{0,1},{1,2},{2,3},{3,0},{4,5},{5,6},{6,7},{7,4},{8,9},{9,10},{10,1... | collective-permute-start | bytes 1179656 | tf_op jit(solution)/shard_map/ppermute | solution.py:23
  231.6 10.0 %collective-permute-start.25 = (bf16[512,256]{1,0:T(8,128)(2,1)S(1)}, bf16[512,256]{1,0:T(8,128)(2,1)S(1)}, u32[]{:S(2)}, u32[]{:S(2)}) collective-permute-start(bf16[512,256]{1,0:T(8,128)(2,1)S(1)} %slice.62), channel_id=1, source_target_pairs={{0,1},{1,2},{2,3},{3,0},{4,5},{5,6},{6,7},{7,4},{8,9},{9,10},{10,1... | collective-permute-start | bytes 786440 | tf_op jit(solution)/shard_map/ppermute | solution.py:23
  231.9 9.7 %collective-permute-start.26 = (bf16[512,256]{1,0:T(8,128)(2,1)S(1)}, bf16[512,256]{1,0:T(8,128)(2,1)S(1)}, u32[]{:S(2)}, u32[]{:S(2)}) collective-permute-start(bf16[512,256]{1,0:T(8,128)(2,1)S(1)} %slice.63), channel_id=1, source_target_pairs={{0,3},{1,0},{2,1},{3,2},{4,7},{5,4},{6,5},{7,6},{8,11},{9,8},{10,9... | collective-permute-start | bytes 786440 | tf_op jit(solution)/shard_map/ppermute | solution.py:27
  (15 other events, 146.4 us)
